TPU v7x, 32 devices: a whole 2x2x4 slice. The times are simulated.
32 devices in a mesh: blk: 2 (over x), dp: 16 (over z, y, core).
Axes of the slice: x: 2, y: 2, z: 4, core: 2. Of those that a mesh axis runs over, the one named last changes fastest.
Arguments:
- content_in: bfloat16 [16, 1024, 768], P('dp', 'blk'), may hold values from -6 to 6
- query_in: bfloat16 [16, 1024, 768], P('dp', 'blk'), may hold values from -6 to 6
- cot_content: bfloat16 [16, 1024, 768], P('dp', 'blk'), may hold values from -6 to 6
- cot_query: bfloat16 [16, 1024, 768], P('dp', 'blk'), may hold values from -6 to 6
- attn_weights: bfloat16 [2, 768, 2304], P(None, 'dp'), may hold values from -0.21875 to 0.21875
- out_weight: bfloat16 [2, 768, 768], P(None, 'dp'), may hold values from -3.5 to 3.5
- ffn_in: bfloat16 [2, 768, 3072], P(None, 'dp'), may hold values from -0.21875 to 0.21875
- ffn_out_t: bfloat16 [2, 768, 3072], P(None, 'dp'), may hold values from -0.109375 to 0.109375
- norm_gains: float32 [2, 2, 768], replicated, may hold values from 0.1 to 1.9
- norm_shifts: float32 [2, 2, 768], replicated, may hold values from -1.5 to 1.5
- bias_table: float32 [32, 12], replicated, may hold values from -4 to 4
- permutation: int32 [16, 1024], P('dp'), may hold values from 0 to 1023, each once within a row
- predicted: int32 [16, 1024], P('dp'), may hold values 0 or 1
- doc_lengths: int32 [16, 4], P('dp'), may hold values from 1 to 512, 1024 in all within a row
Outputs:
- content_out: bfloat16 [16, 1024, 768], P('dp', 'blk')
- query_out: bfloat16 [16, 1024, 768], P('dp', 'blk')
- content_grad: float32 [16, 1024, 768], P('dp', 'blk')
- query_grad: float32 [16, 1024, 768], P('dp', 'blk')
- attn_weights_grad: float32 [2, 768, 2304], P(None, 'dp')
- out_weight_grad: float32 [2, 768, 768], P(None, 'dp')
- ffn_in_grad: float32 [2, 768, 3072], P(None, 'dp')
- ffn_out_t_grad: float32 [2, 768, 3072], P(None, 'dp')
- norm_gains_grad: float32 [2, 2, 768], replicated
- norm_shifts_grad: float32 [2, 2, 768], replicated
- bias_table_grad: float32 [32, 12], replicated
Inputs may be any that keep to these rules, and one draw needn't show every extreme that they name: Each row is a permutation of the initial positions 0 to 1023; entry r is the initial position of the token at rank r. 1 marks a predicted initial position. `doc_lengths`: each row holds the lengths of the 4 documents of one sequence in initial order and sums to 1024.
All inputs are finite; a program needn't handle non-finite values. No bound on the sum of `predicted` on one device may be relied on, other than what follows from the above.
Results may differ from a plain program's by a relative error of at most 0.025.
Values may be sent and summed in bfloat16 or wider, within the bound.
No kernel may reach another device: no remote copies, remote signals or barrier semaphores. Data moves between devices by JAX's collectives and lax.ppermute only.
A program may use at most 320 MiB of HBM per device.

v0:
```python
import math

import jax
import jax.numpy as jnp
from jax import lax
from jax.sharding import PartitionSpec as P

THRESHOLDS = (12, 16, 23, 32, 46, 64, 91)


def bucket_of(relative):
    distance = jnp.abs(relative)
    far_bucket = 8 + sum(((distance >= threshold).astype(jnp.int32) for threshold in THRESHOLDS))
    near_bucket = jnp.where(distance < 8, distance, jnp.minimum(far_bucket, 15))
    return jnp.where(relative > 0, 16, 0).astype(jnp.int32) + near_bucket


def layer_norm(tensor, scale_row, shift_row):
    center = tensor - jnp.mean(tensor, axis=-1, keepdims=True)
    spread = jnp.mean(center * center, axis=-1, keepdims=True)
    return center * lax.rsqrt(spread + 1e-05) * scale_row + shift_row


def gelu_exact(tensor):
    return jax.nn.gelu(tensor, approximate=False)


def flat_dot(left_side, right_side):
    return jnp.dot(left_side, right_side, preferred_element_type=jnp.float32)


def dot_right_t(left_side, right_side):
    return lax.dot_general(
        left_side, right_side, (((1,), (1,)), ((), ())), preferred_element_type=jnp.float32
    )


def dot_left_t(left_side, right_side):
    return lax.dot_general(
        left_side, right_side, (((0,), (0,)), ((), ())), preferred_element_type=jnp.float32
    )


def sequence_meta(rank_anchor, chosen, lengths):
    positions = jnp.arange(rank_anchor.shape[1], dtype=jnp.int32)
    bounds = jnp.cumsum(lengths, axis=1)[:, :-1]
    doc_anchor = jnp.sum((positions[None, :, None] >= bounds[:, None, :]).astype(jnp.int32), axis=2)
    starts = (positions[None, :] == 0) | jnp.any(
        positions[None, :, None] == bounds[:, None, :], axis=2
    )
    chosen_live = ((chosen == 1) & jnp.logical_not(starts)).astype(jnp.int32)
    doc_rank = jnp.take_along_axis(doc_anchor, rank_anchor, axis=1)
    pred_rank = jnp.take_along_axis(chosen_live, rank_anchor, axis=1)
    return (doc_rank, pred_rank)


def block_scores(queries, key_block, bias_table, meta, key_first):
    rank_anchor, doc_rank, pred_rank, query_anchor, query_doc, query_rank = meta
    key_span = key_block.shape[1]
    key_anchor = lax.dynamic_slice_in_dim(rank_anchor, key_first, key_span, 1)
    key_doc = lax.dynamic_slice_in_dim(doc_rank, key_first, key_span, 1)
    key_pred = lax.dynamic_slice_in_dim(pred_rank, key_first, key_span, 1)
    key_rank = key_first + jnp.arange(key_span, dtype=jnp.int32)
    raw_scores = jnp.einsum(
        "sjqhd,skhd->shjqk", queries, key_block, preferred_element_type=jnp.float32
    )
    buckets = bucket_of(key_anchor[:, None, :] - query_anchor[:, :, None])
    bucket_ids = jnp.arange(bias_table.shape[0], dtype=jnp.int32)
    onehot = (buckets[None] == bucket_ids[:, None, None, None]).astype(jnp.float32)
    bias = jnp.einsum("bh,bsqk->shqk", bias_table, onehot, precision=lax.Precision.HIGHEST)
    same_doc = query_doc[:, :, None] == key_doc[:, None, :]
    open_key = (key_pred == 0)[:, None, :]
    earlier = key_rank[None, None, :] <= query_rank[None, :, None]
    strictly = key_rank[None, None, :] < query_rank[None, :, None]
    visible = jnp.stack([same_doc & (open_key | earlier), same_doc & (open_key | strictly)], axis=1)
    scores = jnp.where(visible[:, None], raw_scores * 0.125 + bias[:, :, None], -1e30)
    return (scores, onehot)


def attend_forward(queries, whole_keys, whole_values, bias_table, meta, key_span):
    state_shape = (queries.shape[0], queries.shape[3], 2, queries.shape[2])
    step_count = whole_keys.shape[1] // key_span

    def stats_step(step_index, loop_state):
        running_max, running_sum = loop_state
        key_first = (step_index * key_span).astype(jnp.int32)
        key_block = lax.dynamic_slice_in_dim(whole_keys, key_first, key_span, 1)
        scores = block_scores(queries, key_block, bias_table, meta, key_first)[0]
        new_max = jnp.maximum(running_max, jnp.max(scores, axis=-1))
        new_sum = running_sum * jnp.exp(running_max - new_max) + jnp.sum(
            jnp.exp(scores - new_max[..., None]), axis=-1
        )
        return (new_max, new_sum)

    start_state = (jnp.full(state_shape, -1e30, jnp.float32), jnp.zeros(state_shape, jnp.float32))
    running_max, running_sum = lax.fori_loop(0, step_count, stats_step, start_state)
    log_total = running_max + jnp.log(running_sum)

    def value_step(step_index, weighted):
        key_first = (step_index * key_span).astype(jnp.int32)
        key_block = lax.dynamic_slice_in_dim(whole_keys, key_first, key_span, 1)
        value_block = lax.dynamic_slice_in_dim(whole_values, key_first, key_span, 1)
        scores = block_scores(queries, key_block, bias_table, meta, key_first)[0]
        weights = jnp.exp(scores - log_total[..., None]).astype(jnp.bfloat16)
        return weighted + jnp.einsum(
            "shjqk,skhd->sjqhd", weights, value_block, preferred_element_type=jnp.float32
        )

    weighted = lax.fori_loop(0, step_count, value_step, jnp.zeros(queries.shape, jnp.float32))
    return (log_total, weighted)


def table_term(grad_scores, onehot):
    summed = jnp.sum(grad_scores, axis=2)
    return jnp.einsum("shqk,bsqk->bh", summed, onehot, precision=lax.Precision.HIGHEST)


def attend_backward(
    queries, whole_keys, whole_values, grad_out, row_dots, log_total, bias_table, meta, key_span
):
    seq_count = queries.shape[0]
    model_width = queries.shape[3] * queries.shape[4]
    length = whole_keys.shape[1]

    def back_step(step_index, loop_state):
        grad_query, grad_table, key_terms = loop_state
        key_first = (step_index * key_span).astype(jnp.int32)
        key_block = lax.dynamic_slice_in_dim(whole_keys, key_first, key_span, 1)
        value_block = lax.dynamic_slice_in_dim(whole_values, key_first, key_span, 1)
        scores, onehot = block_scores(queries, key_block, bias_table, meta, key_first)
        softmax_weights = jnp.exp(scores - log_total[..., None])
        grad_weights = jnp.einsum(
            "sjqhd,skhd->shjqk", grad_out, value_block, preferred_element_type=jnp.float32
        )
        grad_scores = softmax_weights * (grad_weights - row_dots[..., None])
        grad_table = grad_table + table_term(grad_scores, onehot)
        grad_raw = (grad_scores * 0.125).astype(jnp.bfloat16)
        grad_query = grad_query + jnp.einsum(
            "shjqk,skhd->sjqhd", grad_raw, key_block, preferred_element_type=jnp.float32
        )
        weights = softmax_weights.astype(jnp.bfloat16)
        grad_key = jnp.einsum(
            "shjqk,sjqhd->kshd", grad_raw, queries, preferred_element_type=jnp.float32
        )
        grad_value = jnp.einsum(
            "shjqk,sjqhd->kshd", weights, grad_out, preferred_element_type=jnp.float32
        )
        both_grads = jnp.concatenate(
            [
                grad_key.reshape(key_span, seq_count, model_width),
                grad_value.reshape(key_span, seq_count, model_width),
            ],
            axis=2,
        )
        key_terms = lax.dynamic_update_slice_in_dim(key_terms, both_grads, key_first, 0)
        return (grad_query, grad_table, key_terms)

    key_start = jnp.zeros((length, seq_count, 2 * model_width), jnp.float32)
    start_state = (
        jnp.zeros(queries.shape, jnp.float32),
        jnp.zeros(bias_table.shape, jnp.float32),
        key_start,
    )
    return lax.fori_loop(0, length // key_span, back_step, start_state)


def fetch_forward(attn_weights, out_weight, ffn_in, ffn_out_t, layer_index):
    return (
        lax.all_gather(attn_weights[layer_index], "dp", axis=0, tiled=True),
        lax.all_gather(out_weight[layer_index], "dp", axis=0, tiled=True),
        lax.all_gather(ffn_in[layer_index], "dp", axis=0, tiled=True),
        lax.all_gather(ffn_out_t[layer_index], "dp", axis=0, tiled=True),
    )


def fetch_again(attn_weights, out_weight, ffn_in, ffn_out_t, layer_index):
    return (
        lax.all_gather(attn_weights[layer_index], "dp", axis=0, tiled=True),
        lax.all_gather(out_weight[layer_index], "dp", axis=0, tiled=True),
        lax.all_gather(ffn_in[layer_index], "dp", axis=0, tiled=True),
        lax.all_gather(ffn_out_t[layer_index], "dp", axis=0, tiled=True),
    )


def shards(
    content_in,
    query_in,
    cot_content,
    cot_query,
    attn_weights,
    out_weight,
    ffn_in,
    ffn_out_t,
    norm_gains,
    norm_shifts,
    bias_table,
    permutation,
    predicted,
    doc_lengths,
):
    seq_count, local_rows, model_width = content_in.shape
    length = permutation.shape[1]
    head_count = bias_table.shape[1]
    head_size = model_width // head_count
    layer_count = attn_weights.shape[0]
    key_span = math.gcd(length, 128)
    token_rows = seq_count * local_rows
    first_rank = lax.axis_index("blk") * local_rows
    doc_rank, pred_rank = sequence_meta(permutation, predicted, doc_lengths)
    query_anchor = lax.dynamic_slice_in_dim(permutation, first_rank, local_rows, 1)
    query_doc = lax.dynamic_slice_in_dim(doc_rank, first_rank, local_rows, 1)
    query_rank = first_rank + jnp.arange(local_rows, dtype=jnp.int32)
    meta = (permutation, doc_rank, pred_rank, query_anchor, query_doc, query_rank)
    five_shape = (seq_count, 2, local_rows, head_count, head_size)
    stream = jnp.stack([content_in, query_in], axis=1).astype(jnp.float32)
    kept_state = []
    for layer_index in range(layer_count):
        matrices = fetch_forward(attn_weights, out_weight, ffn_in, ffn_out_t, layer_index)
        qkv_full, proj_full, inner_full, outer_full = matrices
        stream_low = stream.astype(jnp.bfloat16)
        content_rows = stream_low[:, 0].reshape(token_rows, model_width)
        query_rows = stream_low[:, 1].reshape(token_rows, model_width)
        projected = flat_dot(content_rows, qkv_full).astype(jnp.bfloat16)
        query_own = flat_dot(query_rows, qkv_full[:, :model_width]).astype(jnp.bfloat16)
        queries = jnp.stack(
            [
                projected[:, :model_width].reshape(seq_count, local_rows, model_width),
                query_own.reshape(seq_count, local_rows, model_width),
            ],
            axis=1,
        ).reshape(five_shape)
        keys = projected[:, model_width : 2 * model_width].reshape(
            seq_count, local_rows, model_width
        )
        values = projected[:, 2 * model_width :].reshape(seq_count, local_rows, model_width)
        whole_keys, whole_values = (
            lax.all_gather(keys, "blk", axis=1, tiled=True),
            lax.all_gather(values, "blk", axis=1, tiled=True),
        )
        whole_keys = whole_keys.reshape(seq_count, length, head_count, head_size)
        whole_values = whole_values.reshape(seq_count, length, head_count, head_size)
        log_total, out_exact = attend_forward(
            queries, whole_keys, whole_values, bias_table, meta, key_span
        )
        attended_low = out_exact.reshape(2 * token_rows, model_width).astype(jnp.bfloat16)
        branch = flat_dot(attended_low, proj_full).reshape(seq_count, 2, local_rows, model_width)
        middle, norm_one_back = jax.vjp(
            layer_norm, stream + branch, norm_gains[layer_index, 0], norm_shifts[layer_index, 0]
        )
        middle_low = middle.reshape(2 * token_rows, model_width).astype(jnp.bfloat16)
        inner_pre = flat_dot(middle_low, inner_full)
        activation, gelu_back = jax.vjp(gelu_exact, inner_pre)
        activation_low = activation.astype(jnp.bfloat16)
        outer_out = dot_right_t(activation_low, outer_full).reshape(
            seq_count, 2, local_rows, model_width
        )
        result, norm_two_back = jax.vjp(
            layer_norm, middle + outer_out, norm_gains[layer_index, 1], norm_shifts[layer_index, 1]
        )
        kept_state.append(
            (
                content_rows,
                query_rows,
                queries,
                keys,
                values,
                log_total,
                out_exact,
                attended_low,
                norm_one_back,
                middle_low,
                gelu_back,
                activation_low,
                norm_two_back,
            )
        )
        stream = result
    content_out = stream[:, 0].astype(jnp.bfloat16)
    query_out = stream[:, 1].astype(jnp.bfloat16)
    grad_stream = jnp.stack([cot_content, cot_query], axis=1).astype(jnp.float32)
    gain_rows = [None] * layer_count
    shift_rows = [None] * layer_count
    matrix_rows = [None] * layer_count
    table_grad = jnp.zeros(bias_table.shape, jnp.float32)
    for layer_index in reversed(range(layer_count)):
        (
            content_rows,
            query_rows,
            queries,
            keys,
            values,
            log_total,
            out_exact,
            attended_low,
            norm_one_back,
            middle_low,
            gelu_back,
            activation_low,
            norm_two_back,
        ) = kept_state[layer_index]
        matrices = fetch_again(attn_weights, out_weight, ffn_in, ffn_out_t, layer_index)
        qkv_full, proj_full, inner_full, outer_full = matrices
        grad_sum_two, gain_two, shift_two = norm_two_back(grad_stream)
        grad_outer_low = grad_sum_two.reshape(2 * token_rows, model_width).astype(jnp.bfloat16)
        grad_activation = flat_dot(grad_outer_low, outer_full)
        grad_inner = gelu_back(grad_activation)[0]
        grad_inner_low = grad_inner.astype(jnp.bfloat16)
        grad_middle = grad_sum_two + dot_right_t(grad_inner_low, inner_full).reshape(
            grad_sum_two.shape
        )
        grad_sum_one, gain_one, shift_one = norm_one_back(grad_middle)
        grad_branch_low = grad_sum_one.reshape(2 * token_rows, model_width).astype(jnp.bfloat16)
        grad_attended = (
            dot_right_t(grad_branch_low, proj_full).astype(jnp.bfloat16).reshape(five_shape)
        )
        whole_keys, whole_values = (
            lax.all_gather(keys, "blk", axis=1, tiled=True),
            lax.all_gather(values, "blk", axis=1, tiled=True),
        )
        whole_keys = whole_keys.reshape(seq_count, length, head_count, head_size)
        whole_values = whole_values.reshape(seq_count, length, head_count, head_size)
        row_dots = jnp.transpose(
            jnp.sum(grad_attended.astype(jnp.float32) * out_exact, axis=-1), (0, 3, 1, 2)
        )
        grad_query_sum, table_part, key_terms = attend_backward(
            queries,
            whole_keys,
            whole_values,
            grad_attended,
            row_dots,
            log_total,
            bias_table,
            meta,
            key_span,
        )
        key_sums = lax.psum_scatter(
            key_terms.astype(jnp.bfloat16), "blk", scatter_dimension=0, tiled=True
        ).astype(jnp.float32)
        key_sums = jnp.transpose(key_sums, (1, 0, 2)).astype(jnp.bfloat16)
        table_grad = table_grad + table_part
        grad_keys_low = key_sums[:, :, :model_width].reshape(token_rows, model_width)
        grad_values_low = key_sums[:, :, model_width:].reshape(token_rows, model_width)
        grad_query_low = grad_query_sum.reshape(seq_count, 2, local_rows, model_width).astype(
            jnp.bfloat16
        )
        grad_qkv_content = jnp.concatenate(
            [grad_query_low[:, 0].reshape(token_rows, model_width), grad_keys_low, grad_values_low],
            axis=1,
        )
        grad_query_stream = grad_query_low[:, 1].reshape(token_rows, model_width)
        grad_content_in = dot_right_t(grad_qkv_content, qkv_full).reshape(
            seq_count, local_rows, model_width
        )
        grad_query_in = dot_right_t(grad_query_stream, qkv_full[:, :model_width]).reshape(
            seq_count, local_rows, model_width
        )
        qkv_term = dot_left_t(content_rows, grad_qkv_content)
        qkv_term = qkv_term.at[:, :model_width].add(dot_left_t(query_rows, grad_query_stream))
        proj_term = dot_left_t(attended_low, grad_branch_low)
        inner_term = dot_left_t(middle_low, grad_inner_low)
        outer_term = dot_left_t(grad_outer_low, activation_low)
        grad_shard = lax.psum_scatter(
            jnp.concatenate([qkv_term, proj_term, inner_term, outer_term], axis=1).astype(
                jnp.bfloat16
            ),
            "dp",
            scatter_dimension=0,
            tiled=True,
        )
        matrix_rows[layer_index] = lax.psum(grad_shard, "blk").astype(jnp.float32)
        gain_rows[layer_index] = jnp.stack([gain_one, gain_two], axis=0)
        shift_rows[layer_index] = jnp.stack([shift_one, shift_two], axis=0)
        grad_stream = grad_sum_one + jnp.stack([grad_content_in, grad_query_in], axis=1)
    gains_grad, shifts_grad, table_total = lax.psum(
        (jnp.stack(gain_rows, axis=0), jnp.stack(shift_rows, axis=0), table_grad), ("blk", "dp")
    )
    qkv_width = 3 * model_width
    inner_width = ffn_in.shape[2]
    attn_grad = jnp.stack([rows_all[:, :qkv_width] for rows_all in matrix_rows], axis=0)
    proj_grad = jnp.stack(
        [rows_all[:, qkv_width : qkv_width + model_width] for rows_all in matrix_rows], axis=0
    )
    inner_grad = jnp.stack(
        [
            rows_all[:, qkv_width + model_width : qkv_width + model_width + inner_width]
            for rows_all in matrix_rows
        ],
        axis=0,
    )
    outer_grad = jnp.stack(
        [rows_all[:, qkv_width + model_width + inner_width :] for rows_all in matrix_rows], axis=0
    )
    return (
        content_out,
        query_out,
        grad_stream[:, 0],
        grad_stream[:, 1],
        attn_grad,
        proj_grad,
        inner_grad,
        outer_grad,
        gains_grad,
        shifts_grad,
        table_total,
    )


def solution(mesh):
    placed = (
        P("dp", "blk", None),
        P("dp", "blk", None),
        P("dp", "blk", None),
        P("dp", "blk", None),
        P(None, "dp", None),
        P(None, "dp", None),
        P(None, "dp", None),
        P(None, "dp", None),
        P(),
        P(),
        P(),
        P("dp", None),
        P("dp", None),
        P("dp", None),
    )
    return jax.shard_map(
        shards,
        mesh=mesh,
        in_specs=placed,
        out_specs=(
            P("dp", "blk", None),
            P("dp", "blk", None),
            P("dp", "blk", None),
            P("dp", "blk", None),
            P(None, "dp", None),
            P(None, "dp", None),
            P(None, "dp", None),
            P(None, "dp", None),
            P(),
            P(),
            P(),
        ),
        check_vma=False,
    )
```

profile of v0, /device:TPU:0, one launch (start us, length us, event | category | flops | bytes accessed | tf_op | source)
XLA Modules:
  0.0 2198.1 jit_solution(1486041382215159599)
XLA Ops:
  9.1 51.7 %all-gather.25.cloned.1.call-done = bf16[1,768,2304]{2,1,0:T(8,128)(2,1)} async-done(((bf16[1,48,2304]{2,1,0:T(8,128)(2,1)}), bf16[1,768,2304]{2,1,0:T(8,128)(2,1)}) %all-gather.25.cloned.1.call-update) | async-done | bytes 3538960 | tf_op jit(solution)/shard_map/all_gather | solution.py:169
  95.4 157.6 %while.98 = (s32[]{:T(128)}, f32[1,12,2,512]{3,2,1,0:T(2,128)S(1)}, f32[1,12,2,512]{3,2,1,0:T(2,128)S(1)}, s32[1,512]{1,0:T(1,128)S(1)}, s32[1,1024]{1,0:T(1,128...) while((s32[]{:T(128)}, f32[1,12,2,512]{3,2,1,0:T(2,128)S(1)}, ...), condition=%wide.region_6.8_spmd.clone, body=%wide.region_3.7_spmd.clone.sunk | while | flops 522121984 | bytes 31914464 | solution.py:96
  256.1 130.0 %while.99 = (s32[]{:T(128)}, f32[1,2,512,12,64]{2,4,1,3,0:T(8,128)}, bf16[1,1024,12,64]{1,3,2,0:T(8,128)(2,1)}, s32[1,512]{1,0:T(1,128)S(1)}, s32[1,1024]{1,0:T(...) while((s32[]{:T(128)}, ...), condition=%wide.region_8.10_spmd.clone, body=%wide.region_7.9_spmd.clone.sunk | while | flops 718668544 | bytes 21954532 | solution.py:109
  394.2 35.9 %multiply_convert_fusion.7 = (bf16[1024,3072]{1,0:T(8,128)(2,1)}, f32[1024,3072]{1,0:T(8,128)}, f32[1024,3072]{1,0:T(8,128)}) fusion(bf16[1024,768]{1,0:T(8,128)(2,1)S(1)} %bitcast.863, bf16[1,768,3072]{2,1,0:T(8,128)(2,1)} %all-gather.33.cloned.1.call-done), kind=kOutput, calls=%fused_computation.323 | convolution fusion | flops 5036310528 | bytes 37748736 | tf_op jit(solution)/shard_map/dot_general | solution.py:29
  455.1 20.5 all-gather.41.cloned.1.call-done
  478.6 157.2 %while.100 = (s32[]{:T(128)}, f32[1,12,2,512]{3,2,1,0:T(2,128)S(1)}, f32[1,12,2,512]{3,2,1,0:T(2,128)S(1)}, s32[1,512]{1,0:T(1,128)S(1)}, s32[1,1024]{1,0:T(1,12...) while((s32[]{:T(128)}, f32[1,12,2,512]{3,2,1,0:T(2,128)S(1)}, ...), condition=%wide.region_16.18_spmd.clone, body=%wide.region_13.17_spmd.clone.sunk | while | flops 522121984 | bytes 31914464 | solution.py:96
  639.0 128.6 %while.101 = (s32[]{:T(128)}, f32[1,2,512,12,64]{2,4,1,3,0:T(8,128)}, bf16[1,1024,12,64]{1,3,2,0:T(8,128)(2,1)}, s32[1,512]{1,0:T(1,128)S(1)}, s32[1,1024]{1,0:T...) while((s32[]{:T(128)}, ...), condition=%wide.region_18.20_spmd.clone, body=%wide.region_17.19_spmd.clone.sunk | while | flops 718668544 | bytes 21954532 | solution.py:109
  777.1 36.0 %multiply_convert_fusion.6 = (bf16[1024,3072]{1,0:T(8,128)(2,1)}, f32[1024,3072]{1,0:T(8,128)}, f32[1024,3072]{1,0:T(8,128)}) fusion(bf16[1024,768]{1,0:T(8,128)(2,1)S(1)} %bitcast.865, bf16[1,768,3072]{2,1,0:T(8,128)(2,1)} %all-gather.45.cloned.1.call-done), kind=kOutput, calls=%fused_computation.310 | convolution fusion | flops 5036310528 | bytes 37748736 | tf_op jit(solution)/shard_map/dot_general | solution.py:29
  828.2 16.6 add_convert_fusion.1
  875.4 402.5 %while.102 = (s32[]{:T(128)}, f32[1,2,512,12,64]{2,4,1,3,0:T(8,128)}, f32[32,12]{0,1:T(8,128)}, bf16[1024,1,1536]{0,2,1:T(8,128)(2,1)}, bf16[1,1024,12,64]{1,3,2...) while((s32[]{:T(128)}, ...), condition=%wide.region_30.32_spmd.clone, body=%wide.region_28.31_spmd.clone.sunk | while | flops 1644037632 | bytes 128169648 | solution.py:164
  878.6 12.4 copy.282
  928.0 12.4 copy.282
  978.4 12.4 copy.282
  1028.8 12.4 copy.282
  1079.1 12.4 copy.282
  1129.4 12.4 copy.282
  1179.8 12.4 copy.282
  1230.1 12.4 copy.282
  1283.7 37.8 %reduce-scatter.5.cloned.1.call-done = bf16[512,1,1536]{0,2,1:T(8,128)(2,1)} async-done(((bf16[1024,1,1536]{0,2,1:T(8,128)(2,1)}), bf16[512,1,1536]{0,2,1:T(8,128)(2,1)}) %reduce-scatter.5.cloned.1.call-update) | async-done | bytes 1572880 | tf_op jit(solution)/shard_map/reduce_scatter | solution.py:336
  1333.0 16.5 add_convert_fusion
  1377.1 405.6 %while.103 = (s32[]{:T(128)}, f32[1,2,512,12,64]{2,4,1,3,0:T(8,128)}, f32[32,12]{0,1:T(8,128)}, bf16[1024,1,1536]{0,2,1:T(8,128)(2,1)}, bf16[1,1024,12,64]{1,3,2...) while((s32[]{:T(128)}, ...), condition=%wide.region_39.41_spmd.clone, body=%wide.region_37.40_spmd.clone.sunk | while | flops 1644037632 | bytes 128169648 | solution.py:164
  1383.8 12.4 copy.285
  1433.2 12.4 copy.285
  1483.4 12.4 copy.285
  1533.8 12.4 copy.285
  1584.1 12.4 copy.285
  1634.4 12.4 copy.285
  1684.7 12.4 copy.285
  1735.0 12.4 copy.285
  1893.3 85.6 %reduce-scatter.11.cloned.1.call-done = bf16[48,9216]{1,0:T(8,128)(2,1)} async-done(((bf16[768,9216]{1,0:T(8,128)(2,1)}), bf16[48,9216]{1,0:T(8,128)(2,1)}) %reduce-scatter.11.cloned.1.call-update) | async-done | bytes 884752 | tf_op jit(solution)/shard_map/reduce_scatter | solution.py:362
  1978.9 148.7 %reduce-scatter.9.cloned.1.call-done = bf16[48,9216]{1,0:T(8,128)(2,1)} async-done(((bf16[768,9216]{1,0:T(8,128)(2,1)}), bf16[48,9216]{1,0:T(8,128)(2,1)}) %reduce-scatter.9.cloned.1.call-update) | async-done | bytes 884752 | tf_op jit(solution)/shard_map/reduce_scatter | solution.py:362
  2127.7 40.8 %all-reduce = (f32[2,2,768]{2,1,0:T(2,128)}, f32[2,2,768]{2,1,0:T(2,128)}, f32[32,12]{0,1:T(8,128)}) all-reduce(f32[2,2,768]{2,1,0:T(2,128)S(1)} %pad_maximum_fusion.15, f32[2,2,768]{2,1,0:T(2,128)S(1)} %pad_maximum_fusion.16, f32[32,12]{0,1:T(8,128)S(1)} %add.1278), channel_id=1, replica_groups=mesh['blk'=2,'dp'=16] {'blk','dp'}, use_global_device_ids=true, to_apply=%region_50.52 | all-reduce | flops 6528 | bytes 52224 | tf_op jit(solution)/shard_map/psum | solution.py:374
  (1310 shorter events, 1485.0 us)
Async XLA Ops:
  7.2 53.6 %all-gather.25.cloned.1.call-start = ((), (), s32[]{:S(2)}) async-start(), calls=%async_computation.8 | async-start | bytes 3760128 | tf_op jit(solution)/shard_map/all_gather | solution.py:169
  9.1 83.7 %all-gather.29.cloned.1.call-start = ((), (), s32[]{:S(2)}) async-start(), calls=%async_computation.10 | async-start | bytes 2359296 | tf_op jit(solution)/shard_map/all_gather | solution.py:237
  66.4 187.2 %all-gather.27.cloned.1.call-start = ((), (), s32[]{:S(2)}) async-start(), calls=%async_computation.9 | async-start | bytes 2359296 | tf_op jit(solution)/shard_map/all_gather | solution.py:238
  67.1 321.4 %all-gather.31.cloned.1.call-start = ((), (), s32[]{:S(2)}) async-start(), calls=%async_computation.11 | async-start | bytes 1253376 | tf_op jit(solution)/shard_map/all_gather | solution.py:170
  67.9 326.3 %all-gather.33.cloned.1.call-start = ((), (), s32[]{:S(2)}) async-start(), calls=%async_computation.12 | async-start | bytes 5013504 | tf_op jit(solution)/shard_map/all_gather | solution.py:171
  68.8 361.4 %all-gather.35.cloned.1.call-start = ((), (), s32[]{:S(2)}) async-start(), calls=%async_computation.13 | async-start | bytes 5013504 | tf_op jit(solution)/shard_map/all_gather | solution.py:172
  69.8 372.7 %all-gather.37.cloned.1.call-start = ((), (), s32[]{:S(2)}) async-start(), calls=%async_computation.14 | async-start | bytes 3760128 | tf_op jit(solution)/shard_map/all_gather | solution.py:169
  70.5 405.1 %all-gather.41.cloned.1.call-start = ((), (), s32[]{:S(2)}) async-start(), calls=%async_computation.16 | async-start | bytes 2359296 | tf_op jit(solution)/shard_map/all_gather | solution.py:237
  81.4 311.1 %copy-start.88 = (f32[768]{0:T(1024)}, f32[768]{0:T(1024)S(1)}, u32[]{:S(2)}) copy-start(f32[768]{0:T(1024)S(1)} %get-tuple-element.2067) | copy-start | bytes 9220
  82.1 310.5 %copy-start.109 = (f32[768]{0:T(1024)}, f32[768]{0:T(1024)S(1)}, u32[]{:S(2)}) copy-start(f32[768]{0:T(1024)S(1)} %get-tuple-element.2071) | copy-start | bytes 9220
  392.5 37.7 %copy-start.111 = (f32[2,512]{1,0:T(2,128)}, f32[2,512]{1,0:T(2,128)S(1)}, u32[]{:S(2)}) copy-start(f32[2,512]{1,0:T(2,128)S(1)} %multiply_reduce_fusion.9) | copy-start | bytes 12292
  392.5 37.6 %copy-start.91 = (f32[2,512]{1,0:T(2,128)}, f32[2,512]{1,0:T(2,128)S(1)}, u32[]{:S(2)}) copy-start(f32[2,512]{1,0:T(2,128)S(1)} %fusion.287) | copy-start | bytes 12292
  394.2 36.0 %copy-start.46 = (bf16[2,512,768]{2,1,0:T(8,128)(2,1)}, bf16[2,512,768]{2,1,0:T(8,128)(2,1)S(1)}, u32[]{:S(2)}) copy-start(bf16[2,512,768]{2,1,0:T(8,128)(2,1)S(1)} %fusion.264) | copy-start | bytes 4718596
  440.2 330.9 %copy-start.94 = (f32[2,512]{1,0:T(2,128)}, f32[2,512]{1,0:T(2,128)S(1)}, u32[]{:S(2)}) copy-start(f32[2,512]{1,0:T(2,128)S(1)} %broadcast_multiply_fusion.2) | copy-start | bytes 12292
  440.8 330.4 %copy-start.103 = (f32[2,512]{1,0:T(2,128)}, f32[2,512]{1,0:T(2,128)S(1)}, u32[]{:S(2)}) copy-start(f32[2,512]{1,0:T(2,128)S(1)} %fusion.288) | copy-start | bytes 12292
  448.3 188.1 %all-gather.39.cloned.1.call-start = ((), (), s32[]{:S(2)}) async-start(), calls=%async_computation.15 | async-start | bytes 2359296 | tf_op jit(solution)/shard_map/all_gather | solution.py:238
  449.1 322.1 %all-gather.43.cloned.1.call-start = ((), (), s32[]{:S(2)}) async-start(), calls=%async_computation.17 | async-start | bytes 1253376 | tf_op jit(solution)/shard_map/all_gather | solution.py:170
  449.6 327.4 %all-gather.45.cloned.1.call-start = ((), (), s32[]{:S(2)}) async-start(), calls=%async_computation.18 | async-start | bytes 5013504 | tf_op jit(solution)/shard_map/all_gather | solution.py:171
  450.4 362.7 %all-gather.47.cloned.1.call-start = ((), (), s32[]{:S(2)}) async-start(), calls=%async_computation.19 | async-start | bytes 5013504 | tf_op jit(solution)/shard_map/all_gather | solution.py:172
  451.0 870.5 %reduce-scatter.5.cloned.1.call-start = ((), (), s32[]{:S(2)}) async-start(), calls=%async_computation.4 | async-start | bytes 4718592 | tf_op jit(solution)/shard_map/reduce_scatter | solution.py:336
  453.8 24.7 %copy-start.27 = (f32[32,12]{0,1:T(8,128)S(1)}, f32[32,12]{0,1:T(8,128)}, u32[]{:S(2)}) copy-start(f32[32,12]{0,1:T(8,128)} %copy-done.26) | copy-start | bytes 4612
  775.4 37.7 %copy-start.115 = (f32[2,512]{1,0:T(2,128)}, f32[2,512]{1,0:T(2,128)S(1)}, u32[]{:S(2)}) copy-start(f32[2,512]{1,0:T(2,128)S(1)} %multiply_reduce_fusion.7) | copy-start | bytes 12292
  775.4 37.7 %copy-start.98 = (f32[2,512]{1,0:T(2,128)}, f32[2,512]{1,0:T(2,128)S(1)}, u32[]{:S(2)}) copy-start(f32[2,512]{1,0:T(2,128)S(1)} %fusion.289) | copy-start | bytes 12292
  777.0 36.1 %copy-start.48 = (bf16[2,512,768]{2,1,0:T(8,128)(2,1)}, bf16[2,512,768]{2,1,0:T(8,128)(2,1)S(1)}, u32[]{:S(2)}) copy-start(bf16[2,512,768]{2,1,0:T(8,128)(2,1)S(1)} %fusion.268) | copy-start | bytes 4718596
  1277.9 587.7 %reduce-scatter.7.cloned.1.call-start = ((), (), s32[]{:S(2)}) async-start(), calls=%async_computation.5 | async-start | bytes 4718592 | tf_op jit(solution)/shard_map/reduce_scatter | solution.py:336
  1782.7 196.2 %reduce-scatter.11.cloned.1.call-start = ((), (), s32[]{:S(2)}) async-start(), calls=%async_computation.7 | async-start | bytes 15040512 | tf_op jit(solution)/shard_map/reduce_scatter | solution.py:362
  1833.1 294.5 %reduce-scatter.9.cloned.1.call-start = ((), (), s32[]{:S(2)}) async-start(), calls=%async_computation.6 | async-start | bytes 15040512 | tf_op jit(solution)/shard_map/reduce_scatter | solution.py:362
  1837.2 32.8 %copy-start.32 = (bf16[1,2,512,12,64]{2,4,3,1,0:T(8,128)(2,1)}, bf16[1,2,512,12,64]{2,4,3,1,0:T(8,128)(2,1)S(1)}, u32[]{:S(2)}) copy-start(bf16[1,2,512,12,64]{2,4,3,1,0:T(8,128)(2,1)S(1)} %copy.208) | copy-start | bytes 4718596
  1890.2 295.5 %all-reduce.4.cloned.1.call-start = ((), (), s32[]{:S(2)}) async-start(), calls=%async_computation.20 | async-start | bytes 3538944 | tf_op jit(solution)/shard_map/psum | solution.py:370
  1891.7 276.7 %copy-start.33 = (bf16[1,2,512,12,64]{2,4,3,1,0:T(8,128)(2,1)S(1)}, bf16[1,2,512,12,64]{2,4,3,1,0:T(8,128)(2,1)}, u32[]{:S(2)}) copy-start(bf16[1,2,512,12,64]{2,4,3,1,0:T(8,128)(2,1)} %copy-done.32) | copy-start | bytes 4718596
  1893.2 277.4 %copy-start.65 = (bf16[512,768]{0,1:T(8,128)(2,1)S(1)}, bf16[512,768]{0,1:T(8,128)(2,1)}, u32[]{:S(2)}) copy-start(bf16[512,768]{0,1:T(8,128)(2,1)} %slice_bitcast_fusion.6) | copy-start | bytes 2359300
  1893.2 277.4 %copy-start.71 = (bf16[512,768]{0,1:T(8,128)(2,1)S(1)}, bf16[512,768]{0,1:T(8,128)(2,1)}, u32[]{:S(2)}) copy-start(bf16[512,768]{0,1:T(8,128)(2,1)} %copy-done.70) | copy-start | bytes 2359300
  (201 other events, 846.6 us)
Sparse Core Ops, SparseCore 0:
  10.9 49.8 all-gather.24
  66.5 26.2 all-gather.28
  94.9 27.1 all-gather.26
  124.3 38.3 all-gather.30
  165.3 52.3 all-gather.32
  220.5 51.9 all-gather.34
  274.7 45.7 all-gather.36
  448.4 27.1 all-gather.40
  477.7 27.2 all-gather.38
  507.1 38.3 all-gather.42
  548.4 52.3 all-gather.44
  603.4 51.9 all-gather.46
  1278.0 43.4 reduce-scatter.4
  1782.9 43.3 reduce-scatter.6
  1833.2 145.6 reduce-scatter.10
  1982.9 144.6 reduce-scatter.8
  2129.8 55.7 all-reduce.3
where the time goes:
time: 2210 us; the launch traced here: 2200 us
  matrix products  999 us (45%)
  local copies, waits for them, and re-layouts  533 us (24%)
  waiting for transfers between devices  362 us (16%)
  other arithmetic  238 us (11%)
  blocking collectives  40.8 us (2%)
    reduce_scatter x2, waiting for transfers between devices, shards(): lax.psum_scatter(jnp.concatenate([qkv_term, proj_term, inner_term, outer_...  234 us
    eq x16, local copies, waits for them, and re-layouts, block_scores(): buckets[None] == bucket_ids[:, None, None, None]  198 us
    add x48, local copies, waits for them, and re-layouts, block_scores(): raw_scores * 0.125 + bias[:, :, None]  191 us
    dot_general x48, matrix products, block_scores(): jnp.einsum('bh,bsqk->shqk', bias_table, onehot, precision=lax.Precision.H...  190 us
    dot_general x32, matrix products, block_scores(): jnp.einsum('sjqhd,skhd->shjqk', queries, key_block, preferred_element_typ...  132 us
    dot_general x10, matrix products, flat_dot(): return jnp.dot(left_side, right_side, preferred_element_type=jnp.float32)  125 us
    dot_general x16, matrix products, value_step(): jnp.einsum('shjqk,skhd->sjqhd', weights, value_block, preferred_element_t...  107 us
    dot_general x16, matrix products, back_step(): jnp.einsum('shjqk,skhd->sjqhd', grad_raw, key_block, preferred_element_ty...  97.6 us
  transfers between devices with their start and end apart: 17, of which 7 were waited for; matrix products, arithmetic and copies ran while one was open for 37% of the time, Pallas kernels for 0%

commit v1 on v0

v1 whole, which is shorter than its diff:
```python
import functools

import jax
import jax.numpy as jnp
from jax import lax
from jax.experimental import pallas as pl
from jax.experimental.pallas import tpu as pltpu
from jax.sharding import PartitionSpec as P

THRESHOLDS = (12, 16, 23, 32, 46, 64, 91)
MASKED = -1e30
F32 = jnp.float32
LOW = jnp.bfloat16
VMEM_LIMIT = 56 * 2**20


def dot_nn(left_side, right_side):
    return jnp.dot(left_side, right_side, preferred_element_type=F32)


def dot_nt(left_side, right_side):
    return lax.dot_general(left_side, right_side, (((1,), (1,)), ((), ())), preferred_element_type=F32)


def dot_tn(left_side, right_side):
    return lax.dot_general(left_side, right_side, (((0,), (0,)), ((), ())), preferred_element_type=F32)


def bucket_of(relative):
    distance = jnp.abs(relative)
    far_bucket = 8 + sum(((distance >= threshold).astype(jnp.int32) for threshold in THRESHOLDS))
    near_bucket = jnp.where(distance < 8, distance, jnp.minimum(far_bucket, 15))
    return jnp.where(relative > 0, 16, 0).astype(jnp.int32) + near_bucket


def bias_kernel(table_ref, place_ref, doc_ref, rank_ref, key_doc_ref, key_rank_ref, *refs):
    out_ref = refs[-1]
    head_count, rows, length = out_ref.shape
    place = place_ref[...]
    doc = doc_ref[...]
    rank = rank_ref[...]
    for first in range(0, length, 128):
        key_place = first + lax.broadcasted_iota(jnp.int32, (rows, 128), 1)
        seen = (key_doc_ref[:, first : first + 128] == doc) & (
            key_rank_ref[:, first : first + 128] <= rank
        )
        choice = jnp.where(seen, bucket_of(key_place - place), 32)
        for head in range(head_count):
            for row in range(0, rows, 8):
                line = jnp.broadcast_to(table_ref[head : head + 1, :], (8, 128))
                out_ref[head, row : row + 8, first : first + 128] = jnp.take_along_axis(
                    line, choice[row : row + 8], axis=1
                )


def bias_call(table_rows, place, doc, rank, key_doc, key_rank, *waits):
    head_count = table_rows.shape[0]
    rows, length = place.shape[0], key_doc.shape[1]
    tile = min(32, rows)
    column = pl.BlockSpec((tile, 1), lambda i: (i, 0))
    line = pl.BlockSpec((1, length), lambda i: (0, 0))
    return pl.pallas_call(
        bias_kernel,
        grid=(rows // tile,),
        in_specs=[
            pl.BlockSpec((head_count, 128), lambda i: (0, 0)),
            column,
            column,
            column,
            line,
            line,
        ]
        + [pl.BlockSpec(memory_space=pl.ANY)] * len(waits),
        out_specs=pl.BlockSpec((head_count, tile, length), lambda i: (0, i, 0)),
        out_shape=jax.ShapeDtypeStruct((head_count, rows, length), F32),
        compiler_params=pltpu.CompilerParams(vmem_limit_bytes=VMEM_LIMIT),
        cost_estimate=pl.CostEstimate(
            flops=0, bytes_accessed=head_count * rows * length * 12, transcendentals=0
        ),
        name="bias_rows",
    )(table_rows, place, doc, rank, key_doc, key_rank, *waits)


def attend_kernel(q_ref, k_ref, v_ref, bias_ref, own_ref, *refs):
    o_ref, low_ref, p_ref = refs[-3:]
    rows, length = bias_ref.shape[1:]
    first_half = lax.broadcasted_iota(jnp.int32, (rows, 128), 1) < 64
    key_place = lax.broadcasted_iota(jnp.int32, (rows, length), 1)
    zero = jnp.zeros((rows, 128), LOW)
    for stream in range(2):
        queries = q_ref[stream] * jnp.array(0.125, LOW)
        parts = []
        for half in range(2):
            mine = jnp.where(first_half, queries, zero) if half == 0 else jnp.where(first_half, zero, queries)
            scores = dot_nt(mine, k_ref[...]) + bias_ref[half]
            if stream == 1:
                scores = jnp.where(key_place == own_ref[...], MASKED, scores)
            weights = jnp.exp(scores - jnp.max(scores, axis=1, keepdims=True))
            weights = weights * (1.0 / jnp.sum(weights, axis=1, keepdims=True))
            low = weights.astype(LOW)
            p_ref[half, stream] = low
            parts.append(dot_nn(low, v_ref[...]))
        out = jnp.where(first_half, parts[0], parts[1])
        o_ref[stream] = out
        low_ref[stream] = out.astype(LOW)


def attend_call(queries, keys, values, bias, own, *waits):
    _, rows, width = queries.shape
    length = keys.shape[0]
    tile = min(256, rows)
    pairs = width // 128
    per_row = pl.BlockSpec((2, tile, 128), lambda h, i: (0, i, h))
    per_key = pl.BlockSpec((length, 128), lambda h, i: (0, h))
    return pl.pallas_call(
        attend_kernel,
        grid=(pairs, rows // tile),
        in_specs=[
            per_row,
            per_key,
            per_key,
            pl.BlockSpec((2, tile, length), lambda h, i: (h, i, 0)),
            pl.BlockSpec((tile, 1), lambda h, i: (i, 0)),
        ]
        + [pl.BlockSpec(memory_space=pl.ANY)] * len(waits),
        out_specs=[
            per_row,
            per_row,
            pl.BlockSpec((2, 2, tile, length), lambda h, i: (h, 0, i, 0)),
        ],
        out_shape=[
            jax.ShapeDtypeStruct((2, rows, width), F32),
            jax.ShapeDtypeStruct((2, rows, width), LOW),
            jax.ShapeDtypeStruct((2 * pairs, 2, rows, length), LOW),
        ],
        compiler_params=pltpu.CompilerParams(vmem_limit_bytes=VMEM_LIMIT),
        cost_estimate=pl.CostEstimate(
            flops=16 * rows * length * width,
            bytes_accessed=pairs * rows * length * 16,
            transcendentals=4 * pairs * rows * length,
        ),
        name="attend",
    )(queries, keys, values, bias, own, *waits)


def attend_back_kernel(earlier, *refs):
    q_ref, k_ref, v_ref, do_ref, o_ref, p_ref = refs[:6]
    dq_ref, dk_ref, dv_ref, sum_ref, dk_sum, dv_sum = refs[-6:]
    rows = q_ref.shape[1]
    first_half = lax.broadcasted_iota(jnp.int32, (rows, 128), 1) < 64
    zero = jnp.zeros((rows, 128), LOW)

    @pl.when(pl.program_id(1) == 0)
    def _():
        dk_sum[...] = jnp.zeros_like(dk_sum)
        dv_sum[...] = jnp.zeros_like(dv_sum)

    grads = [[None, None], [None, None]]
    for half in range(2):
        span = slice(64 * half, 64 * half + 64)
        total = refs[6][half] if earlier else None
        for stream in range(2):
            grad_out = do_ref[stream]
            mine = jnp.where(first_half, grad_out, zero) if half == 0 else jnp.where(first_half, zero, grad_out)
            delta = jnp.sum(mine.astype(F32) * o_ref[stream], axis=1, keepdims=True)
            low_p = p_ref[half, stream]
            grad = low_p.astype(F32) * (dot_nt(mine, v_ref[...]) - delta)
            total = grad if total is None else total + grad
            low = grad.astype(LOW)
            grads[stream][half] = dot_nn(low, k_ref[...])
            queries = q_ref[stream] * jnp.array(0.125, LOW)
            dk_sum[span, :] += dot_nn(queries.T[span], low)
            dv_sum[span, :] += dot_nn(grad_out.T[span], low_p)
        sum_ref[half] = total
    for stream in range(2):
        dq_ref[stream] = (jnp.where(first_half, grads[stream][0], grads[stream][1]) * 0.125).astype(LOW)

    @pl.when(pl.program_id(1) == pl.num_programs(1) - 1)
    def _():
        dk_ref[...] = dk_sum[...].T.astype(LOW)
        dv_ref[...] = dv_sum[...].T.astype(LOW)


def attend_back_call(span, queries, keys, values, grad_out, out, weights, earlier, partial, *waits):
    first, pairs = span
    rows, width = queries.shape[1:]
    length = keys.shape[0]
    tile = min(256, rows)
    per_row = pl.BlockSpec((2, tile, 128), lambda h, i: (0, i, h + first))
    per_key = pl.BlockSpec((length, 128), lambda h, i: (0, h + first))
    per_score = pl.BlockSpec((2, tile, length), lambda h, i: (h + first, i, 0))
    more = [] if earlier is None else [earlier]
    begun = [] if partial is None else list(partial)
    return pl.pallas_call(
        functools.partial(attend_back_kernel, earlier is not None),
        grid=(pairs, rows // tile),
        in_specs=[
            per_row,
            per_key,
            per_key,
            per_row,
            per_row,
            pl.BlockSpec((2, 2, tile, length), lambda h, i: (h + first, 0, i, 0)),
        ]
        + [per_score] * len(more)
        + [pl.BlockSpec(memory_space=pl.ANY)] * len(begun + list(waits)),
        out_specs=[per_row, per_key, per_key, per_score],
        out_shape=[
            jax.ShapeDtypeStruct((2, rows, width), LOW),
            jax.ShapeDtypeStruct((length, width), LOW),
            jax.ShapeDtypeStruct((length, width), LOW),
            jax.ShapeDtypeStruct((width // 64, rows, length), F32),
        ],
        input_output_aliases={6 + len(more) + index: index for index in range(len(begun))},
        scratch_shapes=[pltpu.VMEM((128, length), F32)] * 2,
        compiler_params=pltpu.CompilerParams(vmem_limit_bytes=VMEM_LIMIT),
        cost_estimate=pl.CostEstimate(
            flops=32 * rows * length * 128 * pairs,
            bytes_accessed=pairs * rows * length * 24,
            transcendentals=0,
        ),
        name="attend_back",
    )(queries, keys, values, grad_out, out, weights, *more, *begun, *waits)


def table_kernel(sum_count, *refs):
    sum_refs, place_ref, out_ref = refs[:sum_count], refs[sum_count], refs[-1]
    rows, length = sum_refs[0].shape[1:]
    head_count = sum(sum_ref.shape[0] for sum_ref in sum_refs)
    bucket_count = out_ref.shape[0] // 8

    @pl.when(pl.program_id(0) == 0)
    def _():
        out_ref[...] = jnp.zeros_like(out_ref)

    key_place = lax.broadcasted_iota(jnp.int32, (8, length), 1)
    total = jnp.zeros(out_ref.shape, F32)
    for row in range(0, rows, 8):
        choice = bucket_of(key_place - place_ref[row : row + 8])
        chosen = jnp.concatenate(
            [jnp.where(choice == bucket, 1.0, 0.0) for bucket in range(bucket_count)], axis=0
        ).astype(LOW)
        part = jnp.concatenate([sum_ref[:, row : row + 8, :] for sum_ref in sum_refs], axis=0)
        part = part.reshape(head_count * 8, length).astype(LOW)
        total = total + dot_nt(chosen, part)
    out_ref[...] += total


def table_call(score_sums, place, bucket_count, *waits):
    rows, length = score_sums[0].shape[1:]
    head_count = sum(score_sum.shape[0] for score_sum in score_sums)
    tile = min(32, rows)
    grouped = pl.pallas_call(
        functools.partial(table_kernel, len(score_sums)),
        grid=(rows // tile,),
        in_specs=[
            pl.BlockSpec((score_sum.shape[0], tile, length), lambda i: (0, i, 0)) for score_sum in score_sums
        ]
        + [pl.BlockSpec((tile, 1), lambda i: (i, 0))]
        + [pl.BlockSpec(memory_space=pl.ANY)] * len(waits),
        out_specs=pl.BlockSpec((8 * bucket_count, 8 * head_count), lambda i: (0, 0)),
        out_shape=jax.ShapeDtypeStruct((8 * bucket_count, 8 * head_count), F32),
        compiler_params=pltpu.CompilerParams(vmem_limit_bytes=VMEM_LIMIT),
        cost_estimate=pl.CostEstimate(
            flops=512 * rows * length * head_count,
            bytes_accessed=rows * length * head_count * 4,
            transcendentals=0,
        ),
        name="table_sums",
    )(*score_sums, place, *waits)
    grouped = grouped.reshape(bucket_count, 8, head_count, 8)
    return jnp.sum(grouped * jnp.eye(8, dtype=F32)[None, :, None, :], axis=(1, 3))


def norm_rows(tensor, scale_row, shift_row):
    center = tensor - jnp.mean(tensor, axis=1, keepdims=True)
    inverse = lax.rsqrt(jnp.mean(center * center, axis=1, keepdims=True) + 1e-05)
    return center * inverse * scale_row + shift_row, inverse


def norm_rows_back(grad, normal, inverse, scale_row):
    scaled = grad * scale_row
    mean_one = jnp.mean(scaled, axis=1, keepdims=True)
    mean_two = jnp.mean(scaled * normal, axis=1, keepdims=True)
    return inverse * (scaled - mean_one - normal * mean_two)


def pieces_of(pieces):
    arrays, plan = [], []
    for pair in pieces:
        spots = []
        for array, first in pair:
            known = [i for i, other in enumerate(arrays) if other is array]
            if not known:
                arrays.append(array)
            spots.append((known[0] if known else len(arrays) - 1, first))
        plan.append(tuple(spots))
    return arrays, tuple(plan)


def layer_tail_kernel(count, plan, span, *refs):
    (stream_ref, out_ref, proj_ref), refs = refs[:3], refs[3:]
    piece_refs, refs = refs[:count], refs[count:]
    gain_ref, shift_ref = refs[:2]
    result_ref, low_ref, middle_ref, middle_low_ref, active_ref, slope_ref, one_ref, two_ref = refs[-8:]
    mixed = stream_ref[...] + dot_nn(out_ref[...], proj_ref[...])
    middle, one_ref[...] = norm_rows(mixed, gain_ref[0:1], shift_ref[0:1])
    middle_ref[...] = middle
    middle_low = middle.astype(LOW)
    middle_low_ref[...] = middle_low
    total = middle
    for index, ((inner_at, inner_first), (outer_at, outer_first)) in enumerate(plan):
        columns = slice(index * span, (index + 1) * span)
        inner = dot_nn(middle_low, piece_refs[inner_at][:, inner_first : inner_first + span])
        cdf = 0.5 + 0.5 * lax.erf(inner * (2.0**-0.5))
        active = (inner * cdf).astype(LOW)
        active_ref[:, columns] = active
        density = jnp.exp(inner * inner * -0.5) * 0.3989422804014327
        slope_ref[:, columns] = (cdf + inner * density).astype(LOW)
        total = total + dot_nt(active, piece_refs[outer_at][:, outer_first : outer_first + span])
    result, two_ref[...] = norm_rows(total, gain_ref[1:2], shift_ref[1:2])
    result_ref[...] = result
    low_ref[...] = result.astype(LOW)


def layer_tail_call(stream, out_low, proj, pieces, span, gains, shifts, *waits):
    rows, width = stream.shape
    hidden = span * len(pieces)
    pieces, plan = pieces_of(pieces)
    proj, proj_at = proj
    tile = min(256, rows)

    def per_row(columns):
        return pl.BlockSpec((tile, columns), lambda i: (i, 0))

    def fixed(shape):
        return pl.BlockSpec(shape, lambda i: (0, 0), pipeline_mode=pl.Buffered(1))

    def whole(columns, kind):
        return jax.ShapeDtypeStruct((rows, columns), kind)

    return pl.pallas_call(
        functools.partial(layer_tail_kernel, len(pieces), plan, span),
        grid=(rows // tile,),
        in_specs=[per_row(width), per_row(width), pl.BlockSpec((width, width), lambda i: (0, proj_at), pipeline_mode=pl.Buffered(1))]
        + [fixed(piece.shape) for piece in pieces]
        + [fixed((2, width))] * 2
        + [pl.BlockSpec(memory_space=pl.ANY)] * len(waits),
        out_specs=[
            per_row(width), per_row(width), per_row(width), per_row(width),
            per_row(hidden), per_row(hidden), per_row(1), per_row(1),
        ],
        out_shape=[
            whole(width, F32), whole(width, LOW), whole(width, F32), whole(width, LOW),
            whole(hidden, LOW), whole(hidden, LOW), whole(1, F32), whole(1, F32),
        ],
        compiler_params=pltpu.CompilerParams(vmem_limit_bytes=VMEM_LIMIT),
        cost_estimate=pl.CostEstimate(
            flops=2 * rows * width * (width + 2 * hidden),
            bytes_accessed=4 * rows * hidden + 12 * rows * width + 4 * width * hidden,
            transcendentals=2 * rows * hidden,
        ),
        name="layer_tail",
    )(stream, out_low, proj, *pieces, gains, shifts, *waits)


def layer_tail_back_kernel(count, plan, span, *refs):
    (grad_ref, result_ref, two_ref, middle_ref, one_ref, slope_ref, proj_ref), refs = refs[:7], refs[7:]
    piece_refs, refs = refs[:count], refs[count:]
    gain_ref, shift_ref, begun_ref = refs[:3]
    two_low_ref, inner_ref, stream_ref, branch_ref, out_ref, terms_ref = refs[-6:]

    @pl.when(pl.program_id(0) == 0)
    def _():
        terms_ref[...] = begun_ref[...]

    grad = grad_ref[...]
    normal = (result_ref[...] - shift_ref[1:2]) / gain_ref[1:2]
    terms_ref[1:2] += jnp.sum(grad * normal, axis=0, keepdims=True)
    terms_ref[3:4] += jnp.sum(grad, axis=0, keepdims=True)
    grad = norm_rows_back(grad, normal, two_ref[...], gain_ref[1:2])
    low = grad.astype(LOW)
    two_low_ref[...] = low
    for index, ((inner_at, inner_first), (outer_at, outer_first)) in enumerate(plan):
        columns = slice(index * span, (index + 1) * span)
        outer_piece = piece_refs[outer_at][:, outer_first : outer_first + span]
        inner = (dot_nn(low, outer_piece) * slope_ref[:, columns].astype(F32)).astype(LOW)
        inner_ref[:, columns] = inner
        grad = grad + dot_nt(inner, piece_refs[inner_at][:, inner_first : inner_first + span])
    normal = (middle_ref[...] - shift_ref[0:1]) / gain_ref[0:1]
    terms_ref[0:1] += jnp.sum(grad * normal, axis=0, keepdims=True)
    terms_ref[2:3] += jnp.sum(grad, axis=0, keepdims=True)
    grad = norm_rows_back(grad, normal, one_ref[...], gain_ref[0:1])
    stream_ref[...] = grad
    low = grad.astype(LOW)
    branch_ref[...] = low
    out_ref[...] = dot_nt(low, proj_ref[...]).astype(LOW)


def layer_tail_back_call(grad, result, two, middle, one, slope, proj, pieces, span, gains, shifts, part, partial, *waits):
    rows, width = result.shape
    share = 1 if part is None else 2
    hidden = span * len(pieces)
    pieces, plan = pieces_of(pieces)
    proj, proj_at = proj
    tile = min(256, rows // share)

    first = (part or 0) * (rows // 2 // tile)
    begun = [] if partial is None else list(partial[:-1])
    terms = jnp.zeros((8, width), F32) if partial is None else partial[-1]

    def per_row(columns):
        return pl.BlockSpec((tile, columns), lambda i: (i + first, 0))

    def fixed(shape):
        return pl.BlockSpec(shape, lambda i: (0, 0), pipeline_mode=pl.Buffered(1))

    def whole(columns, kind):
        return jax.ShapeDtypeStruct((rows, columns), kind)

    return pl.pallas_call(
        functools.partial(layer_tail_back_kernel, len(pieces), plan, span),
        grid=(rows // share // tile,),
        in_specs=[pl.BlockSpec((tile, width), lambda i: (i, 0)), per_row(width), per_row(1), per_row(width), per_row(1), per_row(hidden)]
        + [pl.BlockSpec((width, width), lambda i: (0, proj_at), pipeline_mode=pl.Buffered(1))]
        + [fixed(piece.shape) for piece in pieces]
        + [fixed((2, width))] * 2
        + [fixed((8, width))]
        + [pl.BlockSpec(memory_space=pl.ANY)] * len(begun + list(waits)),
        out_specs=[
            per_row(width), per_row(hidden), per_row(width), per_row(width), per_row(width),
            pl.BlockSpec((8, width), lambda i: (0, 0)),
        ],
        out_shape=[
            whole(width, LOW), whole(hidden, LOW), whole(width, F32), whole(width, LOW), whole(width, LOW),
            jax.ShapeDtypeStruct((8, width), F32),
        ],
        input_output_aliases={10 + len(pieces) + index: index for index in range(len(begun))},
        compiler_params=pltpu.CompilerParams(vmem_limit_bytes=VMEM_LIMIT),
        cost_estimate=pl.CostEstimate(
            flops=2 * rows // share * width * (width + 2 * hidden),
            bytes_accessed=4 * rows * hidden + 20 * rows * width + 4 * width * hidden,
            transcendentals=0,
        ),
        name="layer_tail_back",
    )(grad, result, two, middle, one, slope, proj, *pieces, gains, shifts, terms, *begun, *waits)


def product_kernel(plan, side_ref, *refs):
    step = pl.program_id(0)
    for index, (lhs, rhs, out, plus) in enumerate(plan):

        @pl.when(step == index)
        def _(lhs=lhs, rhs=rhs, out=out, plus=plus):
            total = dot_tn(refs[lhs][...], refs[rhs][...])
            if plus is not None:
                total = total + refs[plus][...].astype(F32)
            refs[out][...] = total.astype(refs[out].dtype)


def products_call(name, side, steps, outs, waits=()):
    arrays, specs, plan, place = [], [], [], {}
    total = len(steps)

    def column_of(kind, side_ref):
        if kind == "side":
            return side_ref[0]
        if kind == "other":
            return 1 - side_ref[0]
        return kind

    def chain(at):
        table = []
        for step in range(total):
            later = [at[u] for u in sorted(at) if u >= step]
            table.append(later[0] if later else at[max(at)])
        def index(i, side_ref):
            value = column_of(table[-1], side_ref)
            for step in reversed(range(total - 1)):
                if table[step] != table[step + 1]:
                    value = jnp.where(i <= step, column_of(table[step], side_ref), value)
            return (0, value)
        return index

    uses = {}
    for step, (lhs, rhs, span, block, out, out_block, plus) in enumerate(steps):
        uses.setdefault(("in", id(lhs), lhs.shape[1]), [lhs, {}])[1][step] = 0
        uses.setdefault(("in", id(rhs), span), [rhs, {}])[1][step] = block
        if plus is not None:
            uses.setdefault(("in", id(plus), outs[out][2]), [plus, {}])[1][step] = out_block
    for key, (array, at) in uses.items():
        place[key] = len(arrays)
        arrays.append(array)
        specs.append(pl.BlockSpec((array.shape[0], key[2]), chain(at)))
    first_out = len(arrays) + len(waits)
    out_names = list(outs)
    out_specs = []
    for out in out_names:
        at = {step: entry[5] for step, entry in enumerate(steps) if entry[4] == out}
        out_specs.append(pl.BlockSpec((outs[out][0], outs[out][2]), chain(at)))
    flops = 0
    for lhs, rhs, span, block, out, out_block, plus in steps:
        flops += 2 * lhs.shape[0] * lhs.shape[1] * span
        plan.append(
            (
                place[("in", id(lhs), lhs.shape[1])],
                place[("in", id(rhs), span)],
                first_out + out_names.index(out),
                None if plus is None else place[("in", id(plus), outs[out][2])],
            )
        )
    results = pl.pallas_call(
        functools.partial(product_kernel, plan),
        grid_spec=pltpu.PrefetchScalarGridSpec(
            num_scalar_prefetch=1,
            grid=(total,),
            in_specs=specs + [pl.BlockSpec(memory_space=pl.ANY)] * len(waits),
            out_specs=out_specs,
        ),
        out_shape=[jax.ShapeDtypeStruct(outs[out][:2], LOW) for out in out_names],
        compiler_params=pltpu.CompilerParams(vmem_limit_bytes=VMEM_LIMIT),
        cost_estimate=pl.CostEstimate(flops=flops, bytes_accessed=flops // 300, transcendentals=0),
        name=name,
    )(side, *arrays, *waits)
    return dict(zip(out_names, results))


def hold_kernel(*refs):
    del refs


def hold(tensor, *waits):
    anywhere = pl.BlockSpec(memory_space=pl.ANY)
    return pl.pallas_call(
        hold_kernel,
        in_specs=[anywhere] * (1 + len(waits)),
        out_specs=anywhere,
        out_shape=jax.ShapeDtypeStruct(tensor.shape, tensor.dtype),
        input_output_aliases={0: 0},
        cost_estimate=pl.CostEstimate(flops=0, bytes_accessed=0, transcendentals=0),
        name="hold",
    )(tensor, *waits)


def place_kernel(count, place_ref, *refs):
    out_ref = refs[-1]
    for index in range(count):
        out_ref[place_ref[index]] = refs[index][...]


def place_call(name, parts, spots, waits):
    shape = (len(parts), *parts[0].shape)
    return pl.pallas_call(
        functools.partial(place_kernel, len(parts)),
        in_specs=[pl.BlockSpec(memory_space=pltpu.SMEM)]
        + [pl.BlockSpec(memory_space=pltpu.VMEM)] * len(parts)
        + [pl.BlockSpec(memory_space=pl.ANY)] * len(waits),
        out_specs=pl.BlockSpec(memory_space=pltpu.VMEM),
        out_shape=jax.ShapeDtypeStruct(shape, parts[0].dtype),
        compiler_params=pltpu.CompilerParams(vmem_limit_bytes=VMEM_LIMIT),
        cost_estimate=pl.CostEstimate(flops=0, bytes_accessed=4 * parts[0].size * len(parts), transcendentals=0),
        name=name,
    )(jnp.stack(spots).astype(jnp.int32), *parts, *waits)


def weave_kernel(count, place_ref, *refs):
    out_ref = refs[-1]
    for index in range(count):
        for row in range(refs[index].shape[0]):
            out_ref[row, place_ref[index]] = refs[index][row]


def weave_call(name, parts, spots, waits):
    lead, *rest = parts[0].shape
    return pl.pallas_call(
        functools.partial(weave_kernel, len(parts)),
        in_specs=[pl.BlockSpec(memory_space=pltpu.SMEM)]
        + [pl.BlockSpec(memory_space=pltpu.VMEM)] * len(parts)
        + [pl.BlockSpec(memory_space=pl.ANY)] * len(waits),
        out_specs=pl.BlockSpec(memory_space=pltpu.VMEM),
        out_shape=jax.ShapeDtypeStruct((lead, len(parts), *rest), parts[0].dtype),
        compiler_params=pltpu.CompilerParams(vmem_limit_bytes=VMEM_LIMIT),
        cost_estimate=pl.CostEstimate(flops=0, bytes_accessed=4 * parts[0].size * len(parts), transcendentals=0),
        name=name,
    )(jnp.stack(spots).astype(jnp.int32), *parts, *waits)


class Grid:
    def __init__(self, mesh):
        self.blocks = mesh.shape["blk"]
        self.total = mesh.shape["dp"]
        self.paired = self.blocks == 2 and self.total == 16
        self.high = 4
        self.low = self.total // 8

    def place(self):
        index = lax.axis_index("dp")
        self.core_at = index % 2
        self.low_at = index // 2 % self.low
        self.high_at = index // (2 * self.low)
        self.block_at = lax.axis_index("blk")

    def from_core(self, tensor):
        return lax.ppermute(tensor, "dp", [(i, i ^ 1) for i in range(self.total)])

    def from_block(self, tensor):
        return lax.ppermute(tensor, "blk", [(0, 1), (1, 0)])

    def from_low(self, tensor, step):
        span = 2 * self.low
        pairs = [(i, i // span * span + (i + 2 * step) % span) for i in range(self.total)]
        return lax.ppermute(tensor, "dp", pairs)

    def from_high(self, tensor, step):
        return lax.ppermute(tensor, "dp", [(i, (i + 2 * self.low * step) % self.total) for i in range(self.total)])

    def gather(self, shard):
        return lax.all_gather(shard, "dp", axis=0, tiled=True)

    def gather_chip(self, shards, waits):
        rows, columns = shards[0].shape
        width = columns // 4

        def quarter(core):
            first = (2 * self.block_at + core) * width
            parts = [lax.dynamic_slice_in_dim(shard, first, width, 1) for shard in shards]
            return jnp.concatenate(parts, axis=1) if len(parts) > 1 else parts[0]

        mine = quarter(self.core_at)
        other = self.from_core(quarter(1 - self.core_at))
        chip = place_call("chip_rows", [mine, other], [self.core_at, 1 - self.core_at], waits)
        return chip.reshape(2 * rows, -1)

    def gather_line(self, chip, waits):
        parts = [chip] + [self.from_high(chip, step) for step in range(1, self.high)]
        spots = [(self.high_at - step) % self.high for step in range(self.high)]
        return place_call("line_rows", parts, spots, waits)

    def gather_sheet(self, line, waits):
        parts = [line] + [self.from_low(line, step) for step in range(1, self.low)]
        spots = [(self.low_at - step) % self.low for step in range(self.low)]
        return weave_call("sheet_rows", parts, spots, waits).reshape(-1, line.shape[2])

    def scatter_begin(self, tensor, axis):
        size, index, send = (
            (self.low, self.low_at, self.from_low) if axis == 1 else (self.high, self.high_at, self.from_high)
        )

        def at(step):
            return lax.dynamic_index_in_dim(tensor, (index + step) % size, axis, False)

        return at(0), [send(at(step), step) for step in range(1, size)]

    def low_begin(self, tensor):
        rows, columns = tensor.shape
        return self.scatter_begin(tensor.reshape(self.high, self.low, -1, columns), 1)

    def high_begin(self, tensor):
        return self.scatter_begin(tensor, 0)

    def scatter_end(self, begun, *waits):
        own, arrived = begun
        if waits:
            arrived = [hold(arrived[0], *waits), *arrived[1:]]
        return sum((tensor.astype(F32) for tensor in arrived), own.astype(F32)).astype(LOW)

    def sum_blocks(self, tensor):
        return (tensor.astype(F32) + self.from_block(tensor).astype(F32)).astype(LOW)

    def halves(self, tensor):
        rows = tensor.shape[0] // 2
        own = lax.dynamic_slice_in_dim(tensor, self.core_at * rows, rows, 0)
        other = self.from_core(lax.dynamic_slice_in_dim(tensor, (1 - self.core_at) * rows, rows, 0))
        first = self.core_at == 0
        return jnp.where(first, own, other), jnp.where(first, other, own)

    def sum_all(self, tensor):
        if not self.paired or self.total & (self.total - 1):
            return lax.psum(tensor, ("blk", "dp"))
        tensor = tensor + self.from_block(tensor)
        bit = 1
        while bit < self.total:
            tensor = tensor + lax.ppermute(tensor, "dp", [(i, i ^ bit) for i in range(self.total)])
            bit *= 2
        return tensor

    def scatter(self, tensor):
        part = lax.psum_scatter(tensor, "dp", scatter_dimension=0, tiled=True)
        if self.blocks == 2:
            return part.astype(F32) + self.from_block(part).astype(F32)
        return lax.psum(part, "blk").astype(F32)


def shards(
    grid,
    content_in,
    query_in,
    cot_content,
    cot_query,
    attn_weights,
    out_weight,
    ffn_in,
    ffn_out_t,
    norm_gains,
    norm_shifts,
    bias_table,
    permutation,
    predicted,
    doc_lengths,
):
    _, rows, width = content_in.shape
    length = permutation.shape[1]
    blocks = length // rows
    bucket_count, head_count = bias_table.shape
    layer_count = attn_weights.shape[0]
    grid.place()
    block_index = grid.block_at

    anchor = permutation[0]
    positions = jnp.arange(length, dtype=jnp.int32)
    bounds = jnp.cumsum(doc_lengths[0])[:-1].astype(jnp.int32)
    key_doc = jnp.sum((positions[:, None] >= bounds[None, :]).astype(jnp.int32), axis=1)
    starts = (positions == 0) | jnp.any(positions[:, None] == bounds[None, :], axis=1)
    live = (predicted[0] == 1) & jnp.logical_not(starts)
    position_rank = jnp.sum(
        jnp.where(anchor[None, :] == positions[:, None], positions[None, :], 0), axis=1
    )
    key_rank = jnp.where(live, position_rank, -1)
    split = anchor.reshape(blocks, rows)
    order = jnp.sum((split[:, None, :] < split[:, :, None]).astype(jnp.int32), axis=2)
    sorted_place = jnp.sum(
        jnp.where(order[:, None, :] == jnp.arange(rows)[None, :, None], split[:, None, :], 0), axis=2
    )
    own_order = lax.dynamic_index_in_dim(order, block_index, 0, False)
    place = lax.dynamic_index_in_dim(sorted_place, block_index, 0, False)
    sorter = (own_order[None, :] == jnp.arange(rows)[:, None]).astype(LOW)
    if grid.paired:
        own_spread, other_spread = (
            (lax.dynamic_index_in_dim(sorted_place, side, 0, True) == positions[:, None]).astype(LOW)
            for side in (block_index, 1 - block_index)
        )
    spread = (sorted_place.reshape(1, length) == positions[:, None]).astype(LOW)
    at_place = (place[:, None] == positions[None, :]).astype(jnp.int32)
    place_doc = jnp.sum(at_place * key_doc[None, :], axis=1)
    place_rank = jnp.sum(at_place * position_rank[None, :], axis=1)
    place_live = jnp.sum(at_place * live.astype(jnp.int32)[None, :], axis=1)
    own_column = jnp.where(place_live == 1, place, -1)[:, None]
    place_column = place[:, None]
    table_rows = jnp.concatenate(
        [bias_table.T, jnp.full((head_count, 128 - bucket_count), MASKED, F32)], axis=1
    )

    def sort_rows(tensor):
        return dot_nn(sorter, tensor).astype(LOW)

    def other_blocks(tensor):
        if grid.paired:
            other = grid.from_block(tensor)
            return (dot_nn(own_spread, tensor) + dot_nn(other_spread, other)).astype(LOW)
        gathered = lax.all_gather(tensor, "blk", axis=0, tiled=True)
        return dot_nn(spread, gathered).astype(LOW)

    paired = grid.paired
    first_qkv = grid.gather(attn_weights[0])
    others = jnp.concatenate(
        [out_weight[layer_index] for layer_index in range(layer_count)]
        + [attn_weights[layer_index] for layer_index in range(1, layer_count)],
        axis=1,
    )
    others = grid.gather(others)
    starts = [(layer_count + 3 * layer_index) * width for layer_index in range(layer_count - 1)]
    attn_full = [first_qkv] + [others[:, start : start + 3 * width] for start in starts]
    hidden = ffn_in.shape[2]
    span = hidden // 4 if paired else hidden

    def chip_of(layer_index, *waits):
        return grid.gather_chip((ffn_in[layer_index], ffn_out_t[layer_index]), waits)

    stream_low = jnp.concatenate([sort_rows(content_in[0]), sort_rows(query_in[0])], axis=0)
    stream = stream_low.astype(F32)
    if paired:
        chip = chip_of(0)
    bias = bias_call(
        table_rows, place_column, place_doc[:, None], place_rank[:, None], key_doc[None], key_rank[None],
        *((chip, stream_low) if paired else ()),
    )
    if paired:
        line = grid.gather_line(chip, (bias,))
        if layer_count > 1:
            next_chip = chip_of(1, line)
    kept = []
    all_pieces = []
    for layer_index in range(layer_count):
        qkv = attn_full[layer_index]
        all_content = other_blocks(stream_low[:rows])
        queries = dot_nn(stream_low, qkv[:, :width]).astype(LOW).reshape(2, rows, width)
        keys = dot_nn(all_content, qkv[:, width : 2 * width]).astype(LOW)
        values = dot_nn(all_content, qkv[:, 2 * width :]).astype(LOW)
        later = ()
        more = paired and layer_index + 1 < layer_count
        if paired:
            sheet = grid.gather_sheet(line, (queries, keys, values))
            later = (sheet,)
        if more:
            later = (sheet, next_chip)
        out, out_low, weights = attend_call(queries, keys, values, bias, own_column, *later)
        later = ()
        if paired:
            waits_near = (out_low,)
            if more:
                line = grid.gather_line(next_chip, (out_low,))
                waits_near = (out_low, line)
            near = hold(grid.from_block(sheet), *waits_near)
            quarters = (sheet, grid.from_core(sheet), near, grid.from_core(near))
            pieces = [((quarter, 0), (quarter, span)) for quarter in quarters]
        else:
            pieces = [((grid.gather(ffn_in[layer_index]), 0), (grid.gather(ffn_out_t[layer_index]), 0))]
        all_pieces.append(pieces)
        if more:
            later = (line,)
            if layer_index + 2 < layer_count:
                next_chip = chip_of(layer_index + 2, line)
        out_low = out_low.reshape(2 * rows, width)
        result, low, middle, middle_low, active, slope, inverse_one, inverse_two = layer_tail_call(
            stream, out_low, (others, layer_index), pieces, span,
            norm_gains[layer_index], norm_shifts[layer_index], *later,
        )
        kept.append(
            (
                stream_low, all_content, queries, keys, values, out, out_low, weights,
                result, middle, middle_low, active, slope, inverse_one, inverse_two,
            )
        )
        stream, stream_low = result, low

    def unsort(tensor):
        return dot_tn(sorter, tensor)

    def unsort_wide(tensor):
        high = tensor.astype(LOW)
        rest = (tensor - high.astype(F32)).astype(LOW)
        return unsort(high) + unsort(rest)

    content_out = unsort(stream_low[:rows]).astype(LOW)
    query_out = unsort(stream_low[rows:]).astype(LOW)

    grad_stream = [sort_rows(cot_content[0]).astype(F32), sort_rows(cot_query[0]).astype(F32)]
    norm_terms = [None] * layer_count
    matrix_rows = [None] * layer_count
    side = jnp.full((1,), grid.core_at, jnp.int32)
    pairs = width // 128
    score_sum = None
    pending = {}
    third = width // 2

    def keys_back(grad_k, grad_v, qkv):
        return (dot_nt(grad_k, qkv[:, width : 2 * width]) + dot_nt(grad_v, qkv[:, 2 * width :])).astype(LOW)

    def finish_rows(high):
        shared = grid.sum_blocks(high[:, 2 * span :])
        sides = grid.halves(jnp.concatenate([high[:, : 2 * span], shared], axis=1))
        proj_grad = jnp.concatenate([one[:, 2 * span : 2 * span + third] for one in sides], axis=1)
        attn_grad = jnp.concatenate(
            [
                one[:, 2 * span + (1 + index) * third : 2 * span + (2 + index) * third]
                for index in range(3)
                for one in sides
            ],
            axis=1,
        )
        half = jnp.concatenate([one[:, : 2 * span] for one in sides], axis=1)
        other = grid.from_block(half)
        first = grid.block_at == 0
        quarters = (jnp.where(first, half, other), jnp.where(first, other, half))
        inner_grad, outer_grad = (
            jnp.concatenate(
                [
                    one[:, (2 * core + which) * span : (2 * core + which + 1) * span]
                    for one in quarters
                    for core in range(2)
                ],
                axis=1,
            )
            for which in range(2)
        )
        return tuple(tensor.astype(F32) for tensor in (attn_grad, proj_grad, inner_grad, outer_grad))

    def waits(*names):
        return [pending[name] for name in names if name in pending]

    for layer_index in reversed(range(layer_count)):
        (
            stream_low, all_content, queries, keys, values, out, out_low, weights,
            result, middle, middle_low, active, slope, inverse_one, inverse_two,
        ) = kept[layer_index]
        qkv = attn_full[layer_index]
        partial = None
        for part in (None,) if layer_index == layer_count - 1 else (1, 0):
            grad = jnp.concatenate(grad_stream, axis=0) if part is None else grad_stream[part]
            partial = layer_tail_back_call(
                grad, result, inverse_two, middle, inverse_one, slope, (others, layer_index),
                all_pieces[layer_index], span, norm_gains[layer_index], norm_shifts[layer_index],
                part, partial, *waits("sum"),
            )
        two_low, inner_low, grad_one, branch_low, grad_out, norm_terms[layer_index] = partial
        grad_out = grad_out.reshape(2, rows, width)
        back = (queries, keys, values, grad_out, out, weights, score_sum)
        if paired:
            def steps(name, quarter, come=None):
                return [
                    (middle_low, inner_low, span, quarter, name, 0, come),
                    (two_low, active, span, quarter, name, 1, come),
                ]

            sent = products_call(
                "products_sent", side,
                steps("far", 3) + steps("beside", 1) + [(out_low, branch_low, third, "other", "proj", 0, None)],
                {"far": (width, 2 * span, span), "beside": (width, 2 * span, span), "proj": (width, third, third)},
                (),
            )
            come = {name: grid.from_core(tensor) for name, tensor in sent.items()}
            near = products_call(
                "products_near", side, steps("near", 2, come["far"]), {"near": (width, 2 * span, span)}
            )["near"]
            arrived = grid.from_block(near)
            held = products_call(
                "products_held", side,
                steps("mine", 0, come["beside"]) + [(out_low, branch_low, third, "side", "proj", 0, come["proj"])],
                {"mine": (width, 2 * span, span), "proj": (width, third, third)},
                [near],
            )
            partial = attend_back_call((0, pairs // 2), *back, None, *held.values())
            if "low_begun" in pending:
                pending["low"] = grid.scatter_end(pending["low_begun"], partial[0])
                pending["high_begun"] = grid.high_begin(pending["low"])
            grad_q, grad_k, grad_v, score_sum = attend_back_call(
                (pairs // 2, pairs - pairs // 2), *back, partial, *waits("low")
            )
            grad_q = grad_q.reshape(2 * rows, width)
            ffn_sum = (held["mine"].astype(F32) + arrived.astype(F32)).astype(LOW)
            if layer_index == 0:
                ffn_sum = jnp.concatenate([ffn_sum, held["proj"]], axis=1)
                ffn_begun = grid.low_begin(ffn_sum)
            if layer_index > 0:
                grad_all = keys_back(grad_k, grad_v, qkv)
                passed = dot_tn(other_spread, grad_all).astype(LOW)
            attn = products_call(
                "products_attn", side,
                [
                    (lhs, rhs, third, block, out_name, index, None)
                    for block, out_name in (("other", "sent"), ("side", "mine"))
                    for index, (lhs, rhs) in enumerate(
                        ((stream_low, grad_q), (all_content, grad_k), (all_content, grad_v))
                    )
                ],
                {"sent": (width, 3 * third, third), "mine": (width, 3 * third, third)},
                [passed, ffn_sum] if layer_index > 0 else [ffn_sum],
            )
            attn_sum = (attn["mine"].astype(F32) + grid.from_core(attn["sent"]).astype(F32)).astype(LOW)
            if layer_index == 0:
                grad_q, grad_k, grad_v = (hold(tensor, attn["sent"]) for tensor in (grad_q, grad_k, grad_v))
                grad_all = keys_back(grad_k, grad_v, qkv)
                passed = dot_tn(other_spread, grad_all).astype(LOW)
            if "high_begun" in pending:
                high = grid.scatter_end(pending["high_begun"], attn["sent"])
                matrix_rows[layer_index + 1] = finish_rows(high)
            if layer_index > 0:
                total = jnp.concatenate([ffn_sum, held["proj"], attn_sum], axis=1)
                pending = {"attn_sent": attn["sent"], "sum": total, "low_begun": grid.low_begin(total)}
            else:
                attn_begun = grid.low_begin(attn_sum)
                ffn_low = grid.scatter_end(ffn_begun, attn["sent"])
                ffn_begun = grid.high_begin(ffn_low)
                pending = {"attn_sum": attn_sum, "ffn_low": ffn_low}
        else:
            grad_q, grad_k, grad_v, score_sum = attend_back_call((0, pairs), *back, None)
            grad_q = grad_q.reshape(2 * rows, width)
            terms = [
                jnp.concatenate(
                    [dot_tn(stream_low, grad_q), dot_tn(all_content, grad_k), dot_tn(all_content, grad_v)], axis=1
                ),
                dot_tn(out_low, branch_low),
                dot_tn(middle_low, inner_low),
                dot_tn(two_low, active),
            ]
            matrix_rows[layer_index] = tuple(grid.scatter(term.astype(LOW)) for term in terms)
        query_side = grad_one + dot_nt(grad_q, qkv[:, :width])
        if layer_index == 0:
            table_grad = table_call([score_sum], place_column, bucket_count, *waits("attn_sum", "ffn_low"))
        if paired:
            come = grid.from_block(passed)
            if layer_index == 0:
                come = hold(come, table_grad)
            grad_keys_in = dot_tn(own_spread, grad_all) + come.astype(F32)
        else:
            grad_split = dot_tn(spread, keys_back(grad_k, grad_v, qkv)).astype(LOW)
            grad_keys_in = lax.psum_scatter(grad_split, "blk", scatter_dimension=0, tiled=True).astype(F32)
        grad_stream = [query_side[:rows] + grad_keys_in, query_side[rows:]]
    if paired:
        attn_begun = grid.high_begin(grid.scatter_end(attn_begun, table_grad))
        high = jnp.concatenate([grid.scatter_end(ffn_begun, table_grad), grid.scatter_end(attn_begun)], axis=1)
        matrix_rows[0] = finish_rows(high)
    table_lines = jnp.pad(table_grad.T, ((0, 0), (0, width - bucket_count)))
    sums = grid.sum_all(jnp.concatenate([*[terms[:4] for terms in norm_terms], table_lines], axis=0))
    norm_sum = sums[: 4 * layer_count].reshape(layer_count, 2, 2, width)
    table_total = sums[4 * layer_count :, :bucket_count].T
    matrix_grads = tuple(jnp.stack(layers, axis=0) for layers in zip(*matrix_rows))
    return (
        content_out[None],
        query_out[None],
        unsort_wide(grad_stream[0])[None],
        unsort_wide(grad_stream[1])[None],
        *matrix_grads,
        norm_sum[:, 0],
        norm_sum[:, 1],
        table_total,
    )


def solution(mesh):
    tokens = P("dp", "blk", None)
    matrix = P(None, "dp", None)
    whole = P()
    sequence = P("dp", None)
    return jax.shard_map(
        functools.partial(shards, Grid(mesh)),
        mesh=mesh,
        in_specs=(tokens,) * 4 + (matrix,) * 4 + (whole,) * 3 + (sequence,) * 3,
        out_specs=(tokens,) * 4 + (matrix,) * 4 + (whole,) * 3,
        check_vma=False,
    )
```

time: 2210 us -> 788 us (0.36)
  matrix products: 999 us -> 65.4 us
  local copies, waits for them, and re-layouts: 533 us -> 51 us
  Pallas kernels: 0 us -> 387 us
  waiting for transfers between devices: 362 us -> 148 us
  other arithmetic: 238 us -> 53.1 us
  starting transfers between devices: 0.68 us -> 62.2 us
  blocking collectives: 40.8 us -> 0 us
    dot_general x206 -> x30, matrix products: 999 us -> 65.4 us  [the longest x14 28.3 us: dot_nn(): return jnp.dot(left_side, right_side, preferred_element_type=F32)]
    pallas_call x0 -> x38, Pallas kernels: none -> 387 us  [the longest x4 79.8 us: attend_back_call(): pl.pallas_call(functools.partial(attend_back_kernel, earlier is not None)...]
    reduce_scatter x4 -> x0, waiting for transfers between devices: 272 us -> none  [the longest x2 234 us: shards(): lax.psum_scatter(jnp.concatenate([qkv_term, proj_term, inner_term, outer_...]
    eq x64 -> x0, local copies, waits for them, and re-layouts: 230 us -> none  [the longest x16 198 us: block_scores(): buckets[None] == bucket_ids[:, None, None, None]]
    add x48 -> x0, local copies, waits for them, and re-layouts: 191 us -> none  [block_scores(): raw_scores * 0.125 + bias[:, :, None]]
    ppermute x0 -> x53, waiting for transfers between devices: none -> 148 us  [the longest x13 78.6 us: from_block(): return lax.ppermute(tensor, 'blk', [(0, 1), (1, 0)])]
    reduce_sum x33 -> x6, other arithmetic: 104 us -> 4.01 us  [the longest x1 1.7 us: table_call(): jnp.sum(grouped * jnp.eye(8, dtype=F32)[None, :, None, :], axis=(1, 3))]
    all_gather x12 -> x2, waiting for transfers between devices: 77 us -> 0.01 us  [gather(): return lax.all_gather(shard, 'dp', axis=0, tiled=True)]
  transfers between devices with their start and end apart: 17 -> 55, of which waited for: 7 -> 20; matrix products, arithmetic and copies ran while one was open for 37% -> 17% of each run, Pallas kernels for 0% -> 32%
where the time goes in v1:
time: 788 us; the launch traced here: 783 us
  Pallas kernels  387 us (49%)
  waiting for transfers between devices  148 us (19%)
  matrix products  65.4 us (8%)
  starting transfers between devices  62.2 us (8%)
  other arithmetic  53.1 us (7%)
  local copies, waits for them, and re-layouts  51 us (6%)
  between operations  15.8 us (2%)
    pallas_call x4, Pallas kernels, attend_back_call(): pl.pallas_call(functools.partial(attend_back_kernel, earlier is not None)...  79.8 us
    pallas_call x8, Pallas kernels, products_call(): pl.pallas_call(functools.partial(product_kernel, plan), grid_spec=pltpu.P...  79.5 us
    ppermute x13, waiting for transfers between devices, from_block(): return lax.ppermute(tensor, 'blk', [(0, 1), (1, 0)])  78.6 us
    pallas_call x2, Pallas kernels, attend_call(): pl.pallas_call(attend_kernel, grid=(pairs, rows // tile), in_specs=[per_r...  74.4 us
    pallas_call x3, Pallas kernels, layer_tail_back_call(): pl.pallas_call(functools.partial(layer_tail_back_kernel, len(pieces), pla...  51 us
    pallas_call x2, Pallas kernels, layer_tail_call(): pl.pallas_call(functools.partial(layer_tail_kernel, len(pieces), plan, sp...  45.3 us
    ppermute x15, waiting for transfers between devices, from_high(): lax.ppermute(tensor, 'dp', [(i, (i + 2 * self.low * step) % self.total) f...  33.2 us
    dot_general x14, matrix products, dot_nn(): return jnp.dot(left_side, right_side, preferred_element_type=F32)  28.3 us
  transfers between devices with their start and end apart: 55, of which 20 were waited for; matrix products, arithmetic and copies ran while one was open for 17% of the time, Pallas kernels for 32%

profile of v1, /device:TPU:0, one launch (start us, length us, event | category | flops | bytes accessed | tf_op | source)
XLA Modules:
  0.0 782.5 jit_solution(12201505941704848001)
XLA Ops:
  36.9 22.1 %bias_rows.1.refs_4_.bias_ref = f32[12,512,1024]{2,1,0:T(8,128)} custom-call(f32[12,128]{1,0:T(8,128)} %concatenate.195.table_ref, s32[512,1]{1,0:T(8,128)} %copy.81.place_ref.refs_1_, s32[512,1]{1,0:T(8,128)} %copy.82.doc_ref, s32[512,1]{1,0:T(8,128)} %copy.83.rank_ref, s32[1,1024]{1,0:T(1,128)} %bitcast.314, s32[1,1024]{1,0:T(1,128)} %get-tuple-element.176.key_rank_ref, ...), custom_call_target="tpu_custom_call" | custom-call | bytes 75497472 | tf_op jit(solution)/shard_map/bias_rows/pallas_call | solution.py:62
  59.0 14.2 %collective-permute-done.3.refs_2_ = bf16[96,1536]{1,0:T(8,128)(2,1)S(1)} collective-permute-done((bf16[96,1536]{1,0:T(8,128)(2,1)}, bf16[96,1536]{1,0:T(8,128)(2,1)S(1)}, u32[]{:S(2)}, u32[]{:S(2)}) %collective-permute-start.3) | collective-permute-done | bytes 294944 | tf_op jit(solution)/shard_map/ppermute | solution.py:615
  91.0 17.2 %collective-permute-done.5.refs_1_ = bf16[4,96,1536]{2,1,0:T(8,128)(2,1)S(1)} collective-permute-done((bf16[4,96,1536]{2,1,0:T(8,128)(2,1)}, bf16[4,96,1536]{2,1,0:T(8,128)(2,1)S(1)}, u32[]{:S(2)}, u32[]{:S(2)}) %collective-permute-start.5) | collective-permute-done | bytes 1179680 | tf_op jit(solution)/shard_map/ppermute | solution.py:612
  123.0 37.2 %attend.2 = (f32[2,512,768]{2,1,0:T(8,128)}, bf16[2,512,768]{2,1,0:T(8,128)(2,1)}, bf16[12,2,512,1024]{3,2,1,0:T(8,128)(2,1)}) custom-call(bf16[2,512,768]{2,1,0:T(8,128)(2,1)} %bitcast.264, bf16[1024,768]{1,0:T(8,128)(2,1)} %convolution_convert_fusion.4.refs_3_.k_ref.refs_1_, bf16[1024,768]{1,0:T(8,128)(2,1)} %convolution_convert_fusion.3.refs_4_.v_ref.refs_2_, ...), custom_call_target="tpu_custom_call" | custom-call | flops 6442450944 | bytes 50331648 | tf_op jit(solution)/shard_map/attend/pallas_call | solution.py:115
  169.4 22.6 %layer_tail.2 = (f32[1024,768]{1,0:T(8,128)}, bf16[1024,768]{1,0:T(8,128)(2,1)}, f32[1024,768]{1,0:T(8,128)}, bf16[1024,768]{1,0:T(8,128)(2,1)}, bf16[1024,3072]...) custom-call(f32[1024,768]{1,0:T(8,128)} %get-tuple-element.182.refs_0_, ...), custom_call_target="tpu_custom_call" | custom-call | flops 10871635968 | bytes 31457280 | tf_op jit(solution)/shard_map/layer_tail/pallas_call | solution.py:342
  200.2 12.7 %collective-permute-done.13 = bf16[512,768]{1,0:T(8,128)(2,1)S(1)} collective-permute-done((bf16[512,768]{1,0:T(8,128)(2,1)S(1)}, bf16[512,768]{1,0:T(8,128)(2,1)S(1)}, u32[]{:S(2)}, u32[]{:S(2)}) %collective-permute-start.13) | collective-permute-done | bytes 786464 | tf_op jit(solution)/shard_map/ppermute | solution.py:607
  227.3 37.2 %attend.3 = (f32[2,512,768]{2,1,0:T(8,128)}, bf16[2,512,768]{2,1,0:T(8,128)(2,1)}, bf16[12,2,512,1024]{3,2,1,0:T(8,128)(2,1)}) custom-call(bf16[2,512,768]{2,1,0:T(8,128)(2,1)} %bitcast.260, bf16[1024,768]{1,0:T(8,128)(2,1)} %convolution_convert_fusion.1.refs_3_.k_ref.refs_1_, bf16[1024,768]{1,0:T(8,128)(2,1)} %convolution_convert_fusion.refs_4_.v_ref.refs_2_, ...), custom_call_target="tpu_custom_call" | custom-call | flops 6442450944 | bytes 50331648 | tf_op jit(solution)/shard_map/attend/pallas_call | solution.py:115
  264.5 14.5 %collective-permute-done.16.refs_0_ = bf16[768,1536]{1,0:T(8,128)(2,1)S(1)} collective-permute-done((bf16[768,1536]{1,0:T(8,128)(2,1)}, bf16[768,1536]{1,0:T(8,128)(2,1)S(1)}, u32[]{:S(2)}, u32[]{:S(2)}) %collective-permute-start.16) | collective-permute-done | bytes 2359328 | tf_op jit(solution)/shard_map/ppermute | solution.py:607
  286.6 22.7 %layer_tail.3 = (f32[1024,768]{1,0:T(8,128)}, bf16[1024,768]{1,0:T(8,128)(2,1)}, f32[1024,768]{1,0:T(8,128)}, bf16[1024,768]{1,0:T(8,128)(2,1)}, bf16[1024,3072]...) custom-call(f32[1024,768]{1,0:T(8,128)} %get-tuple-element.82.refs_0_.refs_1_, ...), custom_call_target="tpu_custom_call" | custom-call | flops 10871635968 | bytes 31457280 | tf_op jit(solution)/shard_map/layer_tail/pallas_call | solution.py:342
  310.0 22.0 %layer_tail_back.3 = (bf16[1024,768]{1,0:T(8,128)(2,1)}, bf16[1024,3072]{1,0:T(8,128)(2,1)}, f32[1024,768]{1,0:T(8,128)}, bf16[1024,768]{1,0:T(8,128)(2,1)}, bf1...) custom-call(f32[1024,768]{1,0:T(8,128)} %maximum_convert_fusion.refs_0_, f32[1024,768]{1,0:T(8,128)} %get-tuple-element.86.refs_1_, ...), custom_call_target="tpu_custom_call" | custom-call | flops 10871635968 | bytes 37748736 | tf_op jit(solution)/shard_map/layer_tail_back/pallas_call | solution.py:421
  331.9 12.7 %products_sent.2 = (bf16[768,1536]{1,0:T(8,128)(2,1)}, bf16[768,1536]{1,0:T(8,128)(2,1)}, bf16[768,384]{1,0:T(8,128)(2,1)}) custom-call(s32[1]{0:T(128)} %bitcast.16.side_ref, bf16[1024,768]{1,0:T(8,128)(2,1)} %get-tuple-element.95.refs_0_, bf16[1024,3072]{1,0:T(8,128)(2,1)} %get-tuple-element.96.refs_1_, ...), custom_call_target="tpu_custom_call" | custom-call | flops 5435817984 | bytes 18119392 | tf_op jit(solution)/shard_map/products_sent/pallas_call | solution.py:512
  350.8 7.1 products_near.2.refs_8_
  360.7 9.2 %products_held.2 = (bf16[768,1536]{1,0:T(8,128)(2,1)}, bf16[768,384]{1,0:T(8,128)(2,1)}) custom-call(s32[1]{0:T(128)} %bitcast.16.side_ref, bf16[1024,768]{1,0:T(8,128)(2,1)} %get-tuple-element.95.refs_0_, bf16[1024,3072]{1,0:T(8,128)(2,1)} %get-tuple-element.96.refs_1_, bf16[768,1536]{1,0:T(8,128)(2,1)} %copy-done.28, ...), custom_call_target="tpu_custom_call" | custom-call | flops 3019898880 | bytes 10066329 | tf_op jit(solution)/shard_map/products_held/pallas_call | solution.py:512
  369.9 18.5 %attend_back.4 = (bf16[2,512,768]{2,1,0:T(8,128)(2,1)}, bf16[1024,768]{1,0:T(8,128)(2,1)}, bf16[1024,768]{1,0:T(8,128)(2,1)}, f32[12,512,1024]{2,1,0:T(8,128)}) custom-call(bf16[2,512,768]{2,1,0:T(8,128)(2,1)} %bitcast.261, bf16[1024,768]{1,0:T(8,128)(2,1)} %convolution_convert_fusion.1.refs_3_.k_ref.refs_1_, ...), custom_call_target="tpu_custom_call" | custom-call | flops 6442450944 | bytes 37748736 | tf_op jit(solution)/shard_map/attend_back/pallas_call | solution.py:194
  388.5 18.8 %attend_back.5 = (bf16[2,512,768]{2,1,0:T(8,128)(2,1)}, bf16[1024,768]{1,0:T(8,128)(2,1)}, bf16[1024,768]{1,0:T(8,128)(2,1)}, f32[12,512,1024]{2,1,0:T(8,128)}) custom-call(bf16[2,512,768]{2,1,0:T(8,128)(2,1)} %bitcast.262, ...), custom_call_target="tpu_custom_call", output_to_operand_aliasing={{0}: (6, {}), {1}: (7, {}), {2}: (8, {}), {3}: (9, {})} | custom-call | flops 6442450944 | bytes 37748736 | tf_op jit(solution)/shard_map/attend_back/pallas_call | solution.py:194
  417.8 10.7 %products_attn.2 = (bf16[768,1152]{1,0:T(8,128)(2,1)}, bf16[768,1152]{1,0:T(8,128)(2,1)}) custom-call(s32[1]{0:T(128)} %bitcast.16.side_ref, bf16[1024,768]{1,0:T(8,128)(2,1)} %get-tuple-element.83.refs_0_, bf16[1024,768]{1,0:T(8,128)(2,1)} %bitcast.300, bf16[1024,768]{1,0:T(8,128)(2,1)} %copy-done.79, bf16[1024,768]{1,0:T(8,128)(2,1)} %get-tuple-element.110.refs_3_, ...), custom_call_target="tpu_custom_call" | custom-call | flops 3623878656 | bytes 12079595 | tf_op jit(solution)/shard_map/products_attn/pallas_call | solution.py:512
  433.5 14.8 %collective-permute-done.21 = bf16[512,768]{1,0:T(8,128)(2,1)S(1)} collective-permute-done((bf16[512,768]{1,0:T(8,128)(2,1)S(1)}, bf16[512,768]{1,0:T(8,128)(2,1)S(1)}, u32[]{:S(2)}, u32[]{:S(2)}) %collective-permute-start.21) | collective-permute-done | bytes 786464 | tf_op jit(solution)/shard_map/ppermute | solution.py:607
  455.0 14.7 %layer_tail_back.4 = (bf16[1024,768]{1,0:T(8,128)(2,1)}, bf16[1024,3072]{1,0:T(8,128)(2,1)}, f32[1024,768]{1,0:T(8,128)}, bf16[1024,768]{1,0:T(8,128)(2,1)}, bf1...) custom-call(f32[512,768]{1,0:T(8,128)} %slice.312.refs_0_, f32[1024,768]{1,0:T(8,128)} %get-tuple-element.82.refs_0_.refs_1_, ...), custom_call_target="tpu_custom_call" | custom-call | flops 5435817984 | bytes 37748736 | tf_op jit(solution)/shard_map/layer_tail_back/pallas_call | solution.py:421
  469.7 14.4 %layer_tail_back.5 = (bf16[1024,768]{1,0:T(8,128)(2,1)}, bf16[1024,3072]{1,0:T(8,128)(2,1)}, f32[1024,768]{1,0:T(8,128)}, bf16[1024,768]{1,0:T(8,128)(2,1)}, bf1...) custom-call(f32[512,768]{1,0:T(8,128)} %slice_add_fusion.1.refs_0_, ...), custom_call_target="tpu_custom_call", output_to_operand_aliasing={{0}: (14, {}), {1}: (15, {}), {2}: (16, {}), {3}: (17, {}),... | custom-call | flops 5435817984 | bytes 37748736 | tf_op jit(solution)/shard_map/layer_tail_back/pallas_call | solution.py:421
  484.1 12.6 %products_sent.3 = (bf16[768,1536]{1,0:T(8,128)(2,1)}, bf16[768,1536]{1,0:T(8,128)(2,1)}, bf16[768,384]{1,0:T(8,128)(2,1)}) custom-call(s32[1]{0:T(128)} %bitcast.16.side_ref, bf16[1024,768]{1,0:T(8,128)(2,1)} %get-tuple-element.129.refs_0_, bf16[1024,3072]{1,0:T(8,128)(2,1)} %get-tuple-element.130.refs_1_, ...), custom_call_target="tpu_custom_call" | custom-call | flops 5435817984 | bytes 18119392 | tf_op jit(solution)/shard_map/products_sent/pallas_call | solution.py:512
  507.4 7.2 products_near.3.refs_8_
  516.8 9.2 %products_held.3 = (bf16[768,1536]{1,0:T(8,128)(2,1)}, bf16[768,384]{1,0:T(8,128)(2,1)}) custom-call(s32[1]{0:T(128)} %bitcast.16.side_ref, bf16[1024,768]{1,0:T(8,128)(2,1)} %get-tuple-element.129.refs_0_, bf16[1024,3072]{1,0:T(8,128)(2,1)} %get-tuple-element.130.refs_1_, bf16[768,1536]{1,0:T(8,128)(2,1)} %collective-permute-done.24.refs_2_, ...), custom_call_target="tpu_custom_call" | custom-call | flops 3019898880 | bytes 10066329 | tf_op jit(solution)/shard_map/products_held/pallas_call | solution.py:512
  526.1 21.1 %attend_back.6 = (bf16[2,512,768]{2,1,0:T(8,128)(2,1)}, bf16[1024,768]{1,0:T(8,128)(2,1)}, bf16[1024,768]{1,0:T(8,128)(2,1)}, f32[12,512,1024]{2,1,0:T(8,128)}) custom-call(bf16[2,512,768]{2,1,0:T(8,128)(2,1)} %bitcast.265, bf16[1024,768]{1,0:T(8,128)(2,1)} %convolution_convert_fusion.4.refs_3_.k_ref.refs_1_, ...), custom_call_target="tpu_custom_call" | custom-call | flops 6442450944 | bytes 37748736 | tf_op jit(solution)/shard_map/attend_back/pallas_call | solution.py:194
  547.2 6.8 collective-permute-done.27.refs_0_
  565.7 21.4 %attend_back.7 = (bf16[2,512,768]{2,1,0:T(8,128)(2,1)}, bf16[1024,768]{1,0:T(8,128)(2,1)}, bf16[1024,768]{1,0:T(8,128)(2,1)}, f32[12,512,1024]{2,1,0:T(8,128)}) custom-call(bf16[2,512,768]{2,1,0:T(8,128)(2,1)} %bitcast.266, ...), custom_call_target="tpu_custom_call", output_to_operand_aliasing={{0}: (7, {}), {1}: (8, {}), {2}: (9, {}), {3}: (10, {})} | custom-call | flops 6442450944 | bytes 37748736 | tf_op jit(solution)/shard_map/attend_back/pallas_call | solution.py:194
  591.3 10.7 %products_attn.3 = (bf16[768,1152]{1,0:T(8,128)(2,1)}, bf16[768,1152]{1,0:T(8,128)(2,1)}) custom-call(s32[1]{0:T(128)} %bitcast.16.side_ref, bf16[1024,768]{1,0:T(8,128)(2,1)} %get-tuple-element.181.refs_1_.refs_0_, bf16[1024,768]{1,0:T(8,128)(2,1)} %bitcast.276, bf16[1024,768]{1,0:T(8,128)(2,1)} %add_convert_fusion.7.refs_2_, ...), custom_call_target="tpu_custom_call" | custom-call | flops 3623878656 | bytes 12079595 | tf_op jit(solution)/shard_map/products_attn/pallas_call | solution.py:512
  638.0 20.4 %collective-permute-done.47 = bf16[48,3072]{1,0:T(8,128)(2,1)S(1)} collective-permute-done((bf16[48,3072]{1,0:T(8,128)(2,1)S(1)}, bf16[48,3072]{1,0:T(8,128)(2,1)S(1)}, u32[]{:S(2)}, u32[]{:S(2)}) %collective-permute-start.47) | collective-permute-done | bytes 294944 | tf_op jit(solution)/shard_map/ppermute | solution.py:607
  666.6 19.9 %table_sums.1 = f32[256,96]{1,0:T(8,128)} custom-call(f32[12,512,1024]{2,1,0:T(8,128)} %get-tuple-element.147.refs_0_, s32[512,1]{1,0:T(8,128)} %copy.81.place_ref.refs_1_, bf16[768,1152]{1,0:T(8,128)(2,1)} %add_convert_fusion.2.refs_2_, bf16[4,96,1920]{2,1,0:T(8,128)(2,1)} %fusion.1.refs_3_), custom_call_target="tpu_custom_call" | custom-call | flops 3221225472 | bytes 25165824 | tf_op jit(solution)/shard_map/table_sums/pallas_call | solution.py:253
  712.1 13.2 %collective-permute-start.51 = (f32[20,768]{1,0:T(8,128)}, f32[20,768]{1,0:T(8,128)}, u32[]{:S(2)}, u32[]{:S(2)}) collective-permute-start(f32[20,768]{1,0:T(8,128)} %add.329), channel_id=1, source_target_pairs={{0,4},{1,5},{2,6},{3,7},{4,0},{5,1},{6,2},{7,3},{8,12},{9,13},{10,... | collective-permute-start | bytes 184328 | tf_op jit(solution)/shard_map/ppermute | solution.py:683
  731.7 10.4 %collective-permute-done.33 = bf16[96,1920]{1,0:T(8,128)(2,1)} collective-permute-done((bf16[96,1920]{1,0:T(8,128)(2,1)}, bf16[96,1920]{1,0:T(8,128)(2,1)}, u32[]{:S(2)}, u32[]{:S(2)}) %collective-permute-start.33) | collective-permute-done | bytes 368672 | tf_op jit(solution)/shard_map/ppermute | solution.py:615
  744.9 7.4 collective-permute-done.37
  766.7 5.9 collective-permute-done.46
  (437 shorter events, 257.1 us)
Async XLA Ops:
  7.2 74.6 %all-gather.6.cloned.1.call-start = ((), (), s32[]{:S(2)}) async-start(), calls=%async_computation.1 | async-start | bytes 3760128 | tf_op jit(solution)/shard_map/all_gather | solution.py:618
  9.1 156.7 %all-gather.4.cloned.1.call-start = ((), (), s32[]{:S(2)}) async-start(), calls=%async_computation | async-start | bytes 6266880 | tf_op jit(solution)/shard_map/all_gather | solution.py:618
  14.0 64.4 %collective-permute-start = (bf16[512,768]{1,0:T(8,128)(2,1)S(1)}, bf16[512,768]{1,0:T(8,128)(2,1)}, u32[]{:S(2)}, u32[]{:S(2)}) collective-permute-start(bf16[512,768]{1,0:T(8,128)(2,1)S(1)} %convolution_convert_fusion.11), channel_id=1, source_target_pairs={{0,16},{16,0},{1,17},{17,1},{2,18},{18,2},{3,19},{19,3},{4,20},{20... | collective-permute-start | bytes 2359304 | tf_op jit(solution)/shard_map/ppermute | solution.py:607
  30.7 28.3 %collective-permute-start.4 = (bf16[96,1536]{1,0:T(8,128)(2,1)}, bf16[96,1536]{1,0:T(8,128)(2,1)S(1)}, u32[]{:S(2)}, u32[]{:S(2)}) collective-permute-start(bf16[96,1536]{1,0:T(8,128)(2,1)} %bitcast.295), channel_id=1, source_target_pairs={{0,12},{1,13},{2,14},{3,15},{4,0},{5,1},{6,2},{7,3},{8,4},{9,5},{1... | collective-permute-start | bytes 884744 | tf_op jit(solution)/shard_map/ppermute | solution.py:615
  34.3 38.9 %collective-permute-start.3 = (bf16[96,1536]{1,0:T(8,128)(2,1)}, bf16[96,1536]{1,0:T(8,128)(2,1)S(1)}, u32[]{:S(2)}, u32[]{:S(2)}) collective-permute-start(bf16[96,1536]{1,0:T(8,128)(2,1)} %bitcast.296), channel_id=1, source_target_pairs={{0,8},{1,9},{2,10},{3,11},{4,12},{5,13},{6,14},{7,15},{8,0},{9,1},... | collective-permute-start | bytes 884744 | tf_op jit(solution)/shard_map/ppermute | solution.py:615
  34.3 38.9 %collective-permute-start.2 = (bf16[96,1536]{1,0:T(8,128)(2,1)}, bf16[96,1536]{1,0:T(8,128)(2,1)S(1)}, u32[]{:S(2)}, u32[]{:S(2)}) collective-permute-start(bf16[96,1536]{1,0:T(8,128)(2,1)} %bitcast.297), channel_id=1, source_target_pairs={{0,4},{1,5},{2,6},{3,7},{4,8},{5,9},{6,10},{7,11},{8,12},{9,13},{1... | collective-permute-start | bytes 884744 | tf_op jit(solution)/shard_map/ppermute | solution.py:615
  77.0 31.1 %collective-permute-start.5 = (bf16[4,96,1536]{2,1,0:T(8,128)(2,1)}, bf16[4,96,1536]{2,1,0:T(8,128)(2,1)S(1)}, u32[]{:S(2)}, u32[]{:S(2)}) collective-permute-start(bf16[4,96,1536]{2,1,0:T(8,128)(2,1)} %line_rows.2.refs_0_.refs_2_), channel_id=1, source_target_pairs={{0,2},{1,3},{2,0},{3,1},{4,6},{5,7},{6,4},{7,5},{8,10},{9,11},{10,... | collective-permute-start | bytes 3538952 | tf_op jit(solution)/shard_map/ppermute | solution.py:612
  112.5 51.9 %collective-permute-start.8 = (bf16[768,1536]{1,0:T(8,128)(2,1)}, bf16[768,1536]{1,0:T(8,128)(2,1)}, u32[]{:S(2)}, u32[]{:S(2)}) collective-permute-start(bf16[768,1536]{1,0:T(8,128)(2,1)} %bitcast.253), channel_id=1, source_target_pairs={{0,16},{16,0},{1,17},{17,1},{2,18},{18,2},{3,19},{19,3},{4,20},{20... | collective-permute-start | bytes 7077896 | tf_op jit(solution)/shard_map/ppermute | solution.py:607
  118.4 41.8 %collective-permute-start.11 = (bf16[96,1536]{1,0:T(8,128)(2,1)}, bf16[96,1536]{1,0:T(8,128)(2,1)S(1)}, u32[]{:S(2)}, u32[]{:S(2)}) collective-permute-start(bf16[96,1536]{1,0:T(8,128)(2,1)} %bitcast.290), channel_id=1, source_target_pairs={{0,12},{1,13},{2,14},{3,15},{4,0},{5,1},{6,2},{7,3},{8,4},{9,5},{1... | collective-permute-start | bytes 884744 | tf_op jit(solution)/shard_map/ppermute | solution.py:615
  118.4 42.9 %collective-permute-start.10 = (bf16[96,1536]{1,0:T(8,128)(2,1)}, bf16[96,1536]{1,0:T(8,128)(2,1)S(1)}, u32[]{:S(2)}, u32[]{:S(2)}) collective-permute-start(bf16[96,1536]{1,0:T(8,128)(2,1)} %bitcast.291), channel_id=1, source_target_pairs={{0,8},{1,9},{2,10},{3,11},{4,12},{5,13},{6,14},{7,15},{8,0},{9,1},... | collective-permute-start | bytes 884744 | tf_op jit(solution)/shard_map/ppermute | solution.py:615
  120.8 40.5 %collective-permute-start.9 = (bf16[96,1536]{1,0:T(8,128)(2,1)}, bf16[96,1536]{1,0:T(8,128)(2,1)S(1)}, u32[]{:S(2)}, u32[]{:S(2)}) collective-permute-start(bf16[96,1536]{1,0:T(8,128)(2,1)} %bitcast.292), channel_id=1, source_target_pairs={{0,4},{1,5},{2,6},{3,7},{4,8},{5,9},{6,10},{7,11},{8,12},{9,13},{1... | collective-permute-start | bytes 884744 | tf_op jit(solution)/shard_map/ppermute | solution.py:615
  123.0 42.8 %collective-permute-start.7 = (bf16[768,1536]{1,0:T(8,128)(2,1)S(1)}, bf16[768,1536]{1,0:T(8,128)(2,1)}, u32[]{:S(2)}, u32[]{:S(2)}) collective-permute-start(bf16[768,1536]{1,0:T(8,128)(2,1)S(1)} %bitcast.258), channel_id=1, source_target_pairs={{0,1},{1,0},{2,3},{3,2},{4,5},{5,4},{6,7},{7,6},{8,9},{9,8},{10,11... | collective-permute-start | bytes 7077896 | tf_op jit(solution)/shard_map/ppermute | solution.py:604
  194.8 27.7 %collective-permute-start.14 = (bf16[4,96,1536]{2,1,0:T(8,128)(2,1)S(1)}, bf16[4,96,1536]{2,1,0:T(8,128)(2,1)S(1)}, u32[]{:S(2)}, u32[]{:S(2)}) collective-permute-start(bf16[4,96,1536]{2,1,0:T(8,128)(2,1)S(1)} %copy-done.11), channel_id=1, source_target_pairs={{0,2},{1,3},{2,0},{3,1},{4,6},{5,7},{6,4},{7,5},{8,10},{9,11},{10,... | collective-permute-start | bytes 3538952 | tf_op jit(solution)/shard_map/ppermute | solution.py:612
  226.7 52.3 %collective-permute-start.16 = (bf16[768,1536]{1,0:T(8,128)(2,1)}, bf16[768,1536]{1,0:T(8,128)(2,1)S(1)}, u32[]{:S(2)}, u32[]{:S(2)}) collective-permute-start(bf16[768,1536]{1,0:T(8,128)(2,1)} %bitcast.280), channel_id=1, source_target_pairs={{0,16},{16,0},{1,17},{17,1},{2,18},{18,2},{3,19},{19,3},{4,20},{20... | collective-permute-start | bytes 7077896 | tf_op jit(solution)/shard_map/ppermute | solution.py:607
  227.3 57.5 %collective-permute-start.15 = (bf16[768,1536]{1,0:T(8,128)(2,1)}, bf16[768,1536]{1,0:T(8,128)(2,1)}, u32[]{:S(2)}, u32[]{:S(2)}) collective-permute-start(bf16[768,1536]{1,0:T(8,128)(2,1)} %bitcast.281), channel_id=1, source_target_pairs={{0,1},{1,0},{2,3},{3,2},{4,5},{5,4},{6,7},{7,6},{8,9},{9,8},{10,11... | collective-permute-start | bytes 7077896 | tf_op jit(solution)/shard_map/ppermute | solution.py:604
  357.9 55.9 %collective-permute-start.22 = (bf16[768,1536]{1,0:T(8,128)(2,1)}, bf16[768,1536]{1,0:T(8,128)(2,1)}, u32[]{:S(2)}, u32[]{:S(2)}) collective-permute-start(bf16[768,1536]{1,0:T(8,128)(2,1)} %products_near.2.refs_8_), channel_id=1, source_target_pairs={{0,16},{16,0},{1,17},{17,1},{2,18},{18,2},{3,19},{19,3},{4,20},{20... | collective-permute-start | bytes 7077896 | tf_op jit(solution)/shard_map/ppermute | solution.py:607
  428.4 22.4 %collective-permute-start.23 = (bf16[768,1152]{1,0:T(8,128)(2,1)}, bf16[768,1152]{1,0:T(8,128)(2,1)S(1)}, u32[]{:S(2)}, u32[]{:S(2)}) collective-permute-start(bf16[768,1152]{1,0:T(8,128)(2,1)} %get-tuple-element.117), channel_id=1, source_target_pairs={{0,1},{1,0},{2,3},{3,2},{4,5},{5,4},{6,7},{7,6},{8,9},{9,8},{10,11... | collective-permute-start | bytes 5308424 | tf_op jit(solution)/shard_map/ppermute | solution.py:604
  428.4 20.0 %collective-permute-start.21 = (bf16[512,768]{1,0:T(8,128)(2,1)S(1)}, bf16[512,768]{1,0:T(8,128)(2,1)S(1)}, u32[]{:S(2)}, u32[]{:S(2)}) collective-permute-start(bf16[512,768]{1,0:T(8,128)(2,1)S(1)} %copy-done.76), channel_id=1, source_target_pairs={{0,16},{16,0},{1,17},{17,1},{2,18},{18,2},{3,19},{19,3},{4,20},{20... | collective-permute-start | bytes 2359304 | tf_op jit(solution)/shard_map/ppermute | solution.py:607
  500.5 53.4 %collective-permute-start.27 = (bf16[4,96,3072]{2,1,0:T(8,128)(2,1)}, bf16[4,96,3072]{2,1,0:T(8,128)(2,1)S(1)}, u32[]{:S(2)}, u32[]{:S(2)}) collective-permute-start(bf16[4,96,3072]{2,1,0:T(8,128)(2,1)} %dynamic-slice_bitcast_fusion), channel_id=1, source_target_pairs={{0,2},{1,3},{2,0},{3,1},{4,6},{5,7},{6,4},{7,5},{8,10},{9,11},{10,... | collective-permute-start | bytes 7077896 | tf_op jit(solution)/shard_map/ppermute | solution.py:612
  514.5 72.6 %collective-permute-start.28 = (bf16[768,1536]{1,0:T(8,128)(2,1)}, bf16[768,1536]{1,0:T(8,128)(2,1)}, u32[]{:S(2)}, u32[]{:S(2)}) collective-permute-start(bf16[768,1536]{1,0:T(8,128)(2,1)} %products_near.3.refs_8_), channel_id=1, source_target_pairs={{0,16},{16,0},{1,17},{17,1},{2,18},{18,2},{3,19},{19,3},{4,20},{20... | collective-permute-start | bytes 7077896 | tf_op jit(solution)/shard_map/ppermute | solution.py:607
  560.7 52.1 %collective-permute-start.41 = (bf16[96,3072]{1,0:T(8,128)(2,1)}, bf16[96,3072]{1,0:T(8,128)(2,1)S(1)}, u32[]{:S(2)}, u32[]{:S(2)}) collective-permute-start(bf16[96,3072]{1,0:T(8,128)(2,1)} %get-tuple-element.178), channel_id=1, source_target_pairs={{0,4},{1,5},{2,6},{3,7},{4,8},{5,9},{6,10},{7,11},{8,12},{9,13},{1... | collective-permute-start | bytes 1769480 | tf_op jit(solution)/shard_map/ppermute | solution.py:615
  561.7 56.9 %collective-permute-start.43 = (bf16[96,3072]{1,0:T(8,128)(2,1)}, bf16[96,3072]{1,0:T(8,128)(2,1)}, u32[]{:S(2)}, u32[]{:S(2)}) collective-permute-start(bf16[96,3072]{1,0:T(8,128)(2,1)} %get-tuple-element.179), channel_id=1, source_target_pairs={{0,12},{1,13},{2,14},{3,15},{4,0},{5,1},{6,2},{7,3},{8,4},{9,5},{1... | collective-permute-start | bytes 1769480 | tf_op jit(solution)/shard_map/ppermute | solution.py:615
  564.5 54.1 %collective-permute-start.42 = (bf16[96,3072]{1,0:T(8,128)(2,1)}, bf16[96,3072]{1,0:T(8,128)(2,1)}, u32[]{:S(2)}, u32[]{:S(2)}) collective-permute-start(bf16[96,3072]{1,0:T(8,128)(2,1)} %get-tuple-element.180), channel_id=1, source_target_pairs={{0,8},{1,9},{2,10},{3,11},{4,12},{5,13},{6,14},{7,15},{8,0},{9,1},... | collective-permute-start | bytes 1769480 | tf_op jit(solution)/shard_map/ppermute | solution.py:615
  603.5 59.9 %collective-permute-start.30 = (bf16[768,1152]{1,0:T(8,128)(2,1)S(1)}, bf16[768,1152]{1,0:T(8,128)(2,1)}, u32[]{:S(2)}, u32[]{:S(2)}) collective-permute-start(bf16[768,1152]{1,0:T(8,128)(2,1)S(1)} %copy-done.2), channel_id=1, source_target_pairs={{0,1},{1,0},{2,3},{3,2},{4,5},{5,4},{6,7},{7,6},{8,9},{9,8},{10,11... | collective-permute-start | bytes 5308424 | tf_op jit(solution)/shard_map/ppermute | solution.py:604
  606.2 53.8 %collective-permute-start.31 = (bf16[4,96,1920]{2,1,0:T(8,128)(2,1)}, bf16[4,96,1920]{2,1,0:T(8,128)(2,1)}, u32[]{:S(2)}, u32[]{:S(2)}) collective-permute-start(bf16[4,96,1920]{2,1,0:T(8,128)(2,1)} %dynamic-slice_bitcast_fusion.1), channel_id=1, source_target_pairs={{0,2},{1,3},{2,0},{3,1},{4,6},{5,7},{6,4},{7,5},{8,10},{9,11},{10,... | collective-permute-start | bytes 4423688 | tf_op jit(solution)/shard_map/ppermute | solution.py:612
  632.0 70.5 %collective-permute-start.29 = (bf16[512,768]{1,0:T(8,128)(2,1)}, bf16[512,768]{1,0:T(8,128)(2,1)S(1)}, u32[]{:S(2)}, u32[]{:S(2)}) collective-permute-start(bf16[512,768]{1,0:T(8,128)(2,1)} %fusion.12), channel_id=1, source_target_pairs={{0,16},{16,0},{1,17},{17,1},{2,18},{18,2},{3,19},{19,3},{4,20},{20... | collective-permute-start | bytes 2359304 | tf_op jit(solution)/shard_map/ppermute | solution.py:607
  635.9 22.5 %collective-permute-start.47 = (bf16[48,3072]{1,0:T(8,128)(2,1)S(1)}, bf16[48,3072]{1,0:T(8,128)(2,1)S(1)}, u32[]{:S(2)}, u32[]{:S(2)}) collective-permute-start(bf16[48,3072]{1,0:T(8,128)(2,1)S(1)} %pad_maximum_fusion.6), channel_id=1, source_target_pairs={{0,16},{16,0},{1,17},{17,1},{2,18},{18,2},{3,19},{19,3},{4,20},{20... | collective-permute-start | bytes 884744 | tf_op jit(solution)/shard_map/ppermute | solution.py:607
  688.5 36.9 %collective-permute-start.35 = (bf16[4,96,1152]{2,1,0:T(8,128)(2,1)}, bf16[4,96,1152]{2,1,0:T(8,128)(2,1)S(1)}, u32[]{:S(2)}, u32[]{:S(2)}) collective-permute-start(bf16[4,96,1152]{2,1,0:T(8,128)(2,1)} %dynamic-slice_bitcast_fusion.2), channel_id=1, source_target_pairs={{0,2},{1,3},{2,0},{3,1},{4,6},{5,7},{6,4},{7,5},{8,10},{9,11},{10,... | collective-permute-start | bytes 2654216 | tf_op jit(solution)/shard_map/ppermute | solution.py:612
  699.1 32.6 %collective-permute-start.34 = (bf16[96,1920]{1,0:T(8,128)(2,1)}, bf16[96,1920]{1,0:T(8,128)(2,1)}, u32[]{:S(2)}, u32[]{:S(2)}) collective-permute-start(bf16[96,1920]{1,0:T(8,128)(2,1)} %get-tuple-element.184), channel_id=1, source_target_pairs={{0,12},{1,13},{2,14},{3,15},{4,0},{5,1},{6,2},{7,3},{8,4},{9,5},{1... | collective-permute-start | bytes 1105928 | tf_op jit(solution)/shard_map/ppermute | solution.py:615
  702.4 39.7 %collective-permute-start.33 = (bf16[96,1920]{1,0:T(8,128)(2,1)}, bf16[96,1920]{1,0:T(8,128)(2,1)}, u32[]{:S(2)}, u32[]{:S(2)}) collective-permute-start(bf16[96,1920]{1,0:T(8,128)(2,1)} %get-tuple-element.185), channel_id=1, source_target_pairs={{0,8},{1,9},{2,10},{3,11},{4,12},{5,13},{6,14},{7,15},{8,0},{9,1},... | collective-permute-start | bytes 1105928 | tf_op jit(solution)/shard_map/ppermute | solution.py:615
  712.1 31.6 %collective-permute-start.51 = (f32[20,768]{1,0:T(8,128)}, f32[20,768]{1,0:T(8,128)}, u32[]{:S(2)}, u32[]{:S(2)}) collective-permute-start(f32[20,768]{1,0:T(8,128)} %add.329), channel_id=1, source_target_pairs={{0,4},{1,5},{2,6},{3,7},{4,0},{5,1},{6,2},{7,3},{8,12},{9,13},{10,... | collective-permute-start | bytes 184328 | tf_op jit(solution)/shard_map/ppermute | solution.py:683
  731.7 20.6 %collective-permute-start.37 = (bf16[96,1152]{1,0:T(8,128)(2,1)S(1)}, bf16[96,1152]{1,0:T(8,128)(2,1)S(1)}, u32[]{:S(2)}, u32[]{:S(2)}) collective-permute-start(bf16[96,1152]{1,0:T(8,128)(2,1)S(1)} %get-tuple-element.190), channel_id=1, source_target_pairs={{0,8},{1,9},{2,10},{3,11},{4,12},{5,13},{6,14},{7,15},{8,0},{9,1},... | collective-permute-start | bytes 663560 | tf_op jit(solution)/shard_map/ppermute | solution.py:615
  (108 other events, 747.8 us)
Sparse Core Ops, SparseCore 0:
  10.9 65.3 all-gather.5
  79.1 78.8 all-gather.3

commit v2 on v1

--- a/solution.py
+++ b/solution.py
@@ -12,6 +12,8 @@
 F32 = jnp.float32
 LOW = jnp.bfloat16
 VMEM_LIMIT = 56 * 2**20
+ROW_TILE = 128
+PAIRS = 2
 
 
 def dot_nn(left_side, right_side):
@@ -33,36 +35,161 @@
     return jnp.where(relative > 0, 16, 0).astype(jnp.int32) + near_bucket
 
 
-def bias_kernel(table_ref, place_ref, doc_ref, rank_ref, key_doc_ref, key_rank_ref, *refs):
+def window_counts(length):
+    most = length // 128
+    return [count for count in (2, 3, 4, 5, 6) if count < most] + [most]
+
+
+def by_window(window_ref, tile, length, step):
+    def one(at, carry):
+        row = pl.multiple_of(at * tile, tile)
+        first = pl.multiple_of(window_ref[0, at] * 128, 128)
+        for count in window_counts(length):
+
+            @pl.when(window_ref[1, at] == count)
+            def _(count=count):
+                step(pl.ds(row, tile), pl.ds(first, count * 128), count * 128, first)
+
+        return carry
+
+    lax.fori_loop(0, window_ref.shape[1], one, 0)
+
+
+def setup_kernel(side_ref, lengths_ref, row_ref, column_ref, chosen_ref, *refs):
+    streams, refs = refs[:4], refs[4:]
+    outs = refs[-(11 + side_ref.shape[0]) :]
+    window_ref, key_doc_ref, key_rank_ref, place_ref, doc_ref, rank_ref, own_ref, sorter_ref, low_ref, grad_ref = outs[:10]
+    spread_refs = outs[10:-1]
+    rank_row = outs[-1]
+    length, rows = row_ref.shape[1], streams[0].shape[0]
+    for first in range(0, length, 128):
+        position = (first + lax.broadcasted_iota(jnp.int32, (length, 128), 1))
+        rank = lax.broadcasted_iota(jnp.int32, (length, 128), 0).astype(F32)
+        rank_row[:, first : first + 128] = jnp.sum(
+            jnp.where(column_ref[...] == position, rank, 0.0), axis=0, keepdims=True
+        )
+    ranks = rank_row[...]
+    position = lax.broadcasted_iota(jnp.int32, (1, length), 1)
+    doc = jnp.zeros((1, length), jnp.int32)
+    start = position == 0
+    bound = 0
+    for index in range(lengths_ref.shape[1] - 1):
+        bound = bound + lengths_ref[0, index]
+        doc = doc + (position >= bound).astype(jnp.int32)
+        start = start | (position == bound)
+    live = (chosen_ref[...] == 1) & jnp.logical_not(start)
+    key_doc_ref[...] = doc
+    key_rank_ref[...] = jnp.where(live, ranks, -1.0).astype(jnp.int32)
+    below = (
+        lax.broadcasted_iota(jnp.int32, (length, length), 0) <= lax.broadcasted_iota(jnp.int32, (length, length), 1)
+    )
+    below = jnp.where(below, 1.0, 0.0).astype(LOW)
+    slot = lax.broadcasted_iota(jnp.int32, (rows, length), 0).astype(F32)
+    for index, spread_ref in enumerate(spread_refs):
+        least = (side_ref[index] * rows).astype(F32)
+        owned = (ranks >= least) & (ranks < least + rows)
+        counted = jnp.broadcast_to(jnp.where(owned, 1.0, 0.0), (8, length)).astype(LOW)
+        order = jnp.where(owned, dot_nn(counted, below)[0:1] - 1.0, -1.0)
+        chosen = slot == order
+        spread_ref[...] = jnp.where(chosen, 1.0, 0.0).astype(LOW)
+        if index == 0:
+
+            def pick(row):
+                return jnp.sum(jnp.where(chosen, row, 0.0), axis=1, keepdims=True)
+
+            place = pick(position.astype(F32))
+            rank = pick(ranks)
+            place_ref[...] = place.astype(jnp.int32)
+            rank_ref[...] = rank.astype(jnp.int32)
+            doc_ref[...] = pick(doc.astype(F32)).astype(jnp.int32)
+            own_ref[...] = jnp.where(pick(jnp.where(live, 1.0, 0.0)) > 0.0, place, -1.0).astype(jnp.int32)
+            tile = rows // window_ref.shape[1]
+            for at in range(window_ref.shape[1]):
+                lines = place[at * tile : (at + 1) * tile]
+                least_place = jnp.min(lines).astype(jnp.int32)
+                most_place = jnp.max(lines).astype(jnp.int32)
+                first, last, bound = 0, length, 0
+                for doc_index in range(lengths_ref.shape[1] - 1):
+                    bound = bound + lengths_ref[0, doc_index]
+                    first = jnp.where(least_place >= bound, bound, first)
+                    last = jnp.where((most_place < bound) & (last == length), bound, last)
+                first = first // 128
+                needed = (last + 127) // 128 - first
+                count = length // 128
+                for choice in reversed(window_counts(length)):
+                    count = jnp.where(needed <= choice, choice, count)
+                window_ref[0, at] = jnp.minimum(first, length // 128 - count)
+                window_ref[1, at] = count
+            spot = lax.broadcasted_iota(jnp.int32, (rows, rows), 1).astype(F32)
+            sorter = jnp.where(spot == rank - least, 1.0, 0.0).astype(LOW)
+            sorter_ref[...] = sorter
+    for index, stream in enumerate(streams):
+        target = (low_ref, grad_ref)[index // 2]
+        target[index % 2 * rows : (index % 2 + 1) * rows] = dot_nn(sorter, stream[...]).astype(LOW)
+
+
+def setup_call(sides, lengths, anchor, chosen, streams, *waits):
+    length = anchor.shape[1]
+    rows, width = streams[0].shape
+    count = sides.shape[0]
+    here = pl.BlockSpec(memory_space=pltpu.VMEM)
+    scalars = pl.BlockSpec(memory_space=pltpu.SMEM)
+
+    def whole(lines, columns, kind):
+        return jax.ShapeDtypeStruct((lines, columns), kind)
+
+    return pl.pallas_call(
+        setup_kernel,
+        in_specs=[scalars, scalars, here, here, here] + [here] * 4 + [pl.BlockSpec(memory_space=pl.ANY)] * len(waits),
+        out_specs=[scalars] + [here] * (9 + count),
+        out_shape=[whole(2, rows // min(ROW_TILE, rows), jnp.int32)]
+        + [whole(1, length, jnp.int32)] * 2
+        + [whole(rows, 1, jnp.int32)] * 4
+        + [whole(rows, rows, LOW), whole(2 * rows, width, LOW), whole(2 * rows, width, LOW)]
+        + [whole(rows, length, LOW)] * count,
+        scratch_shapes=[pltpu.VMEM((1, length), F32)],
+        compiler_params=pltpu.CompilerParams(vmem_limit_bytes=VMEM_LIMIT),
+        cost_estimate=pl.CostEstimate(flops=8 * rows * rows * width, bytes_accessed=16 * rows * width, transcendentals=0),
+        name="setup_rows",
+    )(sides, lengths, anchor, anchor.reshape(length, 1), chosen, *streams, *waits)
+
+
+def bias_kernel(window_ref, table_ref, place_ref, doc_ref, rank_ref, key_doc_ref, key_rank_ref, *refs):
     out_ref = refs[-1]
     head_count, rows, length = out_ref.shape
     place = place_ref[...]
     doc = doc_ref[...]
     rank = rank_ref[...]
-    for first in range(0, length, 128):
-        key_place = first + lax.broadcasted_iota(jnp.int32, (rows, 128), 1)
-        seen = (key_doc_ref[:, first : first + 128] == doc) & (
-            key_rank_ref[:, first : first + 128] <= rank
-        )
-        choice = jnp.where(seen, bucket_of(key_place - place), 32)
-        for head in range(head_count):
-            for row in range(0, rows, 8):
+    at = pl.program_id(0) * window_ref.shape[1] // pl.num_programs(0)
+    for block in range(length // 128):
+        first = block * 128
+
+        @pl.when((block >= window_ref[0, at]) & (block < window_ref[0, at] + window_ref[1, at]))
+        def _(first=first):
+            key_place = first + lax.broadcasted_iota(jnp.int32, (rows, 128), 1)
+            seen = (key_doc_ref[:, first : first + 128] == doc) & (
+                key_rank_ref[:, first : first + 128] <= rank
+            )
+            choice = jnp.where(seen, bucket_of(key_place - place), 32)
+            for head in range(head_count):
                 line = jnp.broadcast_to(table_ref[head : head + 1, :], (8, 128))
-                out_ref[head, row : row + 8, first : first + 128] = jnp.take_along_axis(
-                    line, choice[row : row + 8], axis=1
-                )
-
-
-def bias_call(table_rows, place, doc, rank, key_doc, key_rank, *waits):
+                for row in range(0, rows, 8):
+                    out_ref[head, row : row + 8, first : first + 128] = jnp.take_along_axis(
+                        line, choice[row : row + 8], axis=1
+                    )
+
+
+def bias_call(window, table_rows, place, doc, rank, key_doc, key_rank, *waits):
     head_count = table_rows.shape[0]
     rows, length = place.shape[0], key_doc.shape[1]
-    tile = min(32, rows)
+    tile = min(64, rows)
     column = pl.BlockSpec((tile, 1), lambda i: (i, 0))
     line = pl.BlockSpec((1, length), lambda i: (0, 0))
     return pl.pallas_call(
         bias_kernel,
         grid=(rows // tile,),
         in_specs=[
+            pl.BlockSpec(memory_space=pltpu.SMEM),
             pl.BlockSpec((head_count, 128), lambda i: (0, 0)),
             column,
             column,
@@ -75,58 +202,74 @@
         out_shape=jax.ShapeDtypeStruct((head_count, rows, length), F32),
         compiler_params=pltpu.CompilerParams(vmem_limit_bytes=VMEM_LIMIT),
         cost_estimate=pl.CostEstimate(
-            flops=0, bytes_accessed=head_count * rows * length * 12, transcendentals=0
+            flops=0, bytes_accessed=head_count * rows * length * 8, transcendentals=0
         ),
         name="bias_rows",
-    )(table_rows, place, doc, rank, key_doc, key_rank, *waits)
-
-
-def attend_kernel(q_ref, k_ref, v_ref, bias_ref, own_ref, *refs):
+    )(window, table_rows, place, doc, rank, key_doc, key_rank, *waits)
+
+
+def attend_kernel(window_ref, q_ref, k_ref, v_ref, bias_ref, own_ref, *refs):
     o_ref, low_ref, p_ref = refs[-3:]
-    rows, length = bias_ref.shape[1:]
-    first_half = lax.broadcasted_iota(jnp.int32, (rows, 128), 1) < 64
-    key_place = lax.broadcasted_iota(jnp.int32, (rows, length), 1)
-    zero = jnp.zeros((rows, 128), LOW)
-    for stream in range(2):
-        queries = q_ref[stream] * jnp.array(0.125, LOW)
+    length = bias_ref.shape[2]
+    tile = bias_ref.shape[1] // window_ref.shape[1]
+    heads = range(bias_ref.shape[0])
+
+    def step(lines, columns, span, first):
+        first_half = lax.broadcasted_iota(jnp.int32, (2 * tile, 128), 1) < 64
+        zero = jnp.zeros((2 * tile, 128), LOW)
+        hidden = lax.broadcasted_iota(jnp.int32, (tile, span), 1) == own_ref[lines, :] - first
+        mine = []
+        for head in heads:
+            lanes = slice(head // 2 * 128, head // 2 * 128 + 128)
+            queries = q_ref[:, lines, lanes].reshape(2 * tile, 128) * jnp.array(0.125, LOW)
+            mine.append(jnp.where(first_half, queries, zero) if head % 2 == 0 else jnp.where(first_half, zero, queries))
+        raw = [dot_nt(mine[head], k_ref[columns, head // 2 * 128 : head // 2 * 128 + 128]) for head in heads]
+        scores = []
+        for head in heads:
+            bias = bias_ref[head, lines, columns]
+            scores.append((raw[head][:tile] + bias, jnp.where(hidden, MASKED, raw[head][tile:] + bias)))
+        most = [[jnp.max(part, axis=1, keepdims=True) for part in pair] for pair in scores]
+        weights = [[jnp.exp(part - top) for part, top in zip(pair, tops)] for pair, tops in zip(scores, most)]
+        shares = [[1.0 / jnp.sum(part, axis=1, keepdims=True) for part in pair] for pair in weights]
+        lows = [[(part * share).astype(LOW) for part, share in zip(pair, both)] for pair, both in zip(weights, shares)]
         parts = []
-        for half in range(2):
-            mine = jnp.where(first_half, queries, zero) if half == 0 else jnp.where(first_half, zero, queries)
-            scores = dot_nt(mine, k_ref[...]) + bias_ref[half]
-            if stream == 1:
-                scores = jnp.where(key_place == own_ref[...], MASKED, scores)
-            weights = jnp.exp(scores - jnp.max(scores, axis=1, keepdims=True))
-            weights = weights * (1.0 / jnp.sum(weights, axis=1, keepdims=True))
-            low = weights.astype(LOW)
-            p_ref[half, stream] = low
-            parts.append(dot_nn(low, v_ref[...]))
-        out = jnp.where(first_half, parts[0], parts[1])
-        o_ref[stream] = out
-        low_ref[stream] = out.astype(LOW)
-
-
-def attend_call(queries, keys, values, bias, own, *waits):
+        for head in heads:
+            for stream in range(2):
+                p_ref[head, stream, lines, columns] = lows[head][stream]
+            values = v_ref[columns, head // 2 * 128 : head // 2 * 128 + 128]
+            parts.append(dot_nn(jnp.concatenate(lows[head], axis=0), values))
+        for pair in range(len(heads) // 2):
+            lanes = slice(pair * 128, pair * 128 + 128)
+            out = jnp.where(first_half, parts[2 * pair], parts[2 * pair + 1])
+            o_ref[:, lines, lanes] = out.reshape(2, tile, 128)
+            low_ref[:, lines, lanes] = out.astype(LOW).reshape(2, tile, 128)
+
+    by_window(window_ref, tile, length, step)
+
+
+def attend_call(window, queries, keys, values, bias, own, *waits):
     _, rows, width = queries.shape
     length = keys.shape[0]
-    tile = min(256, rows)
     pairs = width // 128
-    per_row = pl.BlockSpec((2, tile, 128), lambda h, i: (0, i, h))
-    per_key = pl.BlockSpec((length, 128), lambda h, i: (0, h))
+    group = PAIRS
+    per_row = pl.BlockSpec((2, rows, 128 * group), lambda h: (0, 0, h))
+    per_key = pl.BlockSpec((length, 128 * group), lambda h: (0, h))
     return pl.pallas_call(
         attend_kernel,
-        grid=(pairs, rows // tile),
+        grid=(pairs // group,),
         in_specs=[
+            pl.BlockSpec(memory_space=pltpu.SMEM),
             per_row,
             per_key,
             per_key,
-            pl.BlockSpec((2, tile, length), lambda h, i: (h, i, 0)),
-            pl.BlockSpec((tile, 1), lambda h, i: (i, 0)),
+            pl.BlockSpec((2 * group, rows, length), lambda h: (h, 0, 0)),
+            pl.BlockSpec((rows, 1), lambda h: (0, 0)),
         ]
         + [pl.BlockSpec(memory_space=pl.ANY)] * len(waits),
         out_specs=[
             per_row,
             per_row,
-            pl.BlockSpec((2, 2, tile, length), lambda h, i: (h, 0, i, 0)),
+            pl.BlockSpec((2 * group, 2, rows, length), lambda h: (h, 0, 0, 0)),
         ],
         out_shape=[
             jax.ShapeDtypeStruct((2, rows, width), F32),
@@ -140,126 +283,131 @@
             transcendentals=4 * pairs * rows * length,
         ),
         name="attend",
-    )(queries, keys, values, bias, own, *waits)
-
-
-def attend_back_kernel(earlier, *refs):
+    )(window, queries, keys, values, bias, own, *waits)
+
+
+def attend_back_kernel(window_ref, *refs):
     q_ref, k_ref, v_ref, do_ref, o_ref, p_ref = refs[:6]
     dq_ref, dk_ref, dv_ref, sum_ref, dk_sum, dv_sum = refs[-6:]
-    rows = q_ref.shape[1]
-    first_half = lax.broadcasted_iota(jnp.int32, (rows, 128), 1) < 64
-    zero = jnp.zeros((rows, 128), LOW)
-
-    @pl.when(pl.program_id(1) == 0)
-    def _():
-        dk_sum[...] = jnp.zeros_like(dk_sum)
-        dv_sum[...] = jnp.zeros_like(dv_sum)
-
-    grads = [[None, None], [None, None]]
-    for half in range(2):
-        span = slice(64 * half, 64 * half + 64)
-        total = refs[6][half] if earlier else None
-        for stream in range(2):
-            grad_out = do_ref[stream]
-            mine = jnp.where(first_half, grad_out, zero) if half == 0 else jnp.where(first_half, zero, grad_out)
-            delta = jnp.sum(mine.astype(F32) * o_ref[stream], axis=1, keepdims=True)
-            low_p = p_ref[half, stream]
-            grad = low_p.astype(F32) * (dot_nt(mine, v_ref[...]) - delta)
-            total = grad if total is None else total + grad
-            low = grad.astype(LOW)
-            grads[stream][half] = dot_nn(low, k_ref[...])
-            queries = q_ref[stream] * jnp.array(0.125, LOW)
-            dk_sum[span, :] += dot_nn(queries.T[span], low)
-            dv_sum[span, :] += dot_nn(grad_out.T[span], low_p)
-        sum_ref[half] = total
-    for stream in range(2):
-        dq_ref[stream] = (jnp.where(first_half, grads[stream][0], grads[stream][1]) * 0.125).astype(LOW)
-
-    @pl.when(pl.program_id(1) == pl.num_programs(1) - 1)
-    def _():
-        dk_ref[...] = dk_sum[...].T.astype(LOW)
-        dv_ref[...] = dv_sum[...].T.astype(LOW)
-
-
-def attend_back_call(span, queries, keys, values, grad_out, out, weights, earlier, partial, *waits):
-    first, pairs = span
+    rows, length = sum_ref.shape[1:]
+    tile = rows // window_ref.shape[1]
+    dk_sum[...] = jnp.zeros_like(dk_sum)
+    dv_sum[...] = jnp.zeros_like(dv_sum)
+
+    def step(lines, columns, span, first):
+        first_half = lax.broadcasted_iota(jnp.int32, (2 * tile, 128), 1) < 64
+        zero = jnp.zeros((2 * tile, 128), LOW)
+        queries = q_ref[:, lines, :].reshape(2 * tile, 128) * jnp.array(0.125, LOW)
+        grad_out = do_ref[:, lines, :].reshape(2 * tile, 128)
+        out = o_ref[:, lines, :].reshape(2 * tile, 128)
+        queries_t, grad_out_t = queries.T, grad_out.T
+        keys, values = k_ref[columns, :], v_ref[columns, :]
+        heads = [slice(0, 64), slice(64, 128)]
+        mine = [jnp.where(first_half, grad_out, zero), jnp.where(first_half, zero, grad_out)]
+        raw = [dot_nt(part, values) for part in mine]
+        low_p = [p_ref[half, :, lines, columns].reshape(2 * tile, span) for half in range(2)]
+        for half in range(2):
+            dv_sum[heads[half], columns] += dot_nn(grad_out_t[heads[half]], low_p[half])
+        delta = [jnp.sum(part.astype(F32) * out, axis=1, keepdims=True) for part in mine]
+        grads = [low_p[half].astype(F32) * (raw[half] - delta[half]) for half in range(2)]
+        lows = [grad.astype(LOW) for grad in grads]
+        parts = [dot_nn(low, keys) for low in lows]
+        for half in range(2):
+            sum_ref[half, lines, columns] = (grads[half][:tile] + grads[half][tile:]).astype(LOW)
+            dk_sum[heads[half], columns] += dot_nn(queries_t[heads[half]], lows[half])
+        grad_q = (jnp.where(first_half, parts[0], parts[1]) * 0.125).astype(LOW)
+        dq_ref[:, lines, :] = grad_q.reshape(2, tile, 128)
+
+    by_window(window_ref, tile, length, step)
+    dk_ref[...] = dk_sum[...].T.astype(LOW)
+    dv_ref[...] = dv_sum[...].T.astype(LOW)
+
+
+def attend_back_call(heads, window, queries, keys, values, grad_out, out, weights, partial, *waits):
+    first, pairs = heads
     rows, width = queries.shape[1:]
     length = keys.shape[0]
-    tile = min(256, rows)
-    per_row = pl.BlockSpec((2, tile, 128), lambda h, i: (0, i, h + first))
-    per_key = pl.BlockSpec((length, 128), lambda h, i: (0, h + first))
-    per_score = pl.BlockSpec((2, tile, length), lambda h, i: (h + first, i, 0))
-    more = [] if earlier is None else [earlier]
+    per_row = pl.BlockSpec((2, rows, 128), lambda h: (0, 0, h + first))
+    per_key = pl.BlockSpec((length, 128), lambda h: (0, h + first))
+    per_score = pl.BlockSpec((2, rows, length), lambda h: (h + first, 0, 0))
     begun = [] if partial is None else list(partial)
     return pl.pallas_call(
-        functools.partial(attend_back_kernel, earlier is not None),
-        grid=(pairs, rows // tile),
+        attend_back_kernel,
+        grid=(pairs,),
         in_specs=[
+            pl.BlockSpec(memory_space=pltpu.SMEM),
             per_row,
             per_key,
             per_key,
             per_row,
             per_row,
-            pl.BlockSpec((2, 2, tile, length), lambda h, i: (h + first, 0, i, 0)),
+            pl.BlockSpec((2, 2, rows, length), lambda h: (h + first, 0, 0, 0)),
         ]
-        + [per_score] * len(more)
         + [pl.BlockSpec(memory_space=pl.ANY)] * len(begun + list(waits)),
         out_specs=[per_row, per_key, per_key, per_score],
         out_shape=[
             jax.ShapeDtypeStruct((2, rows, width), LOW),
             jax.ShapeDtypeStruct((length, width), LOW),
             jax.ShapeDtypeStruct((length, width), LOW),
-            jax.ShapeDtypeStruct((width // 64, rows, length), F32),
+            jax.ShapeDtypeStruct((width // 64, rows, length), LOW),
         ],
-        input_output_aliases={6 + len(more) + index: index for index in range(len(begun))},
+        input_output_aliases={7 + index: index for index in range(len(begun))},
         scratch_shapes=[pltpu.VMEM((128, length), F32)] * 2,
         compiler_params=pltpu.CompilerParams(vmem_limit_bytes=VMEM_LIMIT),
         cost_estimate=pl.CostEstimate(
             flops=32 * rows * length * 128 * pairs,
-            bytes_accessed=pairs * rows * length * 24,
+            bytes_accessed=pairs * rows * length * 16,
             transcendentals=0,
         ),
         name="attend_back",
-    )(queries, keys, values, grad_out, out, weights, *more, *begun, *waits)
-
-
-def table_kernel(sum_count, *refs):
-    sum_refs, place_ref, out_ref = refs[:sum_count], refs[sum_count], refs[-1]
-    rows, length = sum_refs[0].shape[1:]
-    head_count = sum(sum_ref.shape[0] for sum_ref in sum_refs)
+    )(window, queries, keys, values, grad_out, out, weights, *begun, *waits)
+
+
+def table_kernel(layers, window_ref, place_ref, *refs):
+    sum_refs, (out_ref, total_ref) = refs[:layers], refs[-2:]
+    head_count, rows, length = sum_refs[0].shape
     bucket_count = out_ref.shape[0] // 8
 
     @pl.when(pl.program_id(0) == 0)
     def _():
-        out_ref[...] = jnp.zeros_like(out_ref)
-
-    key_place = lax.broadcasted_iota(jnp.int32, (8, length), 1)
-    total = jnp.zeros(out_ref.shape, F32)
-    for row in range(0, rows, 8):
-        choice = bucket_of(key_place - place_ref[row : row + 8])
-        chosen = jnp.concatenate(
-            [jnp.where(choice == bucket, 1.0, 0.0) for bucket in range(bucket_count)], axis=0
-        ).astype(LOW)
-        part = jnp.concatenate([sum_ref[:, row : row + 8, :] for sum_ref in sum_refs], axis=0)
-        part = part.reshape(head_count * 8, length).astype(LOW)
-        total = total + dot_nt(chosen, part)
-    out_ref[...] += total
-
-
-def table_call(score_sums, place, bucket_count, *waits):
-    rows, length = score_sums[0].shape[1:]
-    head_count = sum(score_sum.shape[0] for score_sum in score_sums)
-    tile = min(32, rows)
+        total_ref[...] = jnp.zeros_like(total_ref)
+
+    at = pl.program_id(0) * window_ref.shape[1] // pl.num_programs(0)
+    first = pl.multiple_of(window_ref[0, at] * 128, 128)
+    for count in window_counts(length):
+
+        @pl.when(window_ref[1, at] == count)
+        def _(span=count * 128):
+            key_place = first + lax.broadcasted_iota(jnp.int32, (8, span), 1)
+            chosen, parts = [], []
+            for lines in range(0, rows, 16):
+                both = sum(ref[:, lines : lines + 16, pl.ds(first, span)].astype(F32) for ref in sum_refs)
+                for row in range(0, 16, 8):
+                    choice = bucket_of(key_place - place_ref[lines + row : lines + row + 8])
+                    masks = [jnp.where(choice == bucket, 1.0, 0.0) for bucket in range(bucket_count)]
+                    chosen.append(jnp.concatenate(masks, axis=0).astype(LOW))
+                    parts.append(both[:, row : row + 8].reshape(head_count * 8, span).astype(LOW))
+            total_ref[...] += dot_nt(jnp.concatenate(chosen, axis=1), jnp.concatenate(parts, axis=1))
+
+    out_ref[...] = total_ref[...]
+
+
+def table_call(window, score_sums, place, bucket_count, *waits):
+    head_count, rows, length = score_sums[0].shape
+    tile = min(128, rows)
+    layers = len(score_sums)
     grouped = pl.pallas_call(
-        functools.partial(table_kernel, len(score_sums)),
+        functools.partial(table_kernel, layers),
         grid=(rows // tile,),
         in_specs=[
-            pl.BlockSpec((score_sum.shape[0], tile, length), lambda i: (0, i, 0)) for score_sum in score_sums
+            pl.BlockSpec(memory_space=pltpu.SMEM),
+            pl.BlockSpec((tile, 1), lambda i: (i, 0)),
         ]
-        + [pl.BlockSpec((tile, 1), lambda i: (i, 0))]
+        + [pl.BlockSpec((head_count, tile, length), lambda i: (0, i, 0))] * layers
         + [pl.BlockSpec(memory_space=pl.ANY)] * len(waits),
         out_specs=pl.BlockSpec((8 * bucket_count, 8 * head_count), lambda i: (0, 0)),
         out_shape=jax.ShapeDtypeStruct((8 * bucket_count, 8 * head_count), F32),
+        scratch_shapes=[pltpu.VMEM((8 * bucket_count, 8 * head_count), F32)],
         compiler_params=pltpu.CompilerParams(vmem_limit_bytes=VMEM_LIMIT),
         cost_estimate=pl.CostEstimate(
             flops=512 * rows * length * head_count,
@@ -267,7 +415,7 @@
             transcendentals=0,
         ),
         name="table_sums",
-    )(*score_sums, place, *waits)
+    )(window, place, *score_sums, *waits)
     grouped = grouped.reshape(bucket_count, 8, head_count, 8)
     return jnp.sum(grouped * jnp.eye(8, dtype=F32)[None, :, None, :], axis=(1, 3))
 
@@ -303,7 +451,7 @@
     piece_refs, refs = refs[:count], refs[count:]
     gain_ref, shift_ref = refs[:2]
     result_ref, low_ref, middle_ref, middle_low_ref, active_ref, slope_ref, one_ref, two_ref = refs[-8:]
-    mixed = stream_ref[...] + dot_nn(out_ref[...], proj_ref[...])
+    mixed = stream_ref[...].astype(F32) + dot_nn(out_ref[...], proj_ref[...])
     middle, one_ref[...] = norm_rows(mixed, gain_ref[0:1], shift_ref[0:1])
     middle_ref[...] = middle
     middle_low = middle.astype(LOW)
@@ -323,15 +471,18 @@
     low_ref[...] = result.astype(LOW)
 
 
-def layer_tail_call(stream, out_low, proj, pieces, span, gains, shifts, *waits):
+def layer_tail_call(stream, out_low, proj, pieces, span, gains, shifts, part, partial, *waits):
     rows, width = stream.shape
+    share = 1 if part is None else 2
     hidden = span * len(pieces)
     pieces, plan = pieces_of(pieces)
     proj, proj_at = proj
-    tile = min(256, rows)
+    tile = min(256, rows // share)
+    first = (part or 0) * (rows // 2 // tile)
+    begun = [] if partial is None else list(partial)
 
     def per_row(columns):
-        return pl.BlockSpec((tile, columns), lambda i: (i, 0))
+        return pl.BlockSpec((tile, columns), lambda i: (i + first, 0))
 
     def fixed(shape):
         return pl.BlockSpec(shape, lambda i: (0, 0), pipeline_mode=pl.Buffered(1))
@@ -341,11 +492,11 @@
 
     return pl.pallas_call(
         functools.partial(layer_tail_kernel, len(pieces), plan, span),
-        grid=(rows // tile,),
+        grid=(rows // share // tile,),
         in_specs=[per_row(width), per_row(width), pl.BlockSpec((width, width), lambda i: (0, proj_at), pipeline_mode=pl.Buffered(1))]
         + [fixed(piece.shape) for piece in pieces]
         + [fixed((2, width))] * 2
-        + [pl.BlockSpec(memory_space=pl.ANY)] * len(waits),
+        + [pl.BlockSpec(memory_space=pl.ANY)] * len(begun + list(waits)),
         out_specs=[
             per_row(width), per_row(width), per_row(width), per_row(width),
             per_row(hidden), per_row(hidden), per_row(1), per_row(1),
@@ -354,14 +505,15 @@
             whole(width, F32), whole(width, LOW), whole(width, F32), whole(width, LOW),
             whole(hidden, LOW), whole(hidden, LOW), whole(1, F32), whole(1, F32),
         ],
+        input_output_aliases={5 + len(pieces) + index: index for index in range(len(begun))},
         compiler_params=pltpu.CompilerParams(vmem_limit_bytes=VMEM_LIMIT),
         cost_estimate=pl.CostEstimate(
-            flops=2 * rows * width * (width + 2 * hidden),
+            flops=2 * rows // share * width * (width + 2 * hidden),
             bytes_accessed=4 * rows * hidden + 12 * rows * width + 4 * width * hidden,
             transcendentals=2 * rows * hidden,
         ),
         name="layer_tail",
-    )(stream, out_low, proj, *pieces, gains, shifts, *waits)
+    )(stream, out_low, proj, *pieces, gains, shifts, *begun, *waits)
 
 
 def layer_tail_back_kernel(count, plan, span, *refs):
@@ -374,7 +526,7 @@
     def _():
         terms_ref[...] = begun_ref[...]
 
-    grad = grad_ref[...]
+    grad = grad_ref[...].astype(F32)
     normal = (result_ref[...] - shift_ref[1:2]) / gain_ref[1:2]
     terms_ref[1:2] += jnp.sum(grad * normal, axis=0, keepdims=True)
     terms_ref[3:4] += jnp.sum(grad, axis=0, keepdims=True)
@@ -685,7 +837,12 @@
         return tensor
 
     def scatter(self, tensor):
-        part = lax.psum_scatter(tensor, "dp", scatter_dimension=0, tiled=True)
+        return self.scatter_end_blocks(self.scatter_rows(tensor))
+
+    def scatter_rows(self, tensor):
+        return lax.psum_scatter(tensor, "dp", scatter_dimension=0, tiled=True)
+
+    def scatter_end_blocks(self, part):
         if self.blocks == 2:
             return part.astype(F32) + self.from_block(part).astype(F32)
         return lax.psum(part, "blk").astype(F32)
@@ -716,94 +873,74 @@
     grid.place()
     block_index = grid.block_at
 
-    anchor = permutation[0]
-    positions = jnp.arange(length, dtype=jnp.int32)
-    bounds = jnp.cumsum(doc_lengths[0])[:-1].astype(jnp.int32)
-    key_doc = jnp.sum((positions[:, None] >= bounds[None, :]).astype(jnp.int32), axis=1)
-    starts = (positions == 0) | jnp.any(positions[:, None] == bounds[None, :], axis=1)
-    live = (predicted[0] == 1) & jnp.logical_not(starts)
-    position_rank = jnp.sum(
-        jnp.where(anchor[None, :] == positions[:, None], positions[None, :], 0), axis=1
+    paired = grid.paired
+    layers = range(layer_count)
+
+    def chip_of(layer_index, *waits):
+        return grid.gather_chip((ffn_in[layer_index], ffn_out_t[layer_index]), waits)
+
+    chip = chip_of(0) if paired else None
+    sides = jnp.stack([block_index, 1 - block_index]) if paired else (block_index + jnp.arange(blocks)) % blocks
+    (
+        window, key_doc, key_rank, place_column, place_doc, place_rank, own_column, sorter, stream_low, grad_low,
+        *spreads,
+    ) = setup_call(
+        sides.astype(jnp.int32), doc_lengths, permutation, predicted,
+        (content_in[0], query_in[0], cot_content[0], cot_query[0]), *((chip,) if paired else ()),
     )
-    key_rank = jnp.where(live, position_rank, -1)
-    split = anchor.reshape(blocks, rows)
-    order = jnp.sum((split[:, None, :] < split[:, :, None]).astype(jnp.int32), axis=2)
-    sorted_place = jnp.sum(
-        jnp.where(order[:, None, :] == jnp.arange(rows)[None, :, None], split[:, None, :], 0), axis=2
-    )
-    own_order = lax.dynamic_index_in_dim(order, block_index, 0, False)
-    place = lax.dynamic_index_in_dim(sorted_place, block_index, 0, False)
-    sorter = (own_order[None, :] == jnp.arange(rows)[:, None]).astype(LOW)
-    if grid.paired:
-        own_spread, other_spread = (
-            (lax.dynamic_index_in_dim(sorted_place, side, 0, True) == positions[:, None]).astype(LOW)
-            for side in (block_index, 1 - block_index)
-        )
-    spread = (sorted_place.reshape(1, length) == positions[:, None]).astype(LOW)
-    at_place = (place[:, None] == positions[None, :]).astype(jnp.int32)
-    place_doc = jnp.sum(at_place * key_doc[None, :], axis=1)
-    place_rank = jnp.sum(at_place * position_rank[None, :], axis=1)
-    place_live = jnp.sum(at_place * live.astype(jnp.int32)[None, :], axis=1)
-    own_column = jnp.where(place_live == 1, place, -1)[:, None]
-    place_column = place[:, None]
+    stream = stream_low
     table_rows = jnp.concatenate(
         [bias_table.T, jnp.full((head_count, 128 - bucket_count), MASKED, F32)], axis=1
     )
 
-    def sort_rows(tensor):
-        return dot_nn(sorter, tensor).astype(LOW)
-
-    def other_blocks(tensor):
-        if grid.paired:
-            other = grid.from_block(tensor)
-            return (dot_nn(own_spread, tensor) + dot_nn(other_spread, other)).astype(LOW)
-        gathered = lax.all_gather(tensor, "blk", axis=0, tiled=True)
-        return dot_nn(spread, gathered).astype(LOW)
-
-    paired = grid.paired
-    first_qkv = grid.gather(attn_weights[0])
-    others = jnp.concatenate(
-        [out_weight[layer_index] for layer_index in range(layer_count)]
-        + [attn_weights[layer_index] for layer_index in range(1, layer_count)],
-        axis=1,
-    )
-    others = grid.gather(others)
-    starts = [(layer_count + 3 * layer_index) * width for layer_index in range(layer_count - 1)]
-    attn_full = [first_qkv] + [others[:, start : start + 3 * width] for start in starts]
+    def other_blocks(tensor, come):
+        if paired:
+            come = grid.from_block(tensor) if come is None else come
+            return (dot_tn(spreads[0], tensor) + dot_tn(spreads[1], come)).astype(LOW)
+        gathered = lax.all_gather(tensor, "blk", axis=0, tiled=False)
+        parts = [
+            dot_tn(spread, lax.dynamic_index_in_dim(gathered, (block_index + step) % blocks, 0, False))
+            for step, spread in enumerate(spreads)
+        ]
+        return sum(parts).astype(LOW)
+
     hidden = ffn_in.shape[2]
     span = hidden // 4 if paired else hidden
-
-    def chip_of(layer_index, *waits):
-        return grid.gather_chip((ffn_in[layer_index], ffn_out_t[layer_index]), waits)
-
-    stream_low = jnp.concatenate([sort_rows(content_in[0]), sort_rows(query_in[0])], axis=0)
-    stream = stream_low.astype(F32)
-    if paired:
-        chip = chip_of(0)
     bias = bias_call(
-        table_rows, place_column, place_doc[:, None], place_rank[:, None], key_doc[None], key_rank[None],
-        *((chip, stream_low) if paired else ()),
+        window, table_rows, place_column, place_doc, place_rank, key_doc, key_rank, *((chip,) if paired else ())
     )
+    first_qkv = attn_weights[0]
     if paired:
         line = grid.gather_line(chip, (bias,))
         if layer_count > 1:
             next_chip = chip_of(1, line)
+        sheet = grid.gather_sheet(line, ())
+    first_qkv = grid.gather(first_qkv)
+    if paired:
+        first_qkv = hold(first_qkv, sheet)
+    others = grid.gather(
+        jnp.concatenate([out_weight[i] for i in layers] + [attn_weights[i] for i in layers[1:]], axis=1)
+    )
+    starts = [(layer_count + 3 * index) * width for index in range(layer_count - 1)]
+    qkv_full = [first_qkv] + [others[:, start : start + 3 * width] for start in starts]
     kept = []
+    next_content = None
     all_pieces = []
     for layer_index in range(layer_count):
-        qkv = attn_full[layer_index]
-        all_content = other_blocks(stream_low[:rows])
+        qkv = qkv_full[layer_index]
+        all_content = other_blocks(stream_low[:rows], next_content)
         queries = dot_nn(stream_low, qkv[:, :width]).astype(LOW).reshape(2, rows, width)
         keys = dot_nn(all_content, qkv[:, width : 2 * width]).astype(LOW)
         values = dot_nn(all_content, qkv[:, 2 * width :]).astype(LOW)
         later = ()
         more = paired and layer_index + 1 < layer_count
         if paired:
-            sheet = grid.gather_sheet(line, (queries, keys, values))
+            if layer_index > 0:
+                sheet = grid.gather_sheet(line, (stream_low, queries))
             later = (sheet,)
         if more:
             later = (sheet, next_chip)
-        out, out_low, weights = attend_call(queries, keys, values, bias, own_column, *later)
+        out, out_low, weights = attend_call(window, queries, keys, values, bias, own_column, *later)
         later = ()
         if paired:
             waits_near = (out_low,)
@@ -821,10 +958,15 @@
             if layer_index + 2 < layer_count:
                 next_chip = chip_of(layer_index + 2, line)
         out_low = out_low.reshape(2 * rows, width)
-        result, low, middle, middle_low, active, slope, inverse_one, inverse_two = layer_tail_call(
-            stream, out_low, (others, layer_index), pieces, span,
-            norm_gains[layer_index], norm_shifts[layer_index], *later,
-        )
+        partial = None
+        for part in (0, 1) if more else (None,):
+            partial = layer_tail_call(
+                stream, out_low, (others, layer_index), pieces, span,
+                norm_gains[layer_index], norm_shifts[layer_index], part, partial, *later,
+            )
+            if part == 0:
+                next_content = grid.from_block(partial[1][:rows])
+        result, low, middle, middle_low, active, slope, inverse_one, inverse_two = partial
         kept.append(
             (
                 stream_low, all_content, queries, keys, values, out, out_low, weights,
@@ -844,14 +986,22 @@
     content_out = unsort(stream_low[:rows]).astype(LOW)
     query_out = unsort(stream_low[rows:]).astype(LOW)
 
-    grad_stream = [sort_rows(cot_content[0]).astype(F32), sort_rows(cot_query[0]).astype(F32)]
+    grad_stream = None
     norm_terms = [None] * layer_count
     matrix_rows = [None] * layer_count
+    attn_rows = [None] * layer_count
+    attn_parts = [None] * layer_count
     side = jnp.full((1,), grid.core_at, jnp.int32)
     pairs = width // 128
-    score_sum = None
+    score_sums = []
     pending = {}
     third = width // 2
+
+    def content_side(own, come):
+        own, grad_all = own
+        if grad_all is not None:
+            own = own + dot_nn(spreads[0], grad_all)
+        return own + come.astype(F32)
 
     def keys_back(grad_k, grad_v, qkv):
         return (dot_nt(grad_k, qkv[:, width : 2 * width]) + dot_nt(grad_v, qkv[:, 2 * width :])).astype(LOW)
@@ -859,15 +1009,7 @@
     def finish_rows(high):
         shared = grid.sum_blocks(high[:, 2 * span :])
         sides = grid.halves(jnp.concatenate([high[:, : 2 * span], shared], axis=1))
-        proj_grad = jnp.concatenate([one[:, 2 * span : 2 * span + third] for one in sides], axis=1)
-        attn_grad = jnp.concatenate(
-            [
-                one[:, 2 * span + (1 + index) * third : 2 * span + (2 + index) * third]
-                for index in range(3)
-                for one in sides
-            ],
-            axis=1,
-        )
+        proj_grad = jnp.concatenate([one[:, 2 * span :] for one in sides], axis=1)
         half = jnp.concatenate([one[:, : 2 * span] for one in sides], axis=1)
         other = grid.from_block(half)
         first = grid.block_at == 0
@@ -883,28 +1025,34 @@
             )
             for which in range(2)
         )
-        return tuple(tensor.astype(F32) for tensor in (attn_grad, proj_grad, inner_grad, outer_grad))
+        return tuple(tensor.astype(F32) for tensor in (proj_grad, inner_grad, outer_grad))
 
     def waits(*names):
         return [pending[name] for name in names if name in pending]
 
+    come = None
     for layer_index in reversed(range(layer_count)):
         (
             stream_low, all_content, queries, keys, values, out, out_low, weights,
             result, middle, middle_low, active, slope, inverse_one, inverse_two,
         ) = kept[layer_index]
-        qkv = attn_full[layer_index]
+        qkv = qkv_full[layer_index]
         partial = None
         for part in (None,) if layer_index == layer_count - 1 else (1, 0):
-            grad = jnp.concatenate(grad_stream, axis=0) if part is None else grad_stream[part]
+            if part is None:
+                grad = grad_low
+            elif part == 1:
+                grad = grad_stream[1]
+            else:
+                grad = content_side(grad_stream[0], hold(come, partial[0]) if paired else come)
             partial = layer_tail_back_call(
                 grad, result, inverse_two, middle, inverse_one, slope, (others, layer_index),
                 all_pieces[layer_index], span, norm_gains[layer_index], norm_shifts[layer_index],
-                part, partial, *waits("sum"),
+                part, partial, *waits("attn"),
             )
         two_low, inner_low, grad_one, branch_low, grad_out, norm_terms[layer_index] = partial
         grad_out = grad_out.reshape(2, rows, width)
-        back = (queries, keys, values, grad_out, out, weights, score_sum)
+        back = (window, queries, keys, values, grad_out, out, weights)
         if paired:
             def steps(name, quarter, come=None):
                 return [
@@ -936,44 +1084,43 @@
             grad_q, grad_k, grad_v, score_sum = attend_back_call(
                 (pairs // 2, pairs - pairs // 2), *back, partial, *waits("low")
             )
+            score_sums.append(score_sum)
             grad_q = grad_q.reshape(2 * rows, width)
             ffn_sum = (held["mine"].astype(F32) + arrived.astype(F32)).astype(LOW)
+            ffn_sum = jnp.concatenate([ffn_sum, held["proj"]], axis=1)
             if layer_index == 0:
-                ffn_sum = jnp.concatenate([ffn_sum, held["proj"]], axis=1)
                 ffn_begun = grid.low_begin(ffn_sum)
             if layer_index > 0:
                 grad_all = keys_back(grad_k, grad_v, qkv)
-                passed = dot_tn(other_spread, grad_all).astype(LOW)
+                passed = dot_nn(spreads[1], grad_all).astype(LOW)
             attn = products_call(
                 "products_attn", side,
                 [
-                    (lhs, rhs, third, block, out_name, index, None)
-                    for block, out_name in (("other", "sent"), ("side", "mine"))
+                    (lhs, rhs, width, 0, "attn", index, None)
                     for index, (lhs, rhs) in enumerate(
                         ((stream_low, grad_q), (all_content, grad_k), (all_content, grad_v))
                     )
                 ],
-                {"sent": (width, 3 * third, third), "mine": (width, 3 * third, third)},
+                {"attn": (width, 3 * width, width)},
                 [passed, ffn_sum] if layer_index > 0 else [ffn_sum],
-            )
-            attn_sum = (attn["mine"].astype(F32) + grid.from_core(attn["sent"]).astype(F32)).astype(LOW)
+            )["attn"]
             if layer_index == 0:
-                grad_q, grad_k, grad_v = (hold(tensor, attn["sent"]) for tensor in (grad_q, grad_k, grad_v))
+                grad_q, grad_k, grad_v = (hold(tensor, attn) for tensor in (grad_q, grad_k, grad_v))
                 grad_all = keys_back(grad_k, grad_v, qkv)
-                passed = dot_tn(other_spread, grad_all).astype(LOW)
+                ffn_low = grid.scatter_end(ffn_begun, grad_all)
+                ffn_begun = grid.high_begin(ffn_low)
+                passed = dot_nn(spreads[1], grad_all).astype(LOW)
+            attn_part = grid.scatter_rows(attn)
+            attn_parts[layer_index] = attn_part
             if "high_begun" in pending:
-                high = grid.scatter_end(pending["high_begun"], attn["sent"])
-                matrix_rows[layer_index + 1] = finish_rows(high)
+                upper = pending["high_begun"]
             if layer_index > 0:
-                total = jnp.concatenate([ffn_sum, held["proj"], attn_sum], axis=1)
-                pending = {"attn_sent": attn["sent"], "sum": total, "low_begun": grid.low_begin(total)}
+                pending = {"attn": attn, "sum": ffn_sum, "low_begun": grid.low_begin(ffn_sum)}
             else:
-                attn_begun = grid.low_begin(attn_sum)
-                ffn_low = grid.scatter_end(ffn_begun, attn["sent"])
-                ffn_begun = grid.high_begin(ffn_low)
-                pending = {"attn_sum": attn_sum, "ffn_low": ffn_low}
+                pending = {"passed": passed, "ffn_low": ffn_low}
         else:
             grad_q, grad_k, grad_v, score_sum = attend_back_call((0, pairs), *back, None)
+            score_sums.append(score_sum)
             grad_q = grad_q.reshape(2 * rows, width)
             terms = [
                 jnp.concatenate(
@@ -983,33 +1130,42 @@
                 dot_tn(middle_low, inner_low),
                 dot_tn(two_low, active),
             ]
-            matrix_rows[layer_index] = tuple(grid.scatter(term.astype(LOW)) for term in terms)
+            attn_rows[layer_index], *matrix_rows[layer_index] = (grid.scatter(term.astype(LOW)) for term in terms)
         query_side = grad_one + dot_nt(grad_q, qkv[:, :width])
+        grad_stream = [(query_side[:rows], grad_all if paired else None), query_side[rows:]]
         if layer_index == 0:
-            table_grad = table_call([score_sum], place_column, bucket_count, *waits("attn_sum", "ffn_low"))
+            rest = grad_stream[1]
+            if paired:
+                rest = hold(rest, ffn_low)
+            query_grad = unsort_wide(rest)
+            table_grad = table_call(
+                window, score_sums, place_column, bucket_count, *([passed, ffn_low, query_grad] if paired else [])
+            )
         if paired:
             come = grid.from_block(passed)
-            if layer_index == 0:
-                come = hold(come, table_grad)
-            grad_keys_in = dot_tn(own_spread, grad_all) + come.astype(F32)
         else:
-            grad_split = dot_tn(spread, keys_back(grad_k, grad_v, qkv)).astype(LOW)
-            grad_keys_in = lax.psum_scatter(grad_split, "blk", scatter_dimension=0, tiled=True).astype(F32)
-        grad_stream = [query_side[:rows] + grad_keys_in, query_side[rows:]]
+            grad_all = keys_back(grad_k, grad_v, qkv)
+            grad_split = jnp.stack([dot_nn(spread, grad_all).astype(LOW) for spread in spreads])
+            grad_split = jnp.roll(grad_split, block_index, axis=0)
+            come = lax.psum_scatter(grad_split, "blk", scatter_dimension=0, tiled=False)
     if paired:
-        attn_begun = grid.high_begin(grid.scatter_end(attn_begun, table_grad))
-        high = jnp.concatenate([grid.scatter_end(ffn_begun, table_grad), grid.scatter_end(attn_begun)], axis=1)
-        matrix_rows[0] = finish_rows(high)
+        come = hold(come, table_grad)
+        ffn_high = grid.scatter_end(ffn_begun, table_grad)
+        if layer_count > 1:
+            matrix_rows[1] = finish_rows(grid.scatter_end(upper, table_grad))
+        matrix_rows[0] = finish_rows(hold(ffn_high, attn_part))
+        attn_rows = [grid.scatter_end_blocks(hold(part, table_grad)) for part in attn_parts]
+    grad_stream[0] = content_side(grad_stream[0], come)
     table_lines = jnp.pad(table_grad.T, ((0, 0), (0, width - bucket_count)))
     sums = grid.sum_all(jnp.concatenate([*[terms[:4] for terms in norm_terms], table_lines], axis=0))
     norm_sum = sums[: 4 * layer_count].reshape(layer_count, 2, 2, width)
     table_total = sums[4 * layer_count :, :bucket_count].T
-    matrix_grads = tuple(jnp.stack(layers, axis=0) for layers in zip(*matrix_rows))
+    matrix_grads = tuple(jnp.stack(rows_of, axis=0) for rows_of in (attn_rows, *zip(*matrix_rows)))
     return (
         content_out[None],
         query_out[None],
         unsort_wide(grad_stream[0])[None],
-        unsort_wide(grad_stream[1])[None],
+        query_grad[None],
         *matrix_grads,
         norm_sum[:, 0],
         norm_sum[:, 1],

time: 788 us -> 685 us (0.87)
  Pallas kernels: 387 us -> 346 us
  waiting for transfers between devices: 148 us -> 121 us
  other arithmetic: 53.1 us -> 32.7 us
  local copies, waits for them, and re-layouts: 51 us -> 39.8 us
    pallas_call x7 -> x8, Pallas kernels: 174 us -> 135 us  [the longest x2 58.7 us: attend_call(): pl.pallas_call(attend_kernel, grid=(pairs // group,), in_specs=[pl.BlockS...]
    ppermute x13 -> x15, waiting for transfers between devices: 78.6 us -> 39.8 us  [from_block(): return lax.ppermute(tensor, 'blk', [(0, 1), (1, 0)])]
    ppermute x15 -> x12, waiting for transfers between devices: 33.2 us -> 0.03 us  [from_high(): lax.ppermute(tensor, 'dp', [(i, (i + 2 * self.low * step) % self.total) f...]
    ppermute x4, waiting for transfers between devices: 1.56 us -> 23.8 us  [sum_all(): lax.ppermute(tensor, 'dp', [(i, i ^ bit) for i in range(self.total)])]
    ppermute x5 -> x4, waiting for transfers between devices: 26.3 us -> 40.7 us  [from_low(): return lax.ppermute(tensor, 'dp', pairs)]
    pallas_call x2 -> x3, Pallas kernels: 45.3 us -> 51.2 us  [layer_tail_call(): pl.pallas_call(functools.partial(layer_tail_kernel, len(pieces), plan, sp...]
    unnamed x181 -> x124, local copies, waits for them, and re-layouts: 22.1 us -> 16.5 us
    ppermute x13 -> x15, starting transfers between devices: 16.5 us -> 20.2 us  [from_block(): return lax.ppermute(tensor, 'blk', [(0, 1), (1, 0)])]
  transfers between devices with their start and end apart: 55 -> 53, of which waited for: 20 -> 19; matrix products, arithmetic and copies ran while one was open for 17% -> 16% of each run, Pallas kernels for 32% -> 39%
where the time goes in v2:
time: 685 us; the launch traced here: 677 us
  Pallas kernels  346 us (51%)
  waiting for transfers between devices  121 us (18%)
  matrix products  61.7 us (9%)
  starting transfers between devices  60.9 us (9%)
  local copies, waits for them, and re-layouts  39.8 us (6%)
  other arithmetic  32.7 us (5%)
  between operations  15.3 us (2%)
    pallas_call x8, Pallas kernels, products_call(): pl.pallas_call(functools.partial(product_kernel, plan), grid_spec=pltpu.P...  76.5 us
    pallas_call x2, Pallas kernels, attend_call(): pl.pallas_call(attend_kernel, grid=(pairs // group,), in_specs=[pl.BlockS...  58.7 us
    pallas_call x4, Pallas kernels, attend_back_call(): pl.pallas_call(attend_back_kernel, grid=(pairs,), in_specs=[pl.BlockSpec(...  56.6 us
    pallas_call x3, Pallas kernels, layer_tail_call(): pl.pallas_call(functools.partial(layer_tail_kernel, len(pieces), plan, sp...  51.2 us
    pallas_call x3, Pallas kernels, layer_tail_back_call(): pl.pallas_call(functools.partial(layer_tail_back_kernel, len(pieces), pla...  50.8 us
    ppermute x4, waiting for transfers between devices, from_low(): return lax.ppermute(tensor, 'dp', pairs)  40.7 us
    ppermute x15, waiting for transfers between devices, from_block(): return lax.ppermute(tensor, 'blk', [(0, 1), (1, 0)])  39.8 us
    dot_general x10, matrix products, dot_nn(): return jnp.dot(left_side, right_side, preferred_element_type=F32)  30.3 us
  transfers between devices with their start and end apart: 53, of which 19 were waited for; matrix products, arithmetic and copies ran while one was open for 16% of the time, Pallas kernels for 39%

profile of v2, /device:TPU:0, one launch (start us, length us, event | category | flops | bytes accessed | tf_op | source)
XLA Modules:
  0.0 677.4 jit_solution(7643809184417210239)
XLA Ops:
  24.8 7.9 %setup_rows.1 = (s32[2,4]{1,0:T(2,128)}, s32[1,1024]{1,0:T(1,128)}, s32[1,1024]{1,0:T(1,128)}, s32[512,1]{1,0:T(8,128)}, s32[512,1]{1,0:T(8,128)}, /*index=5*/s3...) custom-call(s32[2]{0:T(128)} %pad_add_fusion.side_ref, ...), custom_call_target="tpu_custom_call" | custom-call | flops 1610612736 | bytes 6291456 | tf_op jit(solution)/shard_map/setup_rows/pallas_call | solution.py:141
  32.8 17.7 %bias_rows.1.refs_4_.bias_ref = f32[12,512,1024]{2,1,0:T(8,128)} custom-call(s32[2,4]{1,0:T(2,128)} %get-tuple-element.99.window_ref, f32[12,128]{1,0:T(8,128)} %concatenate.141.table_ref, s32[512,1]{1,0:T(8,128)} %get-tuple-element.100.place_ref, s32[512,1]{1,0:T(8,128)} %get-tuple-element.101.doc_ref, s32[512,1]{1,0:T(8,128)} %get-tuple-element.102.rank_ref, ...), custom_call_target="tpu_custom_call" | custom-call | bytes 50331648 | tf_op jit(solution)/shard_map/bias_rows/pallas_call | solution.py:188
  70.0 21.1 %collective-permute-done.4.refs_1_ = bf16[4,96,1536]{2,1,0:T(8,128)(2,1)S(1)} collective-permute-done((bf16[4,96,1536]{2,1,0:T(8,128)(2,1)}, bf16[4,96,1536]{2,1,0:T(8,128)(2,1)S(1)}, u32[]{:S(2)}, u32[]{:S(2)}) %collective-permute-start.4) | collective-permute-done | bytes 1179680 | tf_op jit(solution)/shard_map/ppermute | solution.py:764
  110.4 29.4 %attend.2 = (f32[2,512,768]{2,1,0:T(8,128)}, bf16[2,512,768]{2,1,0:T(8,128)(2,1)}, bf16[12,2,512,1024]{3,2,1,0:T(8,128)(2,1)}) custom-call(s32[2,4]{1,0:T(2,128)} %get-tuple-element.99.window_ref, bf16[2,512,768]{2,1,0:T(8,128)(2,1)} %bitcast.211, bf16[1024,768]{1,0:T(8,128)(2,1)} %convolution_convert_fusion.4.k_ref.refs_1_, ...), custom_call_target="tpu_custom_call" | custom-call | flops 6442450944 | bytes 50331648 | tf_op jit(solution)/shard_map/attend/pallas_call | solution.py:257
  143.0 5.7 collective-permute-done.8.refs_0_
  157.2 14.2 %layer_tail.3 = (f32[1024,768]{1,0:T(8,128)}, bf16[1024,768]{1,0:T(8,128)(2,1)}, f32[1024,768]{1,0:T(8,128)}, bf16[1024,768]{1,0:T(8,128)(2,1)}, bf16[1024,3072]...) custom-call(bf16[1024,768]{1,0:T(8,128)(2,1)} %get-tuple-element.98.refs_0_, ...), custom_call_target="tpu_custom_call" | custom-call | flops 5435817984 | bytes 31457280 | tf_op jit(solution)/shard_map/layer_tail/pallas_call | solution.py:493
  175.1 14.7 %layer_tail.4 = (f32[1024,768]{1,0:T(8,128)}, bf16[1024,768]{1,0:T(8,128)(2,1)}, f32[1024,768]{1,0:T(8,128)}, bf16[1024,768]{1,0:T(8,128)(2,1)}, bf16[1024,3072]...) custom-call(bf16[1024,768]{1,0:T(8,128)(2,1)} %get-tuple-element.98., ...), custom_call_target="tpu_custom_call", output_to_operand_aliasing={{0}: (9, {}), {1}: (10, {}), {2}: (11, {}), {3}: (12, {}), ... | custom-call | flops 5435817984 | bytes 31457280 | tf_op jit(solution)/shard_map/layer_tail/pallas_call | solution.py:493
  206.3 29.3 %attend.3 = (f32[2,512,768]{2,1,0:T(8,128)}, bf16[2,512,768]{2,1,0:T(8,128)(2,1)}, bf16[12,2,512,1024]{3,2,1,0:T(8,128)(2,1)}) custom-call(s32[2,4]{1,0:T(2,128)} %get-tuple-element.99.window_ref, bf16[2,512,768]{2,1,0:T(8,128)(2,1)} %bitcast.202, bf16[1024,768]{1,0:T(8,128)(2,1)} %convolution_convert_fusion.1.k_ref.refs_1_, ...), custom_call_target="tpu_custom_call" | custom-call | flops 6442450944 | bytes 50331648 | tf_op jit(solution)/shard_map/attend/pallas_call | solution.py:257
  235.6 15.0 %collective-permute-done.16.refs_0_ = bf16[768,1536]{1,0:T(8,128)(2,1)} collective-permute-done((bf16[768,1536]{1,0:T(8,128)(2,1)}, bf16[768,1536]{1,0:T(8,128)(2,1)}, u32[]{:S(2)}, u32[]{:S(2)}) %collective-permute-start.16) | collective-permute-done | bytes 2359328 | tf_op jit(solution)/shard_map/ppermute | solution.py:759
  256.7 22.3 %layer_tail.5 = (f32[1024,768]{1,0:T(8,128)}, bf16[1024,768]{1,0:T(8,128)(2,1)}, f32[1024,768]{1,0:T(8,128)}, bf16[1024,768]{1,0:T(8,128)(2,1)}, bf16[1024,3072]...) custom-call(f32[1024,768]{1,0:T(8,128)} %get-tuple-element.117.refs_0_.refs_1_, ...), custom_call_target="tpu_custom_call" | custom-call | flops 10871635968 | bytes 31457280 | tf_op jit(solution)/shard_map/layer_tail/pallas_call | solution.py:493
  279.6 22.1 %layer_tail_back.3 = (bf16[1024,768]{1,0:T(8,128)(2,1)}, bf16[1024,3072]{1,0:T(8,128)(2,1)}, f32[1024,768]{1,0:T(8,128)}, bf16[1024,768]{1,0:T(8,128)(2,1)}, bf1...) custom-call(bf16[1024,768]{1,0:T(8,128)(2,1)} %get-tuple-element.121.refs_0_, f32[1024,768]{1,0:T(8,128)} %get-tuple-element.122.refs_1_, ...), custom_call_target="tpu_custom_call" | custom-call | flops 10871635968 | bytes 37748736 | tf_op jit(solution)/shard_map/layer_tail_back/pallas_call | solution.py:573
  301.7 12.5 %products_sent.2 = (bf16[768,1536]{1,0:T(8,128)(2,1)}, bf16[768,1536]{1,0:T(8,128)(2,1)}, bf16[768,384]{1,0:T(8,128)(2,1)}) custom-call(s32[1]{0:T(128)} %bitcast.7.side_ref, bf16[1024,768]{1,0:T(8,128)(2,1)} %get-tuple-element.131.refs_0_, bf16[1024,3072]{1,0:T(8,128)(2,1)} %get-tuple-element.132.refs_1_, ...), custom_call_target="tpu_custom_call" | custom-call | flops 5435817984 | bytes 18119392 | tf_op jit(solution)/shard_map/products_sent/pallas_call | solution.py:664
  320.4 7.2 %products_near.2.refs_8_ = bf16[768,1536]{1,0:T(8,128)(2,1)} custom-call(s32[1]{0:T(128)} %bitcast.7.side_ref, bf16[1024,768]{1,0:T(8,128)(2,1)} %get-tuple-element.131.refs_0_, bf16[1024,3072]{1,0:T(8,128)(2,1)} %get-tuple-element.132.refs_1_, bf16[768,1536]{1,0:T(8,128)(2,1)} %copy-done.33, bf16[1024,768]{1,0:T(8,128)(2,1)} %get-tuple-element.133.refs_2_.refs_3_, ...), custom_call_target="tpu_custom_call" | custom-call | flops 2415919104 | bytes 8053063 | tf_op jit(solution)/shard_map/products_near/pallas_call | solution.py:664
  330.4 9.7 %products_held.2 = (bf16[768,1536]{1,0:T(8,128)(2,1)}, bf16[768,384]{1,0:T(8,128)(2,1)}) custom-call(s32[1]{0:T(128)} %bitcast.7.side_ref, bf16[1024,768]{1,0:T(8,128)(2,1)} %get-tuple-element.131.refs_0_, bf16[1024,3072]{1,0:T(8,128)(2,1)} %get-tuple-element.132.refs_1_, bf16[768,1536]{1,0:T(8,128)(2,1)} %copy-done.34, ...), custom_call_target="tpu_custom_call" | custom-call | flops 3019898880 | bytes 10066329 | tf_op jit(solution)/shard_map/products_held/pallas_call | solution.py:664
  340.1 13.9 %attend_back.4 = (bf16[2,512,768]{2,1,0:T(8,128)(2,1)}, bf16[1024,768]{1,0:T(8,128)(2,1)}, bf16[1024,768]{1,0:T(8,128)(2,1)}, bf16[12,512,1024]{2,1,0:T(8,128)(2,1)}) custom-call(s32[2,4]{1,0:T(2,128)} %get-tuple-element.99.window_ref, bf16[2,512,768]{2,1,0:T(8,128)(2,1)} %bitcast.203, bf16[1024,768]{1,0:T(8,128)(2,1)} %convolution_convert_fusion.1.k_ref.refs_1_, ...), custom_call_target="tpu_custom_call" | custom-call | flops 6442450944 | bytes 25165824 | tf_op jit(solution)/shard_map/attend_back/pallas_call | solution.py:334
  354.0 14.1 %attend_back.5 = (bf16[2,512,768]{2,1,0:T(8,128)(2,1)}, bf16[1024,768]{1,0:T(8,128)(2,1)}, bf16[1024,768]{1,0:T(8,128)(2,1)}, bf16[12,512,1024]{2,1,0:T(8,128)(2,1)}) custom-call(s32[2,4]{1,0:T(2,128)} %get-tuple-element.99.window_ref, bf16[2,512,768]{2,1,0:T(8,128)(2,1)} %bitcast.204, ...), custom_call_target="tpu_custom_call", output_to_operand_aliasing={{0}: (7, {}), {1}: (8, {}), {2}: (9, {}), {3}: (10, {})} | custom-call | flops 6442450944 | bytes 25165824 | tf_op jit(solution)/shard_map/attend_back/pallas_call | solution.py:334
  386.1 8.8 %products_attn.2.refs_14_.refs_19_ = bf16[768,2304]{1,0:T(8,128)(2,1)} custom-call(s32[1]{0:T(128)} %bitcast.7.side_ref, bf16[1024,768]{1,0:T(8,128)(2,1)} %get-tuple-element.118.refs_2_.refs_0_, bf16[1024,768]{1,0:T(8,128)(2,1)} %bitcast.223, bf16[1024,768]{1,0:T(8,128)(2,1)} %copy-done.25, bf16[1024,768]{1,0:T(8,128)(2,1)} %get-tuple-element.146.refs_3_, ...), custom_call_target="tpu_custom_call" | custom-call | flops 3623878656 | bytes 12079595 | tf_op jit(solution)/shard_map/products_attn/pallas_call | solution.py:664
  394.9 14.4 %layer_tail_back.4 = (bf16[1024,768]{1,0:T(8,128)(2,1)}, bf16[1024,3072]{1,0:T(8,128)(2,1)}, f32[1024,768]{1,0:T(8,128)}, bf16[1024,768]{1,0:T(8,128)(2,1)}, bf1...) custom-call(f32[512,768]{1,0:T(8,128)} %slice.269.refs_0_, f32[1024,768]{1,0:T(8,128)} %get-tuple-element.117.refs_0_.refs_1_, ...), custom_call_target="tpu_custom_call" | custom-call | flops 5435817984 | bytes 37748736 | tf_op jit(solution)/shard_map/layer_tail_back/pallas_call | solution.py:573
  413.3 14.3 %layer_tail_back.5 = (bf16[1024,768]{1,0:T(8,128)(2,1)}, bf16[1024,3072]{1,0:T(8,128)(2,1)}, f32[1024,768]{1,0:T(8,128)}, bf16[1024,768]{1,0:T(8,128)(2,1)}, bf1...) custom-call(f32[512,768]{1,0:T(8,128)} %fusion.3.refs_0_, ...), custom_call_target="tpu_custom_call", output_to_operand_aliasing={{0}: (14, {}), {1}: (15, {}), {2}: (16, {}), {3}: (17, {}),... | custom-call | flops 5435817984 | bytes 37748736 | tf_op jit(solution)/shard_map/layer_tail_back/pallas_call | solution.py:573
  427.7 12.7 %products_sent.3 = (bf16[768,1536]{1,0:T(8,128)(2,1)}, bf16[768,1536]{1,0:T(8,128)(2,1)}, bf16[768,384]{1,0:T(8,128)(2,1)}) custom-call(s32[1]{0:T(128)} %bitcast.7.side_ref, bf16[1024,768]{1,0:T(8,128)(2,1)} %get-tuple-element.162.refs_0_, bf16[1024,3072]{1,0:T(8,128)(2,1)} %get-tuple-element.163.refs_1_, ...), custom_call_target="tpu_custom_call" | custom-call | flops 5435817984 | bytes 18119392 | tf_op jit(solution)/shard_map/products_sent/pallas_call | solution.py:664
  445.3 7.6 %products_near.3.refs_8_ = bf16[768,1536]{1,0:T(8,128)(2,1)} custom-call(s32[1]{0:T(128)} %bitcast.7.side_ref, bf16[1024,768]{1,0:T(8,128)(2,1)} %get-tuple-element.162.refs_0_, bf16[1024,3072]{1,0:T(8,128)(2,1)} %get-tuple-element.163.refs_1_, bf16[768,1536]{1,0:T(8,128)(2,1)} %collective-permute-done.25.refs_2_, ...), custom_call_target="tpu_custom_call" | custom-call | flops 2415919104 | bytes 8053063 | tf_op jit(solution)/shard_map/products_near/pallas_call | solution.py:664
  455.8 9.3 %products_held.3 = (bf16[768,1536]{1,0:T(8,128)(2,1)}, bf16[768,384]{1,0:T(8,128)(2,1)}) custom-call(s32[1]{0:T(128)} %bitcast.7.side_ref, bf16[1024,768]{1,0:T(8,128)(2,1)} %get-tuple-element.162.refs_0_, bf16[1024,3072]{1,0:T(8,128)(2,1)} %get-tuple-element.163.refs_1_, bf16[768,1536]{1,0:T(8,128)(2,1)} %collective-permute-done.23.refs_2_, ...), custom_call_target="tpu_custom_call" | custom-call | flops 3019898880 | bytes 10066329 | tf_op jit(solution)/shard_map/products_held/pallas_call | solution.py:664
  465.0 14.3 %attend_back.6 = (bf16[2,512,768]{2,1,0:T(8,128)(2,1)}, bf16[1024,768]{1,0:T(8,128)(2,1)}, bf16[1024,768]{1,0:T(8,128)(2,1)}, bf16[12,512,1024]{2,1,0:T(8,128)(2,1)}) custom-call(s32[2,4]{1,0:T(2,128)} %get-tuple-element.99.window_ref, bf16[2,512,768]{2,1,0:T(8,128)(2,1)} %bitcast.212, bf16[1024,768]{1,0:T(8,128)(2,1)} %convolution_convert_fusion.4.k_ref.refs_1_, ...), custom_call_target="tpu_custom_call" | custom-call | flops 6442450944 | bytes 25165824 | tf_op jit(solution)/shard_map/attend_back/pallas_call | solution.py:334
  482.3 6.0 collective-permute-start.39
  488.8 14.2 %attend_back.7 = (bf16[2,512,768]{2,1,0:T(8,128)(2,1)}, bf16[1024,768]{1,0:T(8,128)(2,1)}, bf16[1024,768]{1,0:T(8,128)(2,1)}, bf16[12,512,1024]{2,1,0:T(8,128)(2,1)}) custom-call(s32[2,4]{1,0:T(2,128)} %get-tuple-element.99.window_ref, bf16[2,512,768]{2,1,0:T(8,128)(2,1)} %bitcast.213, ...), custom_call_target="tpu_custom_call", output_to_operand_aliasing={{0}: (7, {}), {1}: (8, {}), {2}: (9, {}), {3}: (10, {})} | custom-call | flops 6442450944 | bytes 25165824 | tf_op jit(solution)/shard_map/attend_back/pallas_call | solution.py:334
  510.7 8.8 %products_attn.3.refs_1_ = bf16[768,2304]{1,0:T(8,128)(2,1)} custom-call(s32[1]{0:T(128)} %bitcast.7.side_ref, bf16[1024,768]{1,0:T(8,128)(2,1)} %get-tuple-element.98.refs_0_, bf16[1024,768]{1,0:T(8,128)(2,1)} %bitcast.205, bf16[1024,768]{1,0:T(8,128)(2,1)} %add_convert_fusion.5.refs_2_, bf16[1024,768]{1,0:T(8,128)(2,1)} %get-tuple-element.177.refs_3_.refs_0_, ...), custom_call_target="tpu_custom_call" | custom-call | flops 3623878656 | bytes 12079595 | tf_op jit(solution)/shard_map/products_attn/pallas_call | solution.py:664
  539.2 19.6 %collective-permute-done.29.refs_0_ = bf16[4,96,1920]{2,1,0:T(8,128)(2,1)} collective-permute-done((bf16[4,96,1920]{2,1,0:T(8,128)(2,1)}, bf16[4,96,1920]{2,1,0:T(8,128)(2,1)}, u32[]{:S(2)}, u32[]{:S(2)}) %collective-permute-start.29) | collective-permute-done | bytes 1474592 | tf_op jit(solution)/shard_map/ppermute | solution.py:764
  566.2 12.0 %table_sums.1 = f32[256,96]{1,0:T(8,128)} custom-call(s32[2,4]{1,0:T(2,128)} %get-tuple-element.99.window_ref, s32[512,1]{1,0:T(8,128)} %get-tuple-element.100.place_ref, bf16[12,512,1024]{2,1,0:T(8,128)(2,1)} %get-tuple-element.179.refs_0_, bf16[12,512,1024]{2,1,0:T(8,128)(2,1)} %get-tuple-element.180.refs_1_, ...), custom_call_target="tpu_custom_call" | custom-call | flops 3221225472 | bytes 25165824 | tf_op jit(solution)/shard_map/table_sums/pallas_call | solution.py:399
  594.5 5.6 collective-permute-start.34
  615.2 10.1 %collective-permute-done.47 = f32[20,768]{1,0:T(8,128)S(1)} collective-permute-done((f32[20,768]{1,0:T(8,128)S(1)}, f32[20,768]{1,0:T(8,128)S(1)}, u32[]{:S(2)}, u32[]{:S(2)}) %collective-permute-start.47) | collective-permute-done | bytes 61472 | tf_op jit(solution)/shard_map/ppermute | solution.py:835
  633.5 9.5 %collective-permute-done.48 = f32[20,768]{1,0:T(8,128)S(1)} collective-permute-done((f32[20,768]{1,0:T(8,128)S(1)}, f32[20,768]{1,0:T(8,128)S(1)}, u32[]{:S(2)}, u32[]{:S(2)}) %collective-permute-start.48) | collective-permute-done | bytes 61472 | tf_op jit(solution)/shard_map/ppermute | solution.py:835
  662.6 5.4 collective-permute-done.42
  (361 shorter events, 232.7 us)
Async XLA Ops:
  7.2 93.6 %all-gather.6.cloned.1.call-start = ((), (), s32[]{:S(2)}) async-start(), calls=%async_computation.5 | async-start | bytes 3760128 | tf_op jit(solution)/shard_map/all_gather | solution.py:770
  9.1 148.1 %all-gather.4.cloned.1.call-start = ((), (), s32[]{:S(2)}) async-start(), calls=%async_computation.2 | async-start | bytes 6266880 | tf_op jit(solution)/shard_map/all_gather | solution.py:770
  10.9 583.2 %reduce-scatter.5.cloned.1.call-start = ((), (), s32[]{:S(2)}) async-start(), calls=%async_computation.4 | async-start | bytes 3760128 | tf_op jit(solution)/shard_map/reduce_scatter | solution.py:843
  15.4 35.0 %collective-permute-start.1 = (bf16[96,1536]{1,0:T(8,128)(2,1)}, bf16[96,1536]{1,0:T(8,128)(2,1)S(1)}, u32[]{:S(2)}, u32[]{:S(2)}) collective-permute-start(bf16[96,1536]{1,0:T(8,128)(2,1)} %bitcast.230), channel_id=1, source_target_pairs={{0,4},{1,5},{2,6},{3,7},{4,8},{5,9},{6,10},{7,11},{8,12},{9,13},{1... | collective-permute-start | bytes 884744 | tf_op jit(solution)/shard_map/ppermute | solution.py:767
  18.1 32.4 %collective-permute-start.2 = (bf16[96,1536]{1,0:T(8,128)(2,1)}, bf16[96,1536]{1,0:T(8,128)(2,1)S(1)}, u32[]{:S(2)}, u32[]{:S(2)}) collective-permute-start(bf16[96,1536]{1,0:T(8,128)(2,1)} %bitcast.231), channel_id=1, source_target_pairs={{0,8},{1,9},{2,10},{3,11},{4,12},{5,13},{6,14},{7,15},{8,0},{9,1},... | collective-permute-start | bytes 884744 | tf_op jit(solution)/shard_map/ppermute | solution.py:767
  20.7 29.8 %collective-permute-start.3 = (bf16[96,1536]{1,0:T(8,128)(2,1)}, bf16[96,1536]{1,0:T(8,128)(2,1)S(1)}, u32[]{:S(2)}, u32[]{:S(2)}) collective-permute-start(bf16[96,1536]{1,0:T(8,128)(2,1)} %bitcast.232), channel_id=1, source_target_pairs={{0,12},{1,13},{2,14},{3,15},{4,0},{5,1},{6,2},{7,3},{8,4},{9,5},{1... | collective-permute-start | bytes 884744 | tf_op jit(solution)/shard_map/ppermute | solution.py:767
  54.3 36.9 %collective-permute-start.4 = (bf16[4,96,1536]{2,1,0:T(8,128)(2,1)}, bf16[4,96,1536]{2,1,0:T(8,128)(2,1)S(1)}, u32[]{:S(2)}, u32[]{:S(2)}) collective-permute-start(bf16[4,96,1536]{2,1,0:T(8,128)(2,1)} %line_rows.2.refs_0_.refs_2_), channel_id=1, source_target_pairs={{0,2},{1,3},{2,0},{3,1},{4,6},{5,7},{6,4},{7,5},{8,10},{9,11},{10,... | collective-permute-start | bytes 3538952 | tf_op jit(solution)/shard_map/ppermute | solution.py:764
  56.1 40.8 %collective-permute-start.5 = (bf16[512,768]{1,0:T(8,128)(2,1)S(1)}, bf16[512,768]{1,0:T(8,128)(2,1)S(1)}, u32[]{:S(2)}, u32[]{:S(2)}) collective-permute-start(bf16[512,768]{1,0:T(8,128)(2,1)S(1)} %slice.205), channel_id=1, source_target_pairs={{0,16},{16,0},{1,17},{17,1},{2,18},{18,2},{3,19},{19,3},{4,20},{20... | collective-permute-start | bytes 2359304 | tf_op jit(solution)/shard_map/ppermute | solution.py:759
  63.9 76.0 %collective-permute-start.9 = (bf16[96,1536]{1,0:T(8,128)(2,1)}, bf16[96,1536]{1,0:T(8,128)(2,1)S(1)}, u32[]{:S(2)}, u32[]{:S(2)}) collective-permute-start(bf16[96,1536]{1,0:T(8,128)(2,1)} %bitcast.236), channel_id=1, source_target_pairs={{0,4},{1,5},{2,6},{3,7},{4,8},{5,9},{6,10},{7,11},{8,12},{9,13},{1... | collective-permute-start | bytes 884744 | tf_op jit(solution)/shard_map/ppermute | solution.py:767
  66.2 73.7 %collective-permute-start.10 = (bf16[96,1536]{1,0:T(8,128)(2,1)}, bf16[96,1536]{1,0:T(8,128)(2,1)S(1)}, u32[]{:S(2)}, u32[]{:S(2)}) collective-permute-start(bf16[96,1536]{1,0:T(8,128)(2,1)} %bitcast.237), channel_id=1, source_target_pairs={{0,8},{1,9},{2,10},{3,11},{4,12},{5,13},{6,14},{7,15},{8,0},{9,1},... | collective-permute-start | bytes 884744 | tf_op jit(solution)/shard_map/ppermute | solution.py:767
  67.2 72.7 %collective-permute-start.11 = (bf16[96,1536]{1,0:T(8,128)(2,1)}, bf16[96,1536]{1,0:T(8,128)(2,1)}, u32[]{:S(2)}, u32[]{:S(2)}) collective-permute-start(bf16[96,1536]{1,0:T(8,128)(2,1)} %bitcast.238), channel_id=1, source_target_pairs={{0,12},{1,13},{2,14},{3,15},{4,0},{5,1},{6,2},{7,3},{8,4},{9,5},{1... | collective-permute-start | bytes 884744 | tf_op jit(solution)/shard_map/ppermute | solution.py:767
  95.4 53.4 %collective-permute-start.8 = (bf16[768,1536]{1,0:T(8,128)(2,1)}, bf16[768,1536]{1,0:T(8,128)(2,1)}, u32[]{:S(2)}, u32[]{:S(2)}) collective-permute-start(bf16[768,1536]{1,0:T(8,128)(2,1)} %bitcast.185), channel_id=1, source_target_pairs={{0,16},{16,0},{1,17},{17,1},{2,18},{18,2},{3,19},{19,3},{4,20},{20... | collective-permute-start | bytes 7077896 | tf_op jit(solution)/shard_map/ppermute | solution.py:759
  100.8 49.6 %collective-permute-start.7 = (bf16[768,1536]{1,0:T(8,128)(2,1)S(1)}, bf16[768,1536]{1,0:T(8,128)(2,1)}, u32[]{:S(2)}, u32[]{:S(2)}) collective-permute-start(bf16[768,1536]{1,0:T(8,128)(2,1)S(1)} %bitcast.192), channel_id=1, source_target_pairs={{0,1},{1,0},{2,3},{3,2},{4,5},{5,4},{6,7},{7,6},{8,9},{9,8},{10,11... | collective-permute-start | bytes 7077896 | tf_op jit(solution)/shard_map/ppermute | solution.py:756
  150.1 43.7 %collective-permute-start.14 = (bf16[4,96,1536]{2,1,0:T(8,128)(2,1)S(1)}, bf16[4,96,1536]{2,1,0:T(8,128)(2,1)}, u32[]{:S(2)}, u32[]{:S(2)}) collective-permute-start(bf16[4,96,1536]{2,1,0:T(8,128)(2,1)S(1)} %copy-done.9), channel_id=1, source_target_pairs={{0,2},{1,3},{2,0},{3,1},{4,6},{5,7},{6,4},{7,5},{8,10},{9,11},{10,... | collective-permute-start | bytes 3538952 | tf_op jit(solution)/shard_map/ppermute | solution.py:764
  173.6 24.1 %collective-permute-start.13 = (bf16[512,768]{1,0:T(8,128)(2,1)}, bf16[512,768]{1,0:T(8,128)(2,1)}, u32[]{:S(2)}, u32[]{:S(2)}) collective-permute-start(bf16[512,768]{1,0:T(8,128)(2,1)} %slice.217), channel_id=1, source_target_pairs={{0,16},{16,0},{1,17},{17,1},{2,18},{18,2},{3,19},{19,3},{4,20},{20... | collective-permute-start | bytes 2359304 | tf_op jit(solution)/shard_map/ppermute | solution.py:759
  197.1 53.4 %collective-permute-start.16 = (bf16[768,1536]{1,0:T(8,128)(2,1)}, bf16[768,1536]{1,0:T(8,128)(2,1)}, u32[]{:S(2)}, u32[]{:S(2)}) collective-permute-start(bf16[768,1536]{1,0:T(8,128)(2,1)} %bitcast.216), channel_id=1, source_target_pairs={{0,16},{16,0},{1,17},{17,1},{2,18},{18,2},{3,19},{19,3},{4,20},{20... | collective-permute-start | bytes 7077896 | tf_op jit(solution)/shard_map/ppermute | solution.py:759
  197.7 52.9 %collective-permute-start.15 = (bf16[768,1536]{1,0:T(8,128)(2,1)}, bf16[768,1536]{1,0:T(8,128)(2,1)}, u32[]{:S(2)}, u32[]{:S(2)}) collective-permute-start(bf16[768,1536]{1,0:T(8,128)(2,1)} %bitcast.217), channel_id=1, source_target_pairs={{0,1},{1,0},{2,3},{3,2},{4,5},{5,4},{6,7},{7,6},{8,9},{9,8},{10,11... | collective-permute-start | bytes 7077896 | tf_op jit(solution)/shard_map/ppermute | solution.py:756
  327.6 54.4 %collective-permute-start.22 = (bf16[768,1536]{1,0:T(8,128)(2,1)}, bf16[768,1536]{1,0:T(8,128)(2,1)}, u32[]{:S(2)}, u32[]{:S(2)}) collective-permute-start(bf16[768,1536]{1,0:T(8,128)(2,1)} %products_near.2.refs_8_), channel_id=1, source_target_pairs={{0,16},{16,0},{1,17},{17,1},{2,18},{18,2},{3,19},{19,3},{4,20},{20... | collective-permute-start | bytes 7077896 | tf_op jit(solution)/shard_map/ppermute | solution.py:759
  374.5 34.8 %collective-permute-start.21 = (bf16[512,768]{1,0:T(8,128)(2,1)}, bf16[512,768]{1,0:T(8,128)(2,1)}, u32[]{:S(2)}, u32[]{:S(2)}) collective-permute-start(bf16[512,768]{1,0:T(8,128)(2,1)} %convolution_convert_fusion.7.refs_5_), channel_id=1, source_target_pairs={{0,16},{16,0},{1,17},{17,1},{2,18},{18,2},{3,19},{19,3},{4,20},{20... | collective-permute-start | bytes 2359304 | tf_op jit(solution)/shard_map/ppermute | solution.py:759
  442.3 37.1 %collective-permute-start.26 = (bf16[4,96,1920]{2,1,0:T(8,128)(2,1)}, bf16[4,96,1920]{2,1,0:T(8,128)(2,1)}, u32[]{:S(2)}, u32[]{:S(2)}) collective-permute-start(bf16[4,96,1920]{2,1,0:T(8,128)(2,1)} %dynamic-slice_bitcast_fusion.1), channel_id=1, source_target_pairs={{0,2},{1,3},{2,0},{3,1},{4,6},{5,7},{6,4},{7,5},{8,10},{9,11},{10,... | collective-permute-start | bytes 4423688 | tf_op jit(solution)/shard_map/ppermute | solution.py:764
  453.0 53.6 %collective-permute-start.27 = (bf16[768,1536]{1,0:T(8,128)(2,1)}, bf16[768,1536]{1,0:T(8,128)(2,1)}, u32[]{:S(2)}, u32[]{:S(2)}) collective-permute-start(bf16[768,1536]{1,0:T(8,128)(2,1)} %products_near.3.refs_8_), channel_id=1, source_target_pairs={{0,16},{16,0},{1,17},{17,1},{2,18},{18,2},{3,19},{19,3},{4,20},{20... | collective-permute-start | bytes 7077896 | tf_op jit(solution)/shard_map/ppermute | solution.py:759
  455.0 193.2 %reduce-scatter.3.cloned.1.call-start = ((), (), s32[]{:S(2)}) async-start(), calls=%async_computation.3 | async-start | bytes 3760128 | tf_op jit(solution)/shard_map/reduce_scatter | solution.py:843
  482.3 108.8 %collective-permute-start.39 = (bf16[96,1920]{1,0:T(8,128)(2,1)}, bf16[96,1920]{1,0:T(8,128)(2,1)}, u32[]{:S(2)}, u32[]{:S(2)}) collective-permute-start(bf16[96,1920]{1,0:T(8,128)(2,1)} %get-tuple-element.209), channel_id=1, source_target_pairs={{0,12},{1,13},{2,14},{3,15},{4,0},{5,1},{6,2},{7,3},{8,4},{9,5},{1... | collective-permute-start | bytes 1105928 | tf_op jit(solution)/shard_map/ppermute | solution.py:767
  488.3 102.8 %collective-permute-start.38 = (bf16[96,1920]{1,0:T(8,128)(2,1)}, bf16[96,1920]{1,0:T(8,128)(2,1)}, u32[]{:S(2)}, u32[]{:S(2)}) collective-permute-start(bf16[96,1920]{1,0:T(8,128)(2,1)} %get-tuple-element.210), channel_id=1, source_target_pairs={{0,8},{1,9},{2,10},{3,11},{4,12},{5,13},{6,14},{7,15},{8,0},{9,1},... | collective-permute-start | bytes 1105928 | tf_op jit(solution)/shard_map/ppermute | solution.py:767
  488.3 102.8 %collective-permute-start.37 = (bf16[96,1920]{1,0:T(8,128)(2,1)}, bf16[96,1920]{1,0:T(8,128)(2,1)}, u32[]{:S(2)}, u32[]{:S(2)}) collective-permute-start(bf16[96,1920]{1,0:T(8,128)(2,1)} %get-tuple-element.208), channel_id=1, source_target_pairs={{0,4},{1,5},{2,6},{3,7},{4,8},{5,9},{6,10},{7,11},{8,12},{9,13},{1... | collective-permute-start | bytes 1105928 | tf_op jit(solution)/shard_map/ppermute | solution.py:767
  522.6 36.2 %collective-permute-start.29 = (bf16[4,96,1920]{2,1,0:T(8,128)(2,1)}, bf16[4,96,1920]{2,1,0:T(8,128)(2,1)}, u32[]{:S(2)}, u32[]{:S(2)}) collective-permute-start(bf16[4,96,1920]{2,1,0:T(8,128)(2,1)} %dynamic-slice_bitcast_fusion), channel_id=1, source_target_pairs={{0,2},{1,3},{2,0},{3,1},{4,6},{5,7},{6,4},{7,5},{8,10},{9,11},{10,... | collective-permute-start | bytes 4423688 | tf_op jit(solution)/shard_map/ppermute | solution.py:764
  529.5 54.2 %collective-permute-start.28 = (bf16[512,768]{1,0:T(8,128)(2,1)}, bf16[512,768]{1,0:T(8,128)(2,1)}, u32[]{:S(2)}, u32[]{:S(2)}) collective-permute-start(bf16[512,768]{1,0:T(8,128)(2,1)} %convolution_convert_fusion.6.refs_2_), channel_id=1, source_target_pairs={{0,16},{16,0},{1,17},{17,1},{2,18},{18,2},{3,19},{19,3},{4,20},{20... | collective-permute-start | bytes 2359304 | tf_op jit(solution)/shard_map/ppermute | solution.py:759
  594.5 50.4 %collective-permute-start.34 = (bf16[96,1920]{1,0:T(8,128)(2,1)S(1)}, bf16[96,1920]{1,0:T(8,128)(2,1)}, u32[]{:S(2)}, u32[]{:S(2)}) collective-permute-start(bf16[96,1920]{1,0:T(8,128)(2,1)S(1)} %get-tuple-element.206), channel_id=1, source_target_pairs={{0,12},{1,13},{2,14},{3,15},{4,0},{5,1},{6,2},{7,3},{8,4},{9,5},{1... | collective-permute-start | bytes 1105928 | tf_op jit(solution)/shard_map/ppermute | solution.py:767
  600.1 44.8 %collective-permute-start.33 = (bf16[96,1920]{1,0:T(8,128)(2,1)S(1)}, bf16[96,1920]{1,0:T(8,128)(2,1)}, u32[]{:S(2)}, u32[]{:S(2)}) collective-permute-start(bf16[96,1920]{1,0:T(8,128)(2,1)S(1)} %get-tuple-element.207), channel_id=1, source_target_pairs={{0,8},{1,9},{2,10},{3,11},{4,12},{5,13},{6,14},{7,15},{8,0},{9,1},... | collective-permute-start | bytes 1105928 | tf_op jit(solution)/shard_map/ppermute | solution.py:767
  600.1 44.1 %collective-permute-start.32 = (bf16[96,1920]{1,0:T(8,128)(2,1)}, bf16[96,1920]{1,0:T(8,128)(2,1)S(1)}, u32[]{:S(2)}, u32[]{:S(2)}) collective-permute-start(bf16[96,1920]{1,0:T(8,128)(2,1)} %get-tuple-element.205), channel_id=1, source_target_pairs={{0,4},{1,5},{2,6},{3,7},{4,8},{5,9},{6,10},{7,11},{8,12},{9,13},{1... | collective-permute-start | bytes 1105928 | tf_op jit(solution)/shard_map/ppermute | solution.py:767
  611.2 19.5 %collective-permute-start.41 = (bf16[48,1920]{1,0:T(8,128)(2,1)S(1)}, bf16[48,1920]{1,0:T(8,128)(2,1)S(1)}, u32[]{:S(2)}, u32[]{:S(2)}) collective-permute-start(bf16[48,1920]{1,0:T(8,128)(2,1)S(1)} %fusion.37), channel_id=1, source_target_pairs={{0,1},{1,0},{2,3},{3,2},{4,5},{5,4},{6,7},{7,6},{8,9},{9,8},{10,11... | collective-permute-start | bytes 552968 | tf_op jit(solution)/shard_map/ppermute | solution.py:756
  625.4 17.6 %collective-permute-start.48 = (f32[20,768]{1,0:T(8,128)S(1)}, f32[20,768]{1,0:T(8,128)S(1)}, u32[]{:S(2)}, u32[]{:S(2)}) collective-permute-start(f32[20,768]{1,0:T(8,128)S(1)} %add.285), channel_id=1, source_target_pairs={{0,8},{1,9},{2,10},{3,11},{4,12},{5,13},{6,14},{7,15},{8,0},{9,1},... | collective-permute-start | bytes 184328 | tf_op jit(solution)/shard_map/ppermute | solution.py:835
  (83 other events, 472.8 us)
Sparse Core Ops, SparseCore 0:
  10.3 82.2 all-gather.5
  95.5 61.6 all-gather.3
  455.2 93.1 reduce-scatter.4
  552.1 86.7 reduce-scatter.2

commit v3 on v2

--- a/solution.py
+++ b/solution.py
@@ -173,10 +173,9 @@
             choice = jnp.where(seen, bucket_of(key_place - place), 32)
             for head in range(head_count):
                 line = jnp.broadcast_to(table_ref[head : head + 1, :], (8, 128))
-                for row in range(0, rows, 8):
-                    out_ref[head, row : row + 8, first : first + 128] = jnp.take_along_axis(
-                        line, choice[row : row + 8], axis=1
-                    )
+                for row in range(0, rows, 16):
+                    taken = [jnp.take_along_axis(line, choice[at : at + 8], axis=1) for at in (row, row + 8)]
+                    out_ref[head, row : row + 16, first : first + 128] = jnp.concatenate(taken, axis=0).astype(LOW)
 
 
 def bias_call(window, table_rows, place, doc, rank, key_doc, key_rank, *waits):
@@ -199,7 +198,7 @@
         ]
         + [pl.BlockSpec(memory_space=pl.ANY)] * len(waits),
         out_specs=pl.BlockSpec((head_count, tile, length), lambda i: (0, i, 0)),
-        out_shape=jax.ShapeDtypeStruct((head_count, rows, length), F32),
+        out_shape=jax.ShapeDtypeStruct((head_count, rows, length), LOW),
         compiler_params=pltpu.CompilerParams(vmem_limit_bytes=VMEM_LIMIT),
         cost_estimate=pl.CostEstimate(
             flops=0, bytes_accessed=head_count * rows * length * 8, transcendentals=0
@@ -226,7 +225,7 @@
         raw = [dot_nt(mine[head], k_ref[columns, head // 2 * 128 : head // 2 * 128 + 128]) for head in heads]
         scores = []
         for head in heads:
-            bias = bias_ref[head, lines, columns]
+            bias = bias_ref[head, lines, columns].astype(F32)
             scores.append((raw[head][:tile] + bias, jnp.where(hidden, MASKED, raw[head][tile:] + bias)))
         most = [[jnp.max(part, axis=1, keepdims=True) for part in pair] for pair in scores]
         weights = [[jnp.exp(part - top) for part, top in zip(pair, tops)] for pair, tops in zip(scores, most)]
@@ -769,17 +768,17 @@
     def gather(self, shard):
         return lax.all_gather(shard, "dp", axis=0, tiled=True)
 
-    def gather_chip(self, shards, waits):
-        rows, columns = shards[0].shape
+    def gather_chip(self, inner, outer, halves, waits):
+        rows, columns = inner.shape
         width = columns // 4
 
-        def quarter(core):
-            first = (2 * self.block_at + core) * width
-            parts = [lax.dynamic_slice_in_dim(shard, first, width, 1) for shard in shards]
-            return jnp.concatenate(parts, axis=1) if len(parts) > 1 else parts[0]
-
-        mine = quarter(self.core_at)
-        other = self.from_core(quarter(1 - self.core_at))
+        def chosen(core):
+            own, other = ((2 * block + core) * width for block in (self.block_at, 1 - self.block_at))
+            parts = ((inner, own), (outer, own), (outer, other))[: 3 if halves else 2]
+            return jnp.concatenate([lax.dynamic_slice_in_dim(shard, first, width, 1) for shard, first in parts], axis=1)
+
+        mine = chosen(self.core_at)
+        other = self.from_core(chosen(1 - self.core_at))
         chip = place_call("chip_rows", [mine, other], [self.core_at, 1 - self.core_at], waits)
         return chip.reshape(2 * rows, -1)
 
@@ -877,7 +876,7 @@
     layers = range(layer_count)
 
     def chip_of(layer_index, *waits):
-        return grid.gather_chip((ffn_in[layer_index], ffn_out_t[layer_index]), waits)
+        return grid.gather_chip(ffn_in[layer_index], ffn_out_t[layer_index], layer_index > 0, waits)
 
     chip = chip_of(0) if paired else None
     sides = jnp.stack([block_index, 1 - block_index]) if paired else (block_index + jnp.arange(blocks)) % blocks
@@ -947,9 +946,17 @@
             if more:
                 line = grid.gather_line(next_chip, (out_low,))
                 waits_near = (out_low, line)
-            near = hold(grid.from_block(sheet), *waits_near)
-            quarters = (sheet, grid.from_core(sheet), near, grid.from_core(near))
-            pieces = [((quarter, 0), (quarter, span)) for quarter in quarters]
+            beside = grid.from_core(sheet)
+            if layer_index > 0:
+                near = hold(grid.from_block(sheet[:, :span]), *waits_near)
+                outers = ((sheet, span), (beside, span), (sheet, 2 * span), (beside, 2 * span))
+            else:
+                near = hold(grid.from_block(sheet), *waits_near)
+            far = grid.from_core(near)
+            quarters = (sheet, beside, near, far)
+            if layer_index == 0:
+                outers = [(quarter, span) for quarter in quarters]
+            pieces = [((quarter, 0), outer) for quarter, outer in zip(quarters, outers)]
         else:
             pieces = [((grid.gather(ffn_in[layer_index]), 0), (grid.gather(ffn_out_t[layer_index]), 0))]
         all_pieces.append(pieces)
@@ -1102,18 +1109,20 @@
                     )
                 ],
                 {"attn": (width, 3 * width, width)},
-                [passed, ffn_sum] if layer_index > 0 else [ffn_sum],
+                [passed, ffn_sum] if layer_index > 0 else (),
             )["attn"]
             if layer_index == 0:
                 grad_q, grad_k, grad_v = (hold(tensor, attn) for tensor in (grad_q, grad_k, grad_v))
                 grad_all = keys_back(grad_k, grad_v, qkv)
-                ffn_low = grid.scatter_end(ffn_begun, grad_all)
+                before = [grad_all]
+                if "high_begun" in pending:
+                    upper = grid.scatter_end(pending["high_begun"], attn)
+                    before.append(upper)
+                ffn_low = grid.scatter_end(ffn_begun, *before)
                 ffn_begun = grid.high_begin(ffn_low)
                 passed = dot_nn(spreads[1], grad_all).astype(LOW)
             attn_part = grid.scatter_rows(attn)
             attn_parts[layer_index] = attn_part
-            if "high_begun" in pending:
-                upper = pending["high_begun"]
             if layer_index > 0:
                 pending = {"attn": attn, "sum": ffn_sum, "low_begun": grid.low_begin(ffn_sum)}
             else:
@@ -1152,7 +1161,7 @@
         come = hold(come, table_grad)
         ffn_high = grid.scatter_end(ffn_begun, table_grad)
         if layer_count > 1:
-            matrix_rows[1] = finish_rows(grid.scatter_end(upper, table_grad))
+            matrix_rows[1] = finish_rows(hold(upper, table_grad))
         matrix_rows[0] = finish_rows(hold(ffn_high, attn_part))
         attn_rows = [grid.scatter_end_blocks(hold(part, table_grad)) for part in attn_parts]
     grad_stream[0] = content_side(grad_stream[0], come)

time: 685 us -> 666 us (0.972)
  Pallas kernels: 346 us -> 332 us
  waiting for transfers between devices: 121 us -> 114 us
    ppermute x15, waiting for transfers between devices: 39.8 us -> 25.8 us  [from_block(): return lax.ppermute(tensor, 'blk', [(0, 1), (1, 0)])]
    ppermute x12, waiting for transfers between devices: 0.03 us -> 12.4 us  [from_high(): lax.ppermute(tensor, 'dp', [(i, (i + 2 * self.low * step) % self.total) f...]
    ppermute x4, waiting for transfers between devices: 40.7 us -> 29.8 us  [from_low(): return lax.ppermute(tensor, 'dp', pairs)]
    pallas_call x2, Pallas kernels: 58.7 us -> 48.5 us  [attend_call(): pl.pallas_call(attend_kernel, grid=(pairs // group,), in_specs=[pl.BlockS...]
    all_gather x2, waiting for transfers between devices: 3.53 us -> 12.8 us  [gather(): return lax.all_gather(shard, 'dp', axis=0, tiled=True)]
    unnamed x124 -> x120, local copies, waits for them, and re-layouts: 16.5 us -> 14.6 us
  transfers between devices with their start and end apart: 53 -> 53, of which waited for: 19 -> 21; matrix products, arithmetic and copies ran while one was open for 16% -> 17% of each run, Pallas kernels for 39% -> 38%
where the time goes in v3:
time: 666 us; the launch traced here: 660 us
  Pallas kernels  332 us (50%)
  waiting for transfers between devices  114 us (17%)
  matrix products  62.5 us (9%)
  starting transfers between devices  59.2 us (9%)
  local copies, waits for them, and re-layouts  41.7 us (6%)
  other arithmetic  35.6 us (5%)
  between operations  15.4 us (2%)
    pallas_call x8, Pallas kernels, products_call(): pl.pallas_call(functools.partial(product_kernel, plan), grid_spec=pltpu.P...  76.9 us
    pallas_call x4, Pallas kernels, attend_back_call(): pl.pallas_call(attend_back_kernel, grid=(pairs,), in_specs=[pl.BlockSpec(...  56 us
    pallas_call x3, Pallas kernels, layer_tail_call(): pl.pallas_call(functools.partial(layer_tail_kernel, len(pieces), plan, sp...  51.2 us
    pallas_call x3, Pallas kernels, layer_tail_back_call(): pl.pallas_call(functools.partial(layer_tail_back_kernel, len(pieces), pla...  50.8 us
    pallas_call x2, Pallas kernels, attend_call(): pl.pallas_call(attend_kernel, grid=(pairs // group,), in_specs=[pl.BlockS...  48.5 us
    dot_general x10, matrix products, dot_nn(): return jnp.dot(left_side, right_side, preferred_element_type=F32)  30.6 us
    ppermute x12, starting transfers between devices, from_high(): lax.ppermute(tensor, 'dp', [(i, (i + 2 * self.low * step) % self.total) f...  30.5 us
    ppermute x4, waiting for transfers between devices, from_low(): return lax.ppermute(tensor, 'dp', pairs)  29.8 us
  transfers between devices with their start and end apart: 53, of which 21 were waited for; matrix products, arithmetic and copies ran while one was open for 17% of the time, Pallas kernels for 38%

profile of v3, /device:TPU:0, one launch (start us, length us, event | category | flops | bytes accessed | tf_op | source)
XLA Modules:
  0.0 660.4 jit_solution(11912368826104739693)
XLA Ops:
  25.0 7.9 %setup_rows.1 = (s32[2,4]{1,0:T(2,128)}, s32[1,1024]{1,0:T(1,128)}, s32[1,1024]{1,0:T(1,128)}, s32[512,1]{1,0:T(8,128)}, s32[512,1]{1,0:T(8,128)}, /*index=5*/s3...) custom-call(s32[2]{0:T(128)} %pad_add_fusion.side_ref, ...), custom_call_target="tpu_custom_call" | custom-call | flops 1610612736 | bytes 6291456 | tf_op jit(solution)/shard_map/setup_rows/pallas_call | solution.py:141
  32.9 13.1 %bias_rows.1.refs_4_.bias_ref = bf16[12,512,1024]{2,1,0:T(8,128)(2,1)} custom-call(s32[2,4]{1,0:T(2,128)} %get-tuple-element.99.window_ref, f32[12,128]{1,0:T(8,128)} %concatenate.141.table_ref, s32[512,1]{1,0:T(8,128)} %get-tuple-element.100.place_ref, s32[512,1]{1,0:T(8,128)} %get-tuple-element.101.doc_ref, s32[512,1]{1,0:T(8,128)} %get-tuple-element.102.rank_ref, ...), custom_call_target="tpu_custom_call" | custom-call | bytes 50331648 | tf_op jit(solution)/shard_map/bias_rows/pallas_call | solution.py:187
  68.7 20.3 %collective-permute-done.4.refs_1_ = bf16[4,96,1536]{2,1,0:T(8,128)(2,1)S(1)} collective-permute-done((bf16[4,96,1536]{2,1,0:T(8,128)(2,1)}, bf16[4,96,1536]{2,1,0:T(8,128)(2,1)S(1)}, u32[]{:S(2)}, u32[]{:S(2)}) %collective-permute-start.4) | collective-permute-done | bytes 1179680 | tf_op jit(solution)/shard_map/ppermute | solution.py:763
  109.6 24.4 %attend.2 = (f32[2,512,768]{2,1,0:T(8,128)}, bf16[2,512,768]{2,1,0:T(8,128)(2,1)}, bf16[12,2,512,1024]{3,2,1,0:T(8,128)(2,1)}) custom-call(s32[2,4]{1,0:T(2,128)} %get-tuple-element.99.window_ref, bf16[2,512,768]{2,1,0:T(8,128)(2,1)} %bitcast.217, bf16[1024,768]{1,0:T(8,128)(2,1)} %convolution_convert_fusion.4.k_ref.refs_1_, ...), custom_call_target="tpu_custom_call" | custom-call | flops 6442450944 | bytes 50331648 | tf_op jit(solution)/shard_map/attend/pallas_call | solution.py:256
  136.8 9.0 %collective-permute-done.8.refs_0_ = bf16[768,1536]{1,0:T(8,128)(2,1)} collective-permute-done((bf16[768,1536]{1,0:T(8,128)(2,1)}, bf16[768,1536]{1,0:T(8,128)(2,1)}, u32[]{:S(2)}, u32[]{:S(2)}) %collective-permute-start.8) | collective-permute-done | bytes 2359328 | tf_op jit(solution)/shard_map/ppermute | solution.py:758
  150.8 11.4 %all-gather.4.cloned.1.call-done.refs_2_.refs_6_ = bf16[768,3840]{1,0:T(8,128)(2,1)} async-done(((bf16[48,3840]{1,0:T(8,128)(2,1)}), bf16[768,3840]{1,0:T(8,128)(2,1)}) %all-gather.4.cloned.1.call-update) | async-done | bytes 5898256 | tf_op jit(solution)/shard_map/all_gather | solution.py:769
  162.2 14.6 %layer_tail.3 = (f32[1024,768]{1,0:T(8,128)}, bf16[1024,768]{1,0:T(8,128)(2,1)}, f32[1024,768]{1,0:T(8,128)}, bf16[1024,768]{1,0:T(8,128)(2,1)}, bf16[1024,3072]...) custom-call(bf16[1024,768]{1,0:T(8,128)(2,1)} %get-tuple-element.98.refs_0_, ...), custom_call_target="tpu_custom_call" | custom-call | flops 5435817984 | bytes 31457280 | tf_op jit(solution)/shard_map/layer_tail/pallas_call | solution.py:492
  180.5 14.3 %layer_tail.4 = (f32[1024,768]{1,0:T(8,128)}, bf16[1024,768]{1,0:T(8,128)(2,1)}, f32[1024,768]{1,0:T(8,128)}, bf16[1024,768]{1,0:T(8,128)(2,1)}, bf16[1024,3072]...) custom-call(bf16[1024,768]{1,0:T(8,128)(2,1)} %get-tuple-element.98., ...), custom_call_target="tpu_custom_call", output_to_operand_aliasing={{0}: (9, {}), {1}: (10, {}), {2}: (11, {}), {3}: (12, {}), ... | custom-call | flops 5435817984 | bytes 31457280 | tf_op jit(solution)/shard_map/layer_tail/pallas_call | solution.py:492
  214.5 24.1 %attend.3 = (f32[2,512,768]{2,1,0:T(8,128)}, bf16[2,512,768]{2,1,0:T(8,128)(2,1)}, bf16[12,2,512,1024]{3,2,1,0:T(8,128)(2,1)}) custom-call(s32[2,4]{1,0:T(2,128)} %get-tuple-element.99.window_ref, bf16[2,512,768]{2,1,0:T(8,128)(2,1)} %bitcast.210, bf16[1024,768]{1,0:T(8,128)(2,1)} %convolution_convert_fusion.1.k_ref.refs_1_, ...), custom_call_target="tpu_custom_call" | custom-call | flops 6442450944 | bytes 50331648 | tf_op jit(solution)/shard_map/attend/pallas_call | solution.py:256
  242.7 22.2 %layer_tail.5 = (f32[1024,768]{1,0:T(8,128)}, bf16[1024,768]{1,0:T(8,128)(2,1)}, f32[1024,768]{1,0:T(8,128)}, bf16[1024,768]{1,0:T(8,128)(2,1)}, bf16[1024,3072]...) custom-call(f32[1024,768]{1,0:T(8,128)} %get-tuple-element.117.refs_0_.refs_1_, ...), custom_call_target="tpu_custom_call" | custom-call | flops 10871635968 | bytes 31457280 | tf_op jit(solution)/shard_map/layer_tail/pallas_call | solution.py:492
  265.6 22.0 %layer_tail_back.3 = (bf16[1024,768]{1,0:T(8,128)(2,1)}, bf16[1024,3072]{1,0:T(8,128)(2,1)}, f32[1024,768]{1,0:T(8,128)}, bf16[1024,768]{1,0:T(8,128)(2,1)}, bf1...) custom-call(bf16[1024,768]{1,0:T(8,128)(2,1)} %get-tuple-element.121.refs_0_, f32[1024,768]{1,0:T(8,128)} %get-tuple-element.122.refs_1_, ...), custom_call_target="tpu_custom_call" | custom-call | flops 10871635968 | bytes 37748736 | tf_op jit(solution)/shard_map/layer_tail_back/pallas_call | solution.py:572
  287.6 12.5 %products_sent.2 = (bf16[768,1536]{1,0:T(8,128)(2,1)}, bf16[768,1536]{1,0:T(8,128)(2,1)}, bf16[768,384]{1,0:T(8,128)(2,1)}) custom-call(s32[1]{0:T(128)} %bitcast.7.side_ref, bf16[1024,768]{1,0:T(8,128)(2,1)} %get-tuple-element.131.refs_0_, bf16[1024,3072]{1,0:T(8,128)(2,1)} %get-tuple-element.132.refs_1_, ...), custom_call_target="tpu_custom_call" | custom-call | flops 5435817984 | bytes 18119392 | tf_op jit(solution)/shard_map/products_sent/pallas_call | solution.py:663
  306.4 7.2 %products_near.2.refs_8_ = bf16[768,1536]{1,0:T(8,128)(2,1)} custom-call(s32[1]{0:T(128)} %bitcast.7.side_ref, bf16[1024,768]{1,0:T(8,128)(2,1)} %get-tuple-element.131.refs_0_, bf16[1024,3072]{1,0:T(8,128)(2,1)} %get-tuple-element.132.refs_1_, bf16[768,1536]{1,0:T(8,128)(2,1)} %copy-done.30, bf16[1024,768]{1,0:T(8,128)(2,1)} %get-tuple-element.133.refs_2_.refs_3_, ...), custom_call_target="tpu_custom_call" | custom-call | flops 2415919104 | bytes 8053063 | tf_op jit(solution)/shard_map/products_near/pallas_call | solution.py:663
  318.3 9.7 %products_held.2 = (bf16[768,1536]{1,0:T(8,128)(2,1)}, bf16[768,384]{1,0:T(8,128)(2,1)}) custom-call(s32[1]{0:T(128)} %bitcast.7.side_ref, bf16[1024,768]{1,0:T(8,128)(2,1)} %get-tuple-element.131.refs_0_, bf16[1024,3072]{1,0:T(8,128)(2,1)} %get-tuple-element.132.refs_1_, bf16[768,1536]{1,0:T(8,128)(2,1)} %copy-done.31, ...), custom_call_target="tpu_custom_call" | custom-call | flops 3019898880 | bytes 10066329 | tf_op jit(solution)/shard_map/products_held/pallas_call | solution.py:663
  327.9 13.9 %attend_back.4 = (bf16[2,512,768]{2,1,0:T(8,128)(2,1)}, bf16[1024,768]{1,0:T(8,128)(2,1)}, bf16[1024,768]{1,0:T(8,128)(2,1)}, bf16[12,512,1024]{2,1,0:T(8,128)(2,1)}) custom-call(s32[2,4]{1,0:T(2,128)} %get-tuple-element.99.window_ref, bf16[2,512,768]{2,1,0:T(8,128)(2,1)} %bitcast.211, bf16[1024,768]{1,0:T(8,128)(2,1)} %convolution_convert_fusion.1.k_ref.refs_1_, ...), custom_call_target="tpu_custom_call" | custom-call | flops 6442450944 | bytes 25165824 | tf_op jit(solution)/shard_map/attend_back/pallas_call | solution.py:333
  341.9 14.0 %attend_back.5 = (bf16[2,512,768]{2,1,0:T(8,128)(2,1)}, bf16[1024,768]{1,0:T(8,128)(2,1)}, bf16[1024,768]{1,0:T(8,128)(2,1)}, bf16[12,512,1024]{2,1,0:T(8,128)(2,1)}) custom-call(s32[2,4]{1,0:T(2,128)} %get-tuple-element.99.window_ref, bf16[2,512,768]{2,1,0:T(8,128)(2,1)} %bitcast.212, ...), custom_call_target="tpu_custom_call", output_to_operand_aliasing={{0}: (7, {}), {1}: (8, {}), {2}: (9, {}), {3}: (10, {})} | custom-call | flops 6442450944 | bytes 25165824 | tf_op jit(solution)/shard_map/attend_back/pallas_call | solution.py:333
  372.4 8.7 %products_attn.2.refs_14_.refs_19_ = bf16[768,2304]{1,0:T(8,128)(2,1)} custom-call(s32[1]{0:T(128)} %bitcast.7.side_ref, bf16[1024,768]{1,0:T(8,128)(2,1)} %get-tuple-element.118.refs_2_.refs_0_, bf16[1024,768]{1,0:T(8,128)(2,1)} %bitcast.222, bf16[1024,768]{1,0:T(8,128)(2,1)} %copy-done.23, bf16[1024,768]{1,0:T(8,128)(2,1)} %get-tuple-element.146.refs_3_, ...), custom_call_target="tpu_custom_call" | custom-call | flops 3623878656 | bytes 12079595 | tf_op jit(solution)/shard_map/products_attn/pallas_call | solution.py:663
  381.1 14.4 %layer_tail_back.4 = (bf16[1024,768]{1,0:T(8,128)(2,1)}, bf16[1024,3072]{1,0:T(8,128)(2,1)}, f32[1024,768]{1,0:T(8,128)}, bf16[1024,768]{1,0:T(8,128)(2,1)}, bf1...) custom-call(f32[512,768]{1,0:T(8,128)} %slice.274.refs_0_, f32[1024,768]{1,0:T(8,128)} %get-tuple-element.117.refs_0_.refs_1_, ...), custom_call_target="tpu_custom_call" | custom-call | flops 5435817984 | bytes 37748736 | tf_op jit(solution)/shard_map/layer_tail_back/pallas_call | solution.py:572
  399.6 14.3 %layer_tail_back.5 = (bf16[1024,768]{1,0:T(8,128)(2,1)}, bf16[1024,3072]{1,0:T(8,128)(2,1)}, f32[1024,768]{1,0:T(8,128)}, bf16[1024,768]{1,0:T(8,128)(2,1)}, bf1...) custom-call(f32[512,768]{1,0:T(8,128)} %fusion.3.refs_0_, ...), custom_call_target="tpu_custom_call", output_to_operand_aliasing={{0}: (14, {}), {1}: (15, {}), {2}: (16, {}), {3}: (17, {}),... | custom-call | flops 5435817984 | bytes 37748736 | tf_op jit(solution)/shard_map/layer_tail_back/pallas_call | solution.py:572
  414.0 12.6 %products_sent.3 = (bf16[768,1536]{1,0:T(8,128)(2,1)}, bf16[768,1536]{1,0:T(8,128)(2,1)}, bf16[768,384]{1,0:T(8,128)(2,1)}) custom-call(s32[1]{0:T(128)} %bitcast.7.side_ref, bf16[1024,768]{1,0:T(8,128)(2,1)} %get-tuple-element.162.refs_0_, bf16[1024,3072]{1,0:T(8,128)(2,1)} %get-tuple-element.163.refs_1_, ...), custom_call_target="tpu_custom_call" | custom-call | flops 5435817984 | bytes 18119392 | tf_op jit(solution)/shard_map/products_sent/pallas_call | solution.py:663
  433.7 7.7 %products_near.3.refs_8_ = bf16[768,1536]{1,0:T(8,128)(2,1)} custom-call(s32[1]{0:T(128)} %bitcast.7.side_ref, bf16[1024,768]{1,0:T(8,128)(2,1)} %get-tuple-element.162.refs_0_, bf16[1024,3072]{1,0:T(8,128)(2,1)} %get-tuple-element.163.refs_1_, bf16[768,1536]{1,0:T(8,128)(2,1)} %collective-permute-done.25.refs_2_, ...), custom_call_target="tpu_custom_call" | custom-call | flops 2415919104 | bytes 8053063 | tf_op jit(solution)/shard_map/products_near/pallas_call | solution.py:663
  442.5 9.7 %products_held.3 = (bf16[768,1536]{1,0:T(8,128)(2,1)}, bf16[768,384]{1,0:T(8,128)(2,1)}) custom-call(s32[1]{0:T(128)} %bitcast.7.side_ref, bf16[1024,768]{1,0:T(8,128)(2,1)} %get-tuple-element.162.refs_0_, bf16[1024,3072]{1,0:T(8,128)(2,1)} %get-tuple-element.163.refs_1_, bf16[768,1536]{1,0:T(8,128)(2,1)} %collective-permute-done.23.refs_2_, ...), custom_call_target="tpu_custom_call" | custom-call | flops 3019898880 | bytes 10066329 | tf_op jit(solution)/shard_map/products_held/pallas_call | solution.py:663
  452.2 14.0 %attend_back.6 = (bf16[2,512,768]{2,1,0:T(8,128)(2,1)}, bf16[1024,768]{1,0:T(8,128)(2,1)}, bf16[1024,768]{1,0:T(8,128)(2,1)}, bf16[12,512,1024]{2,1,0:T(8,128)(2,1)}) custom-call(s32[2,4]{1,0:T(2,128)} %get-tuple-element.99.window_ref, bf16[2,512,768]{2,1,0:T(8,128)(2,1)} %bitcast.218, bf16[1024,768]{1,0:T(8,128)(2,1)} %convolution_convert_fusion.4.k_ref.refs_1_, ...), custom_call_target="tpu_custom_call" | custom-call | flops 6442450944 | bytes 25165824 | tf_op jit(solution)/shard_map/attend_back/pallas_call | solution.py:333
  469.1 14.0 %attend_back.7 = (bf16[2,512,768]{2,1,0:T(8,128)(2,1)}, bf16[1024,768]{1,0:T(8,128)(2,1)}, bf16[1024,768]{1,0:T(8,128)(2,1)}, bf16[12,512,1024]{2,1,0:T(8,128)(2,1)}) custom-call(s32[2,4]{1,0:T(2,128)} %get-tuple-element.99.window_ref, bf16[2,512,768]{2,1,0:T(8,128)(2,1)} %bitcast.219, ...), custom_call_target="tpu_custom_call", output_to_operand_aliasing={{0}: (7, {}), {1}: (8, {}), {2}: (9, {}), {3}: (10, {})} | custom-call | flops 6442450944 | bytes 25165824 | tf_op jit(solution)/shard_map/attend_back/pallas_call | solution.py:333
  483.1 8.9 %products_attn.3.refs_1_ = bf16[768,2304]{1,0:T(8,128)(2,1)} custom-call(s32[1]{0:T(128)} %bitcast.7.side_ref, bf16[1024,768]{1,0:T(8,128)(2,1)} %get-tuple-element.98.refs_0_, bf16[1024,768]{1,0:T(8,128)(2,1)} %bitcast.213, bf16[1024,768]{1,0:T(8,128)(2,1)} %add_convert_fusion.5.refs_2_, bf16[1024,768]{1,0:T(8,128)(2,1)} %get-tuple-element.177.refs_3_.refs_0_, ...), custom_call_target="tpu_custom_call" | custom-call | flops 3623878656 | bytes 12079595 | tf_op jit(solution)/shard_map/products_attn/pallas_call | solution.py:663
  494.4 8.6 %collective-permute-start.32 = (bf16[96,1920]{1,0:T(8,128)(2,1)}, bf16[96,1920]{1,0:T(8,128)(2,1)}, u32[]{:S(2)}, u32[]{:S(2)}) collective-permute-start(bf16[96,1920]{1,0:T(8,128)(2,1)} %get-tuple-element.209), channel_id=1, source_target_pairs={{0,12},{1,13},{2,14},{3,15},{4,0},{5,1},{6,2},{7,3},{8,4},{9,5},{1... | collective-permute-start | bytes 1105928 | tf_op jit(solution)/shard_map/ppermute | solution.py:766
  528.4 7.3 %collective-permute-done.31 = bf16[96,1920]{1,0:T(8,128)(2,1)} collective-permute-done((bf16[96,1920]{1,0:T(8,128)(2,1)}, bf16[96,1920]{1,0:T(8,128)(2,1)}, u32[]{:S(2)}, u32[]{:S(2)}) %collective-permute-start.31) | collective-permute-done | bytes 368672 | tf_op jit(solution)/shard_map/ppermute | solution.py:766
  538.1 9.5 %collective-permute-done.29.refs_0_ = bf16[4,96,1920]{2,1,0:T(8,128)(2,1)} collective-permute-done((bf16[4,96,1920]{2,1,0:T(8,128)(2,1)}, bf16[4,96,1920]{2,1,0:T(8,128)(2,1)}, u32[]{:S(2)}, u32[]{:S(2)}) %collective-permute-start.29) | collective-permute-done | bytes 1474592 | tf_op jit(solution)/shard_map/ppermute | solution.py:763
  555.4 11.5 %table_sums.1 = f32[256,96]{1,0:T(8,128)} custom-call(s32[2,4]{1,0:T(2,128)} %get-tuple-element.99.window_ref, s32[512,1]{1,0:T(8,128)} %get-tuple-element.100.place_ref, bf16[12,512,1024]{2,1,0:T(8,128)(2,1)} %get-tuple-element.179.refs_0_, bf16[12,512,1024]{2,1,0:T(8,128)(2,1)} %get-tuple-element.180.refs_1_, ...), custom_call_target="tpu_custom_call" | custom-call | flops 3221225472 | bytes 25165824 | tf_op jit(solution)/shard_map/table_sums/pallas_call | solution.py:398
  603.5 10.8 %collective-permute-done.47 = f32[20,768]{1,0:T(8,128)S(1)} collective-permute-done((f32[20,768]{1,0:T(8,128)S(1)}, f32[20,768]{1,0:T(8,128)S(1)}, u32[]{:S(2)}, u32[]{:S(2)}) %collective-permute-start.47) | collective-permute-done | bytes 61472 | tf_op jit(solution)/shard_map/ppermute | solution.py:834
  617.3 8.2 %collective-permute-done.48 = f32[20,768]{1,0:T(8,128)S(1)} collective-permute-done((f32[20,768]{1,0:T(8,128)S(1)}, f32[20,768]{1,0:T(8,128)S(1)}, u32[]{:S(2)}, u32[]{:S(2)}) %collective-permute-start.48) | collective-permute-done | bytes 61472 | tf_op jit(solution)/shard_map/ppermute | solution.py:834
  644.5 6.5 collective-permute-done.42
  (359 shorter events, 237.5 us)
Async XLA Ops:
  7.2 92.9 %all-gather.6.cloned.1.call-start = ((), (), s32[]{:S(2)}) async-start(), calls=%async_computation.5 | async-start | bytes 3760128 | tf_op jit(solution)/shard_map/all_gather | solution.py:769
  9.1 153.1 %all-gather.4.cloned.1.call-start = ((), (), s32[]{:S(2)}) async-start(), calls=%async_computation.2 | async-start | bytes 6266880 | tf_op jit(solution)/shard_map/all_gather | solution.py:769
  10.9 573.4 %reduce-scatter.5.cloned.1.call-start = ((), (), s32[]{:S(2)}) async-start(), calls=%async_computation.4 | async-start | bytes 3760128 | tf_op jit(solution)/shard_map/reduce_scatter | solution.py:842
  15.5 30.5 %collective-permute-start.1 = (bf16[96,1536]{1,0:T(8,128)(2,1)}, bf16[96,1536]{1,0:T(8,128)(2,1)S(1)}, u32[]{:S(2)}, u32[]{:S(2)}) collective-permute-start(bf16[96,1536]{1,0:T(8,128)(2,1)} %bitcast.234), channel_id=1, source_target_pairs={{0,4},{1,5},{2,6},{3,7},{4,8},{5,9},{6,10},{7,11},{8,12},{9,13},{1... | collective-permute-start | bytes 884744 | tf_op jit(solution)/shard_map/ppermute | solution.py:766
  18.1 29.6 %collective-permute-start.2 = (bf16[96,1536]{1,0:T(8,128)(2,1)}, bf16[96,1536]{1,0:T(8,128)(2,1)S(1)}, u32[]{:S(2)}, u32[]{:S(2)}) collective-permute-start(bf16[96,1536]{1,0:T(8,128)(2,1)} %bitcast.235), channel_id=1, source_target_pairs={{0,8},{1,9},{2,10},{3,11},{4,12},{5,13},{6,14},{7,15},{8,0},{9,1},... | collective-permute-start | bytes 884744 | tf_op jit(solution)/shard_map/ppermute | solution.py:766
  20.7 27.0 %collective-permute-start.3 = (bf16[96,1536]{1,0:T(8,128)(2,1)}, bf16[96,1536]{1,0:T(8,128)(2,1)S(1)}, u32[]{:S(2)}, u32[]{:S(2)}) collective-permute-start(bf16[96,1536]{1,0:T(8,128)(2,1)} %bitcast.236), channel_id=1, source_target_pairs={{0,12},{1,13},{2,14},{3,15},{4,0},{5,1},{6,2},{7,3},{8,4},{9,5},{1... | collective-permute-start | bytes 884744 | tf_op jit(solution)/shard_map/ppermute | solution.py:766
  51.5 37.5 %collective-permute-start.4 = (bf16[4,96,1536]{2,1,0:T(8,128)(2,1)}, bf16[4,96,1536]{2,1,0:T(8,128)(2,1)S(1)}, u32[]{:S(2)}, u32[]{:S(2)}) collective-permute-start(bf16[4,96,1536]{2,1,0:T(8,128)(2,1)} %line_rows.2.refs_0_.refs_2_), channel_id=1, source_target_pairs={{0,2},{1,3},{2,0},{3,1},{4,6},{5,7},{6,4},{7,5},{8,10},{9,11},{10,... | collective-permute-start | bytes 3538952 | tf_op jit(solution)/shard_map/ppermute | solution.py:763
  54.1 40.6 %collective-permute-start.5 = (bf16[512,768]{1,0:T(8,128)(2,1)}, bf16[512,768]{1,0:T(8,128)(2,1)S(1)}, u32[]{:S(2)}, u32[]{:S(2)}) collective-permute-start(bf16[512,768]{1,0:T(8,128)(2,1)} %slice.208), channel_id=1, source_target_pairs={{0,16},{16,0},{1,17},{17,1},{2,18},{18,2},{3,19},{19,3},{4,20},{20... | collective-permute-start | bytes 2359304 | tf_op jit(solution)/shard_map/ppermute | solution.py:758
  59.7 74.4 %collective-permute-start.9 = (bf16[96,2304]{1,0:T(8,128)(2,1)}, bf16[96,2304]{1,0:T(8,128)(2,1)}, u32[]{:S(2)}, u32[]{:S(2)}) collective-permute-start(bf16[96,2304]{1,0:T(8,128)(2,1)} %bitcast.240), channel_id=1, source_target_pairs={{0,4},{1,5},{2,6},{3,7},{4,8},{5,9},{6,10},{7,11},{8,12},{9,13},{1... | collective-permute-start | bytes 1327112 | tf_op jit(solution)/shard_map/ppermute | solution.py:766
  66.1 67.9 %collective-permute-start.10 = (bf16[96,2304]{1,0:T(8,128)(2,1)}, bf16[96,2304]{1,0:T(8,128)(2,1)}, u32[]{:S(2)}, u32[]{:S(2)}) collective-permute-start(bf16[96,2304]{1,0:T(8,128)(2,1)} %bitcast.241), channel_id=1, source_target_pairs={{0,8},{1,9},{2,10},{3,11},{4,12},{5,13},{6,14},{7,15},{8,0},{9,1},... | collective-permute-start | bytes 1327112 | tf_op jit(solution)/shard_map/ppermute | solution.py:766
  68.4 65.6 %collective-permute-start.11 = (bf16[96,2304]{1,0:T(8,128)(2,1)}, bf16[96,2304]{1,0:T(8,128)(2,1)}, u32[]{:S(2)}, u32[]{:S(2)}) collective-permute-start(bf16[96,2304]{1,0:T(8,128)(2,1)} %bitcast.242), channel_id=1, source_target_pairs={{0,12},{1,13},{2,14},{3,15},{4,0},{5,1},{6,2},{7,3},{8,4},{9,5},{1... | collective-permute-start | bytes 1327112 | tf_op jit(solution)/shard_map/ppermute | solution.py:766
  93.2 52.7 %collective-permute-start.8 = (bf16[768,1536]{1,0:T(8,128)(2,1)}, bf16[768,1536]{1,0:T(8,128)(2,1)}, u32[]{:S(2)}, u32[]{:S(2)}) collective-permute-start(bf16[768,1536]{1,0:T(8,128)(2,1)} %bitcast.193), channel_id=1, source_target_pairs={{0,16},{16,0},{1,17},{17,1},{2,18},{18,2},{3,19},{19,3},{4,20},{20... | collective-permute-start | bytes 7077896 | tf_op jit(solution)/shard_map/ppermute | solution.py:758
  98.6 49.7 %collective-permute-start.7 = (bf16[768,1536]{1,0:T(8,128)(2,1)S(1)}, bf16[768,1536]{1,0:T(8,128)(2,1)}, u32[]{:S(2)}, u32[]{:S(2)}) collective-permute-start(bf16[768,1536]{1,0:T(8,128)(2,1)S(1)} %bitcast.200), channel_id=1, source_target_pairs={{0,1},{1,0},{2,3},{3,2},{4,5},{5,4},{6,7},{7,6},{8,9},{9,8},{10,11... | collective-permute-start | bytes 7077896 | tf_op jit(solution)/shard_map/ppermute | solution.py:755
  145.9 52.9 %collective-permute-start.14 = (bf16[4,96,2304]{2,1,0:T(8,128)(2,1)}, bf16[4,96,2304]{2,1,0:T(8,128)(2,1)}, u32[]{:S(2)}, u32[]{:S(2)}) collective-permute-start(bf16[4,96,2304]{2,1,0:T(8,128)(2,1)} %line_rows.3.refs_2_.refs_9_.refs_17_.refs_0_), channel_id=1, source_target_pairs={{0,2},{1,3},{2,0},{3,1},{4,6},{5,7},{6,4},{7,5},{8,10},{9,11},{10,... | collective-permute-start | bytes 5308424 | tf_op jit(solution)/shard_map/ppermute | solution.py:763
  179.0 26.8 %collective-permute-start.13 = (bf16[512,768]{1,0:T(8,128)(2,1)}, bf16[512,768]{1,0:T(8,128)(2,1)}, u32[]{:S(2)}, u32[]{:S(2)}) collective-permute-start(bf16[512,768]{1,0:T(8,128)(2,1)} %slice.220), channel_id=1, source_target_pairs={{0,16},{16,0},{1,17},{17,1},{2,18},{18,2},{3,19},{19,3},{4,20},{20... | collective-permute-start | bytes 2359304 | tf_op jit(solution)/shard_map/ppermute | solution.py:758
  202.9 38.9 %collective-permute-start.15 = (bf16[768,2304]{1,0:T(8,128)(2,1)}, bf16[768,2304]{1,0:T(8,128)(2,1)}, u32[]{:S(2)}, u32[]{:S(2)}) collective-permute-start(bf16[768,2304]{1,0:T(8,128)(2,1)} %bitcast.225), channel_id=1, source_target_pairs={{0,1},{1,0},{2,3},{3,2},{4,5},{5,4},{6,7},{7,6},{8,9},{9,8},{10,11... | collective-permute-start | bytes 10616840 | tf_op jit(solution)/shard_map/ppermute | solution.py:755
  205.2 33.4 %collective-permute-start.16 = (bf16[768,768]{1,0:T(8,128)(2,1)}, bf16[768,768]{1,0:T(8,128)(2,1)}, u32[]{:S(2)}, u32[]{:S(2)}) collective-permute-start(bf16[768,768]{1,0:T(8,128)(2,1)} %slice.272), channel_id=1, source_target_pairs={{0,16},{16,0},{1,17},{17,1},{2,18},{18,2},{3,19},{19,3},{4,20},{20... | collective-permute-start | bytes 3538952 | tf_op jit(solution)/shard_map/ppermute | solution.py:758
  313.6 54.8 %collective-permute-start.22 = (bf16[768,1536]{1,0:T(8,128)(2,1)}, bf16[768,1536]{1,0:T(8,128)(2,1)}, u32[]{:S(2)}, u32[]{:S(2)}) collective-permute-start(bf16[768,1536]{1,0:T(8,128)(2,1)} %products_near.2.refs_8_), channel_id=1, source_target_pairs={{0,16},{16,0},{1,17},{17,1},{2,18},{18,2},{3,19},{19,3},{4,20},{20... | collective-permute-start | bytes 7077896 | tf_op jit(solution)/shard_map/ppermute | solution.py:758
  362.2 33.3 %collective-permute-start.21 = (bf16[512,768]{1,0:T(8,128)(2,1)}, bf16[512,768]{1,0:T(8,128)(2,1)}, u32[]{:S(2)}, u32[]{:S(2)}) collective-permute-start(bf16[512,768]{1,0:T(8,128)(2,1)} %convolution_convert_fusion.7.refs_5_), channel_id=1, source_target_pairs={{0,16},{16,0},{1,17},{17,1},{2,18},{18,2},{3,19},{19,3},{4,20},{20... | collective-permute-start | bytes 2359304 | tf_op jit(solution)/shard_map/ppermute | solution.py:758
  428.6 37.6 %collective-permute-start.26 = (bf16[4,96,1920]{2,1,0:T(8,128)(2,1)}, bf16[4,96,1920]{2,1,0:T(8,128)(2,1)}, u32[]{:S(2)}, u32[]{:S(2)}) collective-permute-start(bf16[4,96,1920]{2,1,0:T(8,128)(2,1)} %dynamic-slice_bitcast_fusion.1), channel_id=1, source_target_pairs={{0,2},{1,3},{2,0},{3,1},{4,6},{5,7},{6,4},{7,5},{8,10},{9,11},{10,... | collective-permute-start | bytes 4423688 | tf_op jit(solution)/shard_map/ppermute | solution.py:763
  433.0 197.8 %reduce-scatter.3.cloned.1.call-start = ((), (), s32[]{:S(2)}) async-start(), calls=%async_computation.3 | async-start | bytes 3760128 | tf_op jit(solution)/shard_map/reduce_scatter | solution.py:842
  441.4 66.8 %collective-permute-start.28 = (bf16[768,1536]{1,0:T(8,128)(2,1)}, bf16[768,1536]{1,0:T(8,128)(2,1)}, u32[]{:S(2)}, u32[]{:S(2)}) collective-permute-start(bf16[768,1536]{1,0:T(8,128)(2,1)} %products_near.3.refs_8_), channel_id=1, source_target_pairs={{0,16},{16,0},{1,17},{17,1},{2,18},{18,2},{3,19},{19,3},{4,20},{20... | collective-permute-start | bytes 7077896 | tf_op jit(solution)/shard_map/ppermute | solution.py:758
  494.4 34.0 %collective-permute-start.32 = (bf16[96,1920]{1,0:T(8,128)(2,1)}, bf16[96,1920]{1,0:T(8,128)(2,1)}, u32[]{:S(2)}, u32[]{:S(2)}) collective-permute-start(bf16[96,1920]{1,0:T(8,128)(2,1)} %get-tuple-element.209), channel_id=1, source_target_pairs={{0,12},{1,13},{2,14},{3,15},{4,0},{5,1},{6,2},{7,3},{8,4},{9,5},{1... | collective-permute-start | bytes 1105928 | tf_op jit(solution)/shard_map/ppermute | solution.py:766
  503.0 32.8 %collective-permute-start.31 = (bf16[96,1920]{1,0:T(8,128)(2,1)}, bf16[96,1920]{1,0:T(8,128)(2,1)}, u32[]{:S(2)}, u32[]{:S(2)}) collective-permute-start(bf16[96,1920]{1,0:T(8,128)(2,1)} %get-tuple-element.210), channel_id=1, source_target_pairs={{0,8},{1,9},{2,10},{3,11},{4,12},{5,13},{6,14},{7,15},{8,0},{9,1},... | collective-permute-start | bytes 1105928 | tf_op jit(solution)/shard_map/ppermute | solution.py:766
  503.4 24.3 %collective-permute-start.30 = (bf16[96,1920]{1,0:T(8,128)(2,1)}, bf16[96,1920]{1,0:T(8,128)(2,1)S(1)}, u32[]{:S(2)}, u32[]{:S(2)}) collective-permute-start(bf16[96,1920]{1,0:T(8,128)(2,1)} %get-tuple-element.208), channel_id=1, source_target_pairs={{0,4},{1,5},{2,6},{3,7},{4,8},{5,9},{6,10},{7,11},{8,12},{9,13},{1... | collective-permute-start | bytes 1105928 | tf_op jit(solution)/shard_map/ppermute | solution.py:766
  512.6 35.0 %collective-permute-start.29 = (bf16[4,96,1920]{2,1,0:T(8,128)(2,1)}, bf16[4,96,1920]{2,1,0:T(8,128)(2,1)}, u32[]{:S(2)}, u32[]{:S(2)}) collective-permute-start(bf16[4,96,1920]{2,1,0:T(8,128)(2,1)} %dynamic-slice_bitcast_fusion), channel_id=1, source_target_pairs={{0,2},{1,3},{2,0},{3,1},{4,6},{5,7},{6,4},{7,5},{8,10},{9,11},{10,... | collective-permute-start | bytes 4423688 | tf_op jit(solution)/shard_map/ppermute | solution.py:763
  517.3 58.0 %collective-permute-start.27 = (bf16[512,768]{1,0:T(8,128)(2,1)}, bf16[512,768]{1,0:T(8,128)(2,1)}, u32[]{:S(2)}, u32[]{:S(2)}) collective-permute-start(bf16[512,768]{1,0:T(8,128)(2,1)} %convolution_convert_fusion.6.refs_2_), channel_id=1, source_target_pairs={{0,16},{16,0},{1,17},{17,1},{2,18},{18,2},{3,19},{19,3},{4,20},{20... | collective-permute-start | bytes 2359304 | tf_op jit(solution)/shard_map/ppermute | solution.py:758
  573.0 17.1 %collective-permute-start.44 = (f32[20,768]{1,0:T(8,128)}, f32[20,768]{1,0:T(8,128)S(1)}, u32[]{:S(2)}, u32[]{:S(2)}) collective-permute-start(f32[20,768]{1,0:T(8,128)} %select_maximum_fusion), channel_id=1, source_target_pairs={{0,16},{16,0},{1,17},{17,1},{2,18},{18,2},{3,19},{19,3},{4,20},{20... | collective-permute-start | bytes 184328 | tf_op jit(solution)/shard_map/ppermute | solution.py:758
  584.3 15.9 %collective-permute-start.34 = (bf16[48,2304]{1,0:T(8,128)(2,1)}, bf16[48,2304]{1,0:T(8,128)(2,1)S(1)}, u32[]{:S(2)}, u32[]{:S(2)}) collective-permute-start(bf16[48,2304]{1,0:T(8,128)(2,1)} %hold.30), channel_id=1, source_target_pairs={{0,16},{16,0},{1,17},{17,1},{2,18},{18,2},{3,19},{19,3},{4,20},{20... | collective-permute-start | bytes 663560 | tf_op jit(solution)/shard_map/ppermute | solution.py:758
  584.5 43.0 %collective-permute-start.37 = (bf16[96,1920]{1,0:T(8,128)(2,1)S(1)}, bf16[96,1920]{1,0:T(8,128)(2,1)}, u32[]{:S(2)}, u32[]{:S(2)}) collective-permute-start(bf16[96,1920]{1,0:T(8,128)(2,1)S(1)} %get-tuple-element.206), channel_id=1, source_target_pairs={{0,12},{1,13},{2,14},{3,15},{4,0},{5,1},{6,2},{7,3},{8,4},{9,5},{1... | collective-permute-start | bytes 1105928 | tf_op jit(solution)/shard_map/ppermute | solution.py:766
  588.6 38.9 %collective-permute-start.36 = (bf16[96,1920]{1,0:T(8,128)(2,1)S(1)}, bf16[96,1920]{1,0:T(8,128)(2,1)}, u32[]{:S(2)}, u32[]{:S(2)}) collective-permute-start(bf16[96,1920]{1,0:T(8,128)(2,1)S(1)} %get-tuple-element.207), channel_id=1, source_target_pairs={{0,8},{1,9},{2,10},{3,11},{4,12},{5,13},{6,14},{7,15},{8,0},{9,1},... | collective-permute-start | bytes 1105928 | tf_op jit(solution)/shard_map/ppermute | solution.py:766
  589.9 36.9 %collective-permute-start.35 = (bf16[96,1920]{1,0:T(8,128)(2,1)}, bf16[96,1920]{1,0:T(8,128)(2,1)S(1)}, u32[]{:S(2)}, u32[]{:S(2)}) collective-permute-start(bf16[96,1920]{1,0:T(8,128)(2,1)} %get-tuple-element.205), channel_id=1, source_target_pairs={{0,4},{1,5},{2,6},{3,7},{4,8},{5,9},{6,10},{7,11},{8,12},{9,13},{1... | collective-permute-start | bytes 1105928 | tf_op jit(solution)/shard_map/ppermute | solution.py:766
  (81 other events, 540.7 us)
Sparse Core Ops, SparseCore 0:
  10.3 89.6 all-gather.5
  102.9 59.2 all-gather.3
  433.1 72.3 reduce-scatter.4
  520.4 68.6 reduce-scatter.2

commit v4 on v3

--- a/solution.py
+++ b/solution.py
@@ -415,8 +415,8 @@
         ),
         name="table_sums",
     )(window, place, *score_sums, *waits)
-    grouped = grouped.reshape(bucket_count, 8, head_count, 8)
-    return jnp.sum(grouped * jnp.eye(8, dtype=F32)[None, :, None, :], axis=(1, 3))
+    table = grouped.reshape(bucket_count, 8, head_count, 8)
+    return jnp.sum(table * jnp.eye(8, dtype=F32)[None, :, None, :], axis=(1, 3)), grouped
 
 
 def norm_rows(tensor, scale_row, shift_row):
@@ -1147,7 +1147,7 @@
             if paired:
                 rest = hold(rest, ffn_low)
             query_grad = unsort_wide(rest)
-            table_grad = table_call(
+            table_grad, table_raw = table_call(
                 window, score_sums, place_column, bucket_count, *([passed, ffn_low, query_grad] if paired else [])
             )
         if paired:
@@ -1158,15 +1158,18 @@
             grad_split = jnp.roll(grad_split, block_index, axis=0)
             come = lax.psum_scatter(grad_split, "blk", scatter_dimension=0, tiled=False)
     if paired:
-        come = hold(come, table_grad)
-        ffn_high = grid.scatter_end(ffn_begun, table_grad)
+        ffn_high = grid.scatter_end(ffn_begun, table_raw)
+        come = hold(come, ffn_high)
         if layer_count > 1:
-            matrix_rows[1] = finish_rows(hold(upper, table_grad))
-        matrix_rows[0] = finish_rows(hold(ffn_high, attn_part))
-        attn_rows = [grid.scatter_end_blocks(hold(part, table_grad)) for part in attn_parts]
+            matrix_rows[1] = finish_rows(hold(upper, ffn_high))
+        matrix_rows[0] = finish_rows(ffn_high)
+        attn_rows = [grid.scatter_end_blocks(hold(part, ffn_high)) for part in attn_parts]
     grad_stream[0] = content_side(grad_stream[0], come)
+    norm_lines = jnp.concatenate([terms[:4] for terms in norm_terms], axis=0)
+    if paired:
+        norm_lines = hold(norm_lines, ffn_high, attn_part)
     table_lines = jnp.pad(table_grad.T, ((0, 0), (0, width - bucket_count)))
-    sums = grid.sum_all(jnp.concatenate([*[terms[:4] for terms in norm_terms], table_lines], axis=0))
+    sums = grid.sum_all(jnp.concatenate([norm_lines, table_lines], axis=0))
     norm_sum = sums[: 4 * layer_count].reshape(layer_count, 2, 2, width)
     table_total = sums[4 * layer_count :, :bucket_count].T
     matrix_grads = tuple(jnp.stack(rows_of, axis=0) for rows_of in (attn_rows, *zip(*matrix_rows)))

time: 666 us -> 674 us (1.012)
  starting transfers between devices: 59.2 us -> 68.1 us
    ppermute x12, waiting for transfers between devices: 12.4 us -> 34.1 us  [from_high(): lax.ppermute(tensor, 'dp', [(i, (i + 2 * self.low * step) % self.total) f...]
    ppermute x4, waiting for transfers between devices: 23.6 us -> 6.14 us  [sum_all(): lax.ppermute(tensor, 'dp', [(i, i ^ bit) for i in range(self.total)])]
    unnamed x120 -> x128, local copies, waits for them, and re-layouts: 14.6 us -> 15.4 us
  transfers between devices with their start and end apart: 53 -> 53, of which waited for: 21 -> 21; matrix products, arithmetic and copies ran while one was open for 17% -> 16% of each run, Pallas kernels for 38% -> 37%
where the time goes in v4:
time: 674 us; the launch traced here: 666 us
  Pallas kernels  333 us (49%)
  waiting for transfers between devices  118 us (18%)
  starting transfers between devices  68.1 us (10%)
  matrix products  61.5 us (9%)
  local copies, waits for them, and re-layouts  38.7 us (6%)
  other arithmetic  30.8 us (5%)
  between operations  15.4 us (2%)
    pallas_call x8, Pallas kernels, products_call(): pl.pallas_call(functools.partial(product_kernel, plan), grid_spec=pltpu.P...  76.9 us
    pallas_call x4, Pallas kernels, attend_back_call(): pl.pallas_call(attend_back_kernel, grid=(pairs,), in_specs=[pl.BlockSpec(...  56.6 us
    pallas_call x3, Pallas kernels, layer_tail_call(): pl.pallas_call(functools.partial(layer_tail_kernel, len(pieces), plan, sp...  51.2 us
    pallas_call x3, Pallas kernels, layer_tail_back_call(): pl.pallas_call(functools.partial(layer_tail_back_kernel, len(pieces), pla...  50.7 us
    pallas_call x2, Pallas kernels, attend_call(): pl.pallas_call(attend_kernel, grid=(pairs // group,), in_specs=[pl.BlockS...  48.4 us
    ppermute x12, waiting for transfers between devices, from_high(): lax.ppermute(tensor, 'dp', [(i, (i + 2 * self.low * step) % self.total) f...  34.1 us
    ppermute x15, waiting for transfers between devices, from_block(): return lax.ppermute(tensor, 'blk', [(0, 1), (1, 0)])  31.7 us
    dot_general x10, matrix products, dot_nn(): return jnp.dot(left_side, right_side, preferred_element_type=F32)  30.4 us
  transfers between devices with their start and end apart: 53, of which 21 were waited for; matrix products, arithmetic and copies ran while one was open for 16% of the time, Pallas kernels for 37%

profile of v4, /device:TPU:0, one launch (start us, length us, event | category | flops | bytes accessed | tf_op | source)
XLA Modules:
  0.0 666.0 jit_solution(8107162113655667969)
XLA Ops:
  24.9 7.9 %setup_rows.1 = (s32[2,4]{1,0:T(2,128)}, s32[1,1024]{1,0:T(1,128)}, s32[1,1024]{1,0:T(1,128)}, s32[512,1]{1,0:T(8,128)}, s32[512,1]{1,0:T(8,128)}, /*index=5*/s3...) custom-call(s32[2]{0:T(128)} %pad_add_fusion.side_ref, ...), custom_call_target="tpu_custom_call" | custom-call | flops 1610612736 | bytes 6291456 | tf_op jit(solution)/shard_map/setup_rows/pallas_call | solution.py:141
  32.8 13.6 %bias_rows.1.refs_4_.bias_ref = bf16[12,512,1024]{2,1,0:T(8,128)(2,1)} custom-call(s32[2,4]{1,0:T(2,128)} %get-tuple-element.99.window_ref, f32[12,128]{1,0:T(8,128)} %concatenate.144.table_ref, s32[512,1]{1,0:T(8,128)} %get-tuple-element.100.place_ref, s32[512,1]{1,0:T(8,128)} %get-tuple-element.101.doc_ref, s32[512,1]{1,0:T(8,128)} %get-tuple-element.102.rank_ref, ...), custom_call_target="tpu_custom_call" | custom-call | bytes 50331648 | tf_op jit(solution)/shard_map/bias_rows/pallas_call | solution.py:187
  60.2 5.9 collective-permute-start.9
  68.6 20.3 %collective-permute-done.4.refs_1_ = bf16[4,96,1536]{2,1,0:T(8,128)(2,1)S(1)} collective-permute-done((bf16[4,96,1536]{2,1,0:T(8,128)(2,1)}, bf16[4,96,1536]{2,1,0:T(8,128)(2,1)S(1)}, u32[]{:S(2)}, u32[]{:S(2)}) %collective-permute-start.4) | collective-permute-done | bytes 1179680 | tf_op jit(solution)/shard_map/ppermute | solution.py:763
  109.4 24.2 %attend.2 = (f32[2,512,768]{2,1,0:T(8,128)}, bf16[2,512,768]{2,1,0:T(8,128)(2,1)}, bf16[12,2,512,1024]{3,2,1,0:T(8,128)(2,1)}) custom-call(s32[2,4]{1,0:T(2,128)} %get-tuple-element.99.window_ref, bf16[2,512,768]{2,1,0:T(8,128)(2,1)} %bitcast.221, bf16[1024,768]{1,0:T(8,128)(2,1)} %convolution_convert_fusion.4.k_ref.refs_1_, ...), custom_call_target="tpu_custom_call" | custom-call | flops 6442450944 | bytes 50331648 | tf_op jit(solution)/shard_map/attend/pallas_call | solution.py:256
  136.4 11.2 %collective-permute-done.8.refs_0_ = bf16[768,1536]{1,0:T(8,128)(2,1)} collective-permute-done((bf16[768,1536]{1,0:T(8,128)(2,1)}, bf16[768,1536]{1,0:T(8,128)(2,1)}, u32[]{:S(2)}, u32[]{:S(2)}) %collective-permute-start.8) | collective-permute-done | bytes 2359328 | tf_op jit(solution)/shard_map/ppermute | solution.py:758
  152.6 7.4 %all-gather.4.cloned.1.call-done.refs_2_.refs_6_ = bf16[768,3840]{1,0:T(8,128)(2,1)} async-done(((bf16[48,3840]{1,0:T(8,128)(2,1)}), bf16[768,3840]{1,0:T(8,128)(2,1)}) %all-gather.4.cloned.1.call-update) | async-done | bytes 5898256 | tf_op jit(solution)/shard_map/all_gather | solution.py:769
  160.0 14.6 %layer_tail.3 = (f32[1024,768]{1,0:T(8,128)}, bf16[1024,768]{1,0:T(8,128)(2,1)}, f32[1024,768]{1,0:T(8,128)}, bf16[1024,768]{1,0:T(8,128)(2,1)}, bf16[1024,3072]...) custom-call(bf16[1024,768]{1,0:T(8,128)(2,1)} %get-tuple-element.98.refs_0_, ...), custom_call_target="tpu_custom_call" | custom-call | flops 5435817984 | bytes 31457280 | tf_op jit(solution)/shard_map/layer_tail/pallas_call | solution.py:492
  178.4 14.3 %layer_tail.4 = (f32[1024,768]{1,0:T(8,128)}, bf16[1024,768]{1,0:T(8,128)(2,1)}, f32[1024,768]{1,0:T(8,128)}, bf16[1024,768]{1,0:T(8,128)(2,1)}, bf16[1024,3072]...) custom-call(bf16[1024,768]{1,0:T(8,128)(2,1)} %get-tuple-element.98., ...), custom_call_target="tpu_custom_call", output_to_operand_aliasing={{0}: (9, {}), {1}: (10, {}), {2}: (11, {}), {3}: (12, {}), ... | custom-call | flops 5435817984 | bytes 31457280 | tf_op jit(solution)/shard_map/layer_tail/pallas_call | solution.py:492
  212.4 24.2 %attend.3 = (f32[2,512,768]{2,1,0:T(8,128)}, bf16[2,512,768]{2,1,0:T(8,128)(2,1)}, bf16[12,2,512,1024]{3,2,1,0:T(8,128)(2,1)}) custom-call(s32[2,4]{1,0:T(2,128)} %get-tuple-element.99.window_ref, bf16[2,512,768]{2,1,0:T(8,128)(2,1)} %bitcast.214, bf16[1024,768]{1,0:T(8,128)(2,1)} %convolution_convert_fusion.1.k_ref.refs_1_, ...), custom_call_target="tpu_custom_call" | custom-call | flops 6442450944 | bytes 50331648 | tf_op jit(solution)/shard_map/attend/pallas_call | solution.py:256
  241.0 22.2 %layer_tail.5 = (f32[1024,768]{1,0:T(8,128)}, bf16[1024,768]{1,0:T(8,128)(2,1)}, f32[1024,768]{1,0:T(8,128)}, bf16[1024,768]{1,0:T(8,128)(2,1)}, bf16[1024,3072]...) custom-call(f32[1024,768]{1,0:T(8,128)} %get-tuple-element.117.refs_0_.refs_1_, ...), custom_call_target="tpu_custom_call" | custom-call | flops 10871635968 | bytes 31457280 | tf_op jit(solution)/shard_map/layer_tail/pallas_call | solution.py:492
  263.8 22.0 %layer_tail_back.3 = (bf16[1024,768]{1,0:T(8,128)(2,1)}, bf16[1024,3072]{1,0:T(8,128)(2,1)}, f32[1024,768]{1,0:T(8,128)}, bf16[1024,768]{1,0:T(8,128)(2,1)}, bf1...) custom-call(bf16[1024,768]{1,0:T(8,128)(2,1)} %get-tuple-element.121.refs_0_, f32[1024,768]{1,0:T(8,128)} %get-tuple-element.122.refs_1_, ...), custom_call_target="tpu_custom_call" | custom-call | flops 10871635968 | bytes 37748736 | tf_op jit(solution)/shard_map/layer_tail_back/pallas_call | solution.py:572
  285.8 12.6 %products_sent.2 = (bf16[768,1536]{1,0:T(8,128)(2,1)}, bf16[768,1536]{1,0:T(8,128)(2,1)}, bf16[768,384]{1,0:T(8,128)(2,1)}) custom-call(s32[1]{0:T(128)} %bitcast.7.side_ref, bf16[1024,768]{1,0:T(8,128)(2,1)} %get-tuple-element.131.refs_0_, bf16[1024,3072]{1,0:T(8,128)(2,1)} %get-tuple-element.132.refs_1_, ...), custom_call_target="tpu_custom_call" | custom-call | flops 5435817984 | bytes 18119392 | tf_op jit(solution)/shard_map/products_sent/pallas_call | solution.py:663
  304.6 7.2 %products_near.2.refs_8_ = bf16[768,1536]{1,0:T(8,128)(2,1)} custom-call(s32[1]{0:T(128)} %bitcast.7.side_ref, bf16[1024,768]{1,0:T(8,128)(2,1)} %get-tuple-element.131.refs_0_, bf16[1024,3072]{1,0:T(8,128)(2,1)} %get-tuple-element.132.refs_1_, bf16[768,1536]{1,0:T(8,128)(2,1)} %copy-done.33, bf16[1024,768]{1,0:T(8,128)(2,1)} %get-tuple-element.133.refs_2_.refs_3_, ...), custom_call_target="tpu_custom_call" | custom-call | flops 2415919104 | bytes 8053063 | tf_op jit(solution)/shard_map/products_near/pallas_call | solution.py:663
  316.0 9.7 %products_held.2 = (bf16[768,1536]{1,0:T(8,128)(2,1)}, bf16[768,384]{1,0:T(8,128)(2,1)}) custom-call(s32[1]{0:T(128)} %bitcast.7.side_ref, bf16[1024,768]{1,0:T(8,128)(2,1)} %get-tuple-element.131.refs_0_, bf16[1024,3072]{1,0:T(8,128)(2,1)} %get-tuple-element.132.refs_1_, bf16[768,1536]{1,0:T(8,128)(2,1)} %copy-done.34, ...), custom_call_target="tpu_custom_call" | custom-call | flops 3019898880 | bytes 10066329 | tf_op jit(solution)/shard_map/products_held/pallas_call | solution.py:663
  325.6 14.1 %attend_back.4 = (bf16[2,512,768]{2,1,0:T(8,128)(2,1)}, bf16[1024,768]{1,0:T(8,128)(2,1)}, bf16[1024,768]{1,0:T(8,128)(2,1)}, bf16[12,512,1024]{2,1,0:T(8,128)(2,1)}) custom-call(s32[2,4]{1,0:T(2,128)} %get-tuple-element.99.window_ref, bf16[2,512,768]{2,1,0:T(8,128)(2,1)} %bitcast.215, bf16[1024,768]{1,0:T(8,128)(2,1)} %convolution_convert_fusion.1.k_ref.refs_1_, ...), custom_call_target="tpu_custom_call" | custom-call | flops 6442450944 | bytes 25165824 | tf_op jit(solution)/shard_map/attend_back/pallas_call | solution.py:333
  339.7 14.2 %attend_back.5 = (bf16[2,512,768]{2,1,0:T(8,128)(2,1)}, bf16[1024,768]{1,0:T(8,128)(2,1)}, bf16[1024,768]{1,0:T(8,128)(2,1)}, bf16[12,512,1024]{2,1,0:T(8,128)(2,1)}) custom-call(s32[2,4]{1,0:T(2,128)} %get-tuple-element.99.window_ref, bf16[2,512,768]{2,1,0:T(8,128)(2,1)} %bitcast.216, ...), custom_call_target="tpu_custom_call", output_to_operand_aliasing={{0}: (7, {}), {1}: (8, {}), {2}: (9, {}), {3}: (10, {})} | custom-call | flops 6442450944 | bytes 25165824 | tf_op jit(solution)/shard_map/attend_back/pallas_call | solution.py:333
  370.2 8.7 %products_attn.2.refs_14_.refs_19_ = bf16[768,2304]{1,0:T(8,128)(2,1)} custom-call(s32[1]{0:T(128)} %bitcast.7.side_ref, bf16[1024,768]{1,0:T(8,128)(2,1)} %get-tuple-element.118.refs_2_.refs_0_, bf16[1024,768]{1,0:T(8,128)(2,1)} %bitcast.226, bf16[1024,768]{1,0:T(8,128)(2,1)} %copy-done.25, bf16[1024,768]{1,0:T(8,128)(2,1)} %get-tuple-element.146.refs_3_, ...), custom_call_target="tpu_custom_call" | custom-call | flops 3623878656 | bytes 12079595 | tf_op jit(solution)/shard_map/products_attn/pallas_call | solution.py:663
  378.9 14.4 %layer_tail_back.4 = (bf16[1024,768]{1,0:T(8,128)(2,1)}, bf16[1024,3072]{1,0:T(8,128)(2,1)}, f32[1024,768]{1,0:T(8,128)}, bf16[1024,768]{1,0:T(8,128)(2,1)}, bf1...) custom-call(f32[512,768]{1,0:T(8,128)} %slice.274.refs_0_, f32[1024,768]{1,0:T(8,128)} %get-tuple-element.117.refs_0_.refs_1_, ...), custom_call_target="tpu_custom_call" | custom-call | flops 5435817984 | bytes 37748736 | tf_op jit(solution)/shard_map/layer_tail_back/pallas_call | solution.py:572
  397.5 14.3 %layer_tail_back.5 = (bf16[1024,768]{1,0:T(8,128)(2,1)}, bf16[1024,3072]{1,0:T(8,128)(2,1)}, f32[1024,768]{1,0:T(8,128)}, bf16[1024,768]{1,0:T(8,128)(2,1)}, bf1...) custom-call(f32[512,768]{1,0:T(8,128)} %fusion.3.refs_0_, ...), custom_call_target="tpu_custom_call", output_to_operand_aliasing={{0}: (14, {}), {1}: (15, {}), {2}: (16, {}), {3}: (17, {}),... | custom-call | flops 5435817984 | bytes 37748736 | tf_op jit(solution)/shard_map/layer_tail_back/pallas_call | solution.py:572
  411.8 12.6 %products_sent.3 = (bf16[768,1536]{1,0:T(8,128)(2,1)}, bf16[768,1536]{1,0:T(8,128)(2,1)}, bf16[768,384]{1,0:T(8,128)(2,1)}) custom-call(s32[1]{0:T(128)} %bitcast.7.side_ref, bf16[1024,768]{1,0:T(8,128)(2,1)} %get-tuple-element.162.refs_0_, bf16[1024,3072]{1,0:T(8,128)(2,1)} %get-tuple-element.163.refs_1_, ...), custom_call_target="tpu_custom_call" | custom-call | flops 5435817984 | bytes 18119392 | tf_op jit(solution)/shard_map/products_sent/pallas_call | solution.py:663
  435.8 7.6 %products_near.3.refs_8_ = bf16[768,1536]{1,0:T(8,128)(2,1)} custom-call(s32[1]{0:T(128)} %bitcast.7.side_ref, bf16[1024,768]{1,0:T(8,128)(2,1)} %get-tuple-element.162.refs_0_, bf16[1024,3072]{1,0:T(8,128)(2,1)} %get-tuple-element.163.refs_1_, bf16[768,1536]{1,0:T(8,128)(2,1)} %collective-permute-done.25.refs_2_, ...), custom_call_target="tpu_custom_call" | custom-call | flops 2415919104 | bytes 8053063 | tf_op jit(solution)/shard_map/products_near/pallas_call | solution.py:663
  443.8 9.7 %products_held.3 = (bf16[768,1536]{1,0:T(8,128)(2,1)}, bf16[768,384]{1,0:T(8,128)(2,1)}) custom-call(s32[1]{0:T(128)} %bitcast.7.side_ref, bf16[1024,768]{1,0:T(8,128)(2,1)} %get-tuple-element.162.refs_0_, bf16[1024,3072]{1,0:T(8,128)(2,1)} %get-tuple-element.163.refs_1_, bf16[768,1536]{1,0:T(8,128)(2,1)} %collective-permute-done.23.refs_2_, ...), custom_call_target="tpu_custom_call" | custom-call | flops 3019898880 | bytes 10066329 | tf_op jit(solution)/shard_map/products_held/pallas_call | solution.py:663
  453.5 14.0 %attend_back.6 = (bf16[2,512,768]{2,1,0:T(8,128)(2,1)}, bf16[1024,768]{1,0:T(8,128)(2,1)}, bf16[1024,768]{1,0:T(8,128)(2,1)}, bf16[12,512,1024]{2,1,0:T(8,128)(2,1)}) custom-call(s32[2,4]{1,0:T(2,128)} %get-tuple-element.99.window_ref, bf16[2,512,768]{2,1,0:T(8,128)(2,1)} %bitcast.222, bf16[1024,768]{1,0:T(8,128)(2,1)} %convolution_convert_fusion.4.k_ref.refs_1_, ...), custom_call_target="tpu_custom_call" | custom-call | flops 6442450944 | bytes 25165824 | tf_op jit(solution)/shard_map/attend_back/pallas_call | solution.py:333
  470.4 14.3 %attend_back.7 = (bf16[2,512,768]{2,1,0:T(8,128)(2,1)}, bf16[1024,768]{1,0:T(8,128)(2,1)}, bf16[1024,768]{1,0:T(8,128)(2,1)}, bf16[12,512,1024]{2,1,0:T(8,128)(2,1)}) custom-call(s32[2,4]{1,0:T(2,128)} %get-tuple-element.99.window_ref, bf16[2,512,768]{2,1,0:T(8,128)(2,1)} %bitcast.223, ...), custom_call_target="tpu_custom_call", output_to_operand_aliasing={{0}: (7, {}), {1}: (8, {}), {2}: (9, {}), {3}: (10, {})} | custom-call | flops 6442450944 | bytes 25165824 | tf_op jit(solution)/shard_map/attend_back/pallas_call | solution.py:333
  484.7 8.8 %products_attn.3.refs_1_ = bf16[768,2304]{1,0:T(8,128)(2,1)} custom-call(s32[1]{0:T(128)} %bitcast.7.side_ref, bf16[1024,768]{1,0:T(8,128)(2,1)} %get-tuple-element.98.refs_0_, bf16[1024,768]{1,0:T(8,128)(2,1)} %bitcast.217, bf16[1024,768]{1,0:T(8,128)(2,1)} %add_convert_fusion.5.refs_2_, bf16[1024,768]{1,0:T(8,128)(2,1)} %get-tuple-element.177.refs_3_.refs_0_, ...), custom_call_target="tpu_custom_call" | custom-call | flops 3623878656 | bytes 12079595 | tf_op jit(solution)/shard_map/products_attn/pallas_call | solution.py:663
  527.6 7.1 %collective-permute-done.31 = bf16[96,1920]{1,0:T(8,128)(2,1)} collective-permute-done((bf16[96,1920]{1,0:T(8,128)(2,1)}, bf16[96,1920]{1,0:T(8,128)(2,1)}, u32[]{:S(2)}, u32[]{:S(2)}) %collective-permute-start.31) | collective-permute-done | bytes 368672 | tf_op jit(solution)/shard_map/ppermute | solution.py:766
  536.9 9.1 %collective-permute-done.29.refs_0_ = bf16[4,96,1920]{2,1,0:T(8,128)(2,1)S(1)} collective-permute-done((bf16[4,96,1920]{2,1,0:T(8,128)(2,1)}, bf16[4,96,1920]{2,1,0:T(8,128)(2,1)S(1)}, u32[]{:S(2)}, u32[]{:S(2)}) %collective-permute-start.29) | collective-permute-done | bytes 1474592 | tf_op jit(solution)/shard_map/ppermute | solution.py:763
  558.2 11.8 %table_sums.1.refs_1_ = f32[256,96]{1,0:T(8,128)} custom-call(s32[2,4]{1,0:T(2,128)} %get-tuple-element.99.window_ref, s32[512,1]{1,0:T(8,128)} %get-tuple-element.100.place_ref, bf16[12,512,1024]{2,1,0:T(8,128)(2,1)} %get-tuple-element.179.refs_0_, bf16[12,512,1024]{2,1,0:T(8,128)(2,1)} %get-tuple-element.180.refs_1_, ...), custom_call_target="tpu_custom_call" | custom-call | flops 3221225472 | bytes 25165824 | tf_op jit(solution)/shard_map/table_sums/pallas_call | solution.py:398
  572.1 16.7 %collective-permute-done.33.refs_0_ = bf16[96,1920]{1,0:T(8,128)(2,1)S(1)} collective-permute-done((bf16[96,1920]{1,0:T(8,128)(2,1)}, bf16[96,1920]{1,0:T(8,128)(2,1)S(1)}, u32[]{:S(2)}, u32[]{:S(2)}) %collective-permute-start.33) | collective-permute-done | bytes 368672 | tf_op jit(solution)/shard_map/ppermute | solution.py:766
  589.6 8.4 %collective-permute-done.34 = bf16[96,1920]{1,0:T(8,128)(2,1)} collective-permute-done((bf16[96,1920]{1,0:T(8,128)(2,1)S(1)}, bf16[96,1920]{1,0:T(8,128)(2,1)}, u32[]{:S(2)}, u32[]{:S(2)}) %collective-permute-start.34) | collective-permute-done | bytes 368672 | tf_op jit(solution)/shard_map/ppermute | solution.py:766
  620.2 6.5 collective-permute-done.43
  (367 shorter events, 241.0 us)
Async XLA Ops:
  7.2 92.6 %all-gather.6.cloned.1.call-start = ((), (), s32[]{:S(2)}) async-start(), calls=%async_computation.5 | async-start | bytes 3760128 | tf_op jit(solution)/shard_map/all_gather | solution.py:769
  9.1 150.9 %all-gather.4.cloned.1.call-start = ((), (), s32[]{:S(2)}) async-start(), calls=%async_computation.2 | async-start | bytes 6266880 | tf_op jit(solution)/shard_map/all_gather | solution.py:769
  10.9 597.6 %reduce-scatter.5.cloned.1.call-start = ((), (), s32[]{:S(2)}) async-start(), calls=%async_computation.4 | async-start | bytes 3760128 | tf_op jit(solution)/shard_map/reduce_scatter | solution.py:842
  15.5 30.9 %collective-permute-start.1 = (bf16[96,1536]{1,0:T(8,128)(2,1)}, bf16[96,1536]{1,0:T(8,128)(2,1)S(1)}, u32[]{:S(2)}, u32[]{:S(2)}) collective-permute-start(bf16[96,1536]{1,0:T(8,128)(2,1)} %bitcast.238), channel_id=1, source_target_pairs={{0,4},{1,5},{2,6},{3,7},{4,8},{5,9},{6,10},{7,11},{8,12},{9,13},{1... | collective-permute-start | bytes 884744 | tf_op jit(solution)/shard_map/ppermute | solution.py:766
  18.1 29.6 %collective-permute-start.2 = (bf16[96,1536]{1,0:T(8,128)(2,1)}, bf16[96,1536]{1,0:T(8,128)(2,1)S(1)}, u32[]{:S(2)}, u32[]{:S(2)}) collective-permute-start(bf16[96,1536]{1,0:T(8,128)(2,1)} %bitcast.239), channel_id=1, source_target_pairs={{0,8},{1,9},{2,10},{3,11},{4,12},{5,13},{6,14},{7,15},{8,0},{9,1},... | collective-permute-start | bytes 884744 | tf_op jit(solution)/shard_map/ppermute | solution.py:766
  20.7 27.0 %collective-permute-start.3 = (bf16[96,1536]{1,0:T(8,128)(2,1)}, bf16[96,1536]{1,0:T(8,128)(2,1)S(1)}, u32[]{:S(2)}, u32[]{:S(2)}) collective-permute-start(bf16[96,1536]{1,0:T(8,128)(2,1)} %bitcast.240), channel_id=1, source_target_pairs={{0,12},{1,13},{2,14},{3,15},{4,0},{5,1},{6,2},{7,3},{8,4},{9,5},{1... | collective-permute-start | bytes 884744 | tf_op jit(solution)/shard_map/ppermute | solution.py:766
  51.4 37.5 %collective-permute-start.4 = (bf16[4,96,1536]{2,1,0:T(8,128)(2,1)}, bf16[4,96,1536]{2,1,0:T(8,128)(2,1)S(1)}, u32[]{:S(2)}, u32[]{:S(2)}) collective-permute-start(bf16[4,96,1536]{2,1,0:T(8,128)(2,1)} %line_rows.2.refs_0_.refs_2_), channel_id=1, source_target_pairs={{0,2},{1,3},{2,0},{3,1},{4,6},{5,7},{6,4},{7,5},{8,10},{9,11},{10,... | collective-permute-start | bytes 3538952 | tf_op jit(solution)/shard_map/ppermute | solution.py:763
  54.5 40.9 %collective-permute-start.5 = (bf16[512,768]{1,0:T(8,128)(2,1)}, bf16[512,768]{1,0:T(8,128)(2,1)S(1)}, u32[]{:S(2)}, u32[]{:S(2)}) collective-permute-start(bf16[512,768]{1,0:T(8,128)(2,1)} %slice.208), channel_id=1, source_target_pairs={{0,16},{16,0},{1,17},{17,1},{2,18},{18,2},{3,19},{19,3},{4,20},{20... | collective-permute-start | bytes 2359304 | tf_op jit(solution)/shard_map/ppermute | solution.py:758
  60.2 73.4 %collective-permute-start.9 = (bf16[96,2304]{1,0:T(8,128)(2,1)}, bf16[96,2304]{1,0:T(8,128)(2,1)}, u32[]{:S(2)}, u32[]{:S(2)}) collective-permute-start(bf16[96,2304]{1,0:T(8,128)(2,1)} %bitcast.244), channel_id=1, source_target_pairs={{0,4},{1,5},{2,6},{3,7},{4,8},{5,9},{6,10},{7,11},{8,12},{9,13},{1... | collective-permute-start | bytes 1327112 | tf_op jit(solution)/shard_map/ppermute | solution.py:766
  66.1 67.5 %collective-permute-start.10 = (bf16[96,2304]{1,0:T(8,128)(2,1)}, bf16[96,2304]{1,0:T(8,128)(2,1)}, u32[]{:S(2)}, u32[]{:S(2)}) collective-permute-start(bf16[96,2304]{1,0:T(8,128)(2,1)} %bitcast.245), channel_id=1, source_target_pairs={{0,8},{1,9},{2,10},{3,11},{4,12},{5,13},{6,14},{7,15},{8,0},{9,1},... | collective-permute-start | bytes 1327112 | tf_op jit(solution)/shard_map/ppermute | solution.py:766
  68.3 65.3 %collective-permute-start.11 = (bf16[96,2304]{1,0:T(8,128)(2,1)}, bf16[96,2304]{1,0:T(8,128)(2,1)}, u32[]{:S(2)}, u32[]{:S(2)}) collective-permute-start(bf16[96,2304]{1,0:T(8,128)(2,1)} %bitcast.246), channel_id=1, source_target_pairs={{0,12},{1,13},{2,14},{3,15},{4,0},{5,1},{6,2},{7,3},{8,4},{9,5},{1... | collective-permute-start | bytes 1327112 | tf_op jit(solution)/shard_map/ppermute | solution.py:766
  93.2 54.4 %collective-permute-start.8 = (bf16[768,1536]{1,0:T(8,128)(2,1)}, bf16[768,1536]{1,0:T(8,128)(2,1)}, u32[]{:S(2)}, u32[]{:S(2)}) collective-permute-start(bf16[768,1536]{1,0:T(8,128)(2,1)} %bitcast.197), channel_id=1, source_target_pairs={{0,16},{16,0},{1,17},{17,1},{2,18},{18,2},{3,19},{19,3},{4,20},{20... | collective-permute-start | bytes 7077896 | tf_op jit(solution)/shard_map/ppermute | solution.py:758
  99.3 50.6 %collective-permute-start.7 = (bf16[768,1536]{1,0:T(8,128)(2,1)S(1)}, bf16[768,1536]{1,0:T(8,128)(2,1)}, u32[]{:S(2)}, u32[]{:S(2)}) collective-permute-start(bf16[768,1536]{1,0:T(8,128)(2,1)S(1)} %bitcast.204), channel_id=1, source_target_pairs={{0,1},{1,0},{2,3},{3,2},{4,5},{5,4},{6,7},{7,6},{8,9},{9,8},{10,11... | collective-permute-start | bytes 7077896 | tf_op jit(solution)/shard_map/ppermute | solution.py:755
  147.6 49.1 %collective-permute-start.14 = (bf16[4,96,2304]{2,1,0:T(8,128)(2,1)}, bf16[4,96,2304]{2,1,0:T(8,128)(2,1)}, u32[]{:S(2)}, u32[]{:S(2)}) collective-permute-start(bf16[4,96,2304]{2,1,0:T(8,128)(2,1)} %line_rows.3.refs_2_.refs_9_.refs_17_.refs_0_), channel_id=1, source_target_pairs={{0,2},{1,3},{2,0},{3,1},{4,6},{5,7},{6,4},{7,5},{8,10},{9,11},{10,... | collective-permute-start | bytes 5308424 | tf_op jit(solution)/shard_map/ppermute | solution.py:763
  176.9 26.8 %collective-permute-start.13 = (bf16[512,768]{1,0:T(8,128)(2,1)}, bf16[512,768]{1,0:T(8,128)(2,1)}, u32[]{:S(2)}, u32[]{:S(2)}) collective-permute-start(bf16[512,768]{1,0:T(8,128)(2,1)} %slice.220), channel_id=1, source_target_pairs={{0,16},{16,0},{1,17},{17,1},{2,18},{18,2},{3,19},{19,3},{4,20},{20... | collective-permute-start | bytes 2359304 | tf_op jit(solution)/shard_map/ppermute | solution.py:758
  200.7 39.2 %collective-permute-start.15 = (bf16[768,2304]{1,0:T(8,128)(2,1)}, bf16[768,2304]{1,0:T(8,128)(2,1)}, u32[]{:S(2)}, u32[]{:S(2)}) collective-permute-start(bf16[768,2304]{1,0:T(8,128)(2,1)} %bitcast.229), channel_id=1, source_target_pairs={{0,1},{1,0},{2,3},{3,2},{4,5},{5,4},{6,7},{7,6},{8,9},{9,8},{10,11... | collective-permute-start | bytes 10616840 | tf_op jit(solution)/shard_map/ppermute | solution.py:755
  203.1 33.4 %collective-permute-start.16 = (bf16[768,768]{1,0:T(8,128)(2,1)}, bf16[768,768]{1,0:T(8,128)(2,1)}, u32[]{:S(2)}, u32[]{:S(2)}) collective-permute-start(bf16[768,768]{1,0:T(8,128)(2,1)} %slice.272), channel_id=1, source_target_pairs={{0,16},{16,0},{1,17},{17,1},{2,18},{18,2},{3,19},{19,3},{4,20},{20... | collective-permute-start | bytes 3538952 | tf_op jit(solution)/shard_map/ppermute | solution.py:758
  311.8 54.4 %collective-permute-start.22 = (bf16[768,1536]{1,0:T(8,128)(2,1)}, bf16[768,1536]{1,0:T(8,128)(2,1)}, u32[]{:S(2)}, u32[]{:S(2)}) collective-permute-start(bf16[768,1536]{1,0:T(8,128)(2,1)} %products_near.2.refs_8_), channel_id=1, source_target_pairs={{0,16},{16,0},{1,17},{17,1},{2,18},{18,2},{3,19},{19,3},{4,20},{20... | collective-permute-start | bytes 7077896 | tf_op jit(solution)/shard_map/ppermute | solution.py:758
  360.3 33.1 %collective-permute-start.21 = (bf16[512,768]{1,0:T(8,128)(2,1)}, bf16[512,768]{1,0:T(8,128)(2,1)}, u32[]{:S(2)}, u32[]{:S(2)}) collective-permute-start(bf16[512,768]{1,0:T(8,128)(2,1)} %convolution_convert_fusion.7.refs_5_), channel_id=1, source_target_pairs={{0,16},{16,0},{1,17},{17,1},{2,18},{18,2},{3,19},{19,3},{4,20},{20... | collective-permute-start | bytes 2359304 | tf_op jit(solution)/shard_map/ppermute | solution.py:758
  424.5 19.3 %collective-permute-start.23 = (bf16[768,1536]{1,0:T(8,128)(2,1)}, bf16[768,1536]{1,0:T(8,128)(2,1)}, u32[]{:S(2)}, u32[]{:S(2)}) collective-permute-start(bf16[768,1536]{1,0:T(8,128)(2,1)} %get-tuple-element.167), channel_id=1, source_target_pairs={{0,1},{1,0},{2,3},{3,2},{4,5},{5,4},{6,7},{7,6},{8,9},{9,8},{10,11... | collective-permute-start | bytes 7077896 | tf_op jit(solution)/shard_map/ppermute | solution.py:755
  425.0 18.8 %collective-permute-start.24 = (bf16[768,384]{1,0:T(8,128)(2,1)}, bf16[768,384]{1,0:T(8,128)(2,1)}, u32[]{:S(2)}, u32[]{:S(2)}) collective-permute-start(bf16[768,384]{1,0:T(8,128)(2,1)} %get-tuple-element.168), channel_id=1, source_target_pairs={{0,1},{1,0},{2,3},{3,2},{4,5},{5,4},{6,7},{7,6},{8,9},{9,8},{10,11... | collective-permute-start | bytes 1769480 | tf_op jit(solution)/shard_map/ppermute | solution.py:755
  426.4 41.2 %collective-permute-start.26 = (bf16[4,96,1920]{2,1,0:T(8,128)(2,1)}, bf16[4,96,1920]{2,1,0:T(8,128)(2,1)}, u32[]{:S(2)}, u32[]{:S(2)}) collective-permute-start(bf16[4,96,1920]{2,1,0:T(8,128)(2,1)} %dynamic-slice_bitcast_fusion.1), channel_id=1, source_target_pairs={{0,2},{1,3},{2,0},{3,1},{4,6},{5,7},{6,4},{7,5},{8,10},{9,11},{10,... | collective-permute-start | bytes 4423688 | tf_op jit(solution)/shard_map/ppermute | solution.py:763
  434.5 198.3 %reduce-scatter.3.cloned.1.call-start = ((), (), s32[]{:S(2)}) async-start(), calls=%async_computation.3 | async-start | bytes 3760128 | tf_op jit(solution)/shard_map/reduce_scatter | solution.py:842
  443.4 65.5 %collective-permute-start.28 = (bf16[768,1536]{1,0:T(8,128)(2,1)}, bf16[768,1536]{1,0:T(8,128)(2,1)}, u32[]{:S(2)}, u32[]{:S(2)}) collective-permute-start(bf16[768,1536]{1,0:T(8,128)(2,1)} %products_near.3.refs_8_), channel_id=1, source_target_pairs={{0,16},{16,0},{1,17},{17,1},{2,18},{18,2},{3,19},{19,3},{4,20},{20... | collective-permute-start | bytes 7077896 | tf_op jit(solution)/shard_map/ppermute | solution.py:758
  495.9 31.7 %collective-permute-start.32 = (bf16[96,1920]{1,0:T(8,128)(2,1)}, bf16[96,1920]{1,0:T(8,128)(2,1)}, u32[]{:S(2)}, u32[]{:S(2)}) collective-permute-start(bf16[96,1920]{1,0:T(8,128)(2,1)} %get-tuple-element.187), channel_id=1, source_target_pairs={{0,12},{1,13},{2,14},{3,15},{4,0},{5,1},{6,2},{7,3},{8,4},{9,5},{1... | collective-permute-start | bytes 1105928 | tf_op jit(solution)/shard_map/ppermute | solution.py:766
  500.0 34.7 %collective-permute-start.31 = (bf16[96,1920]{1,0:T(8,128)(2,1)}, bf16[96,1920]{1,0:T(8,128)(2,1)}, u32[]{:S(2)}, u32[]{:S(2)}) collective-permute-start(bf16[96,1920]{1,0:T(8,128)(2,1)} %get-tuple-element.188), channel_id=1, source_target_pairs={{0,8},{1,9},{2,10},{3,11},{4,12},{5,13},{6,14},{7,15},{8,0},{9,1},... | collective-permute-start | bytes 1105928 | tf_op jit(solution)/shard_map/ppermute | solution.py:766
  502.4 25.2 %collective-permute-start.30 = (bf16[96,1920]{1,0:T(8,128)(2,1)}, bf16[96,1920]{1,0:T(8,128)(2,1)}, u32[]{:S(2)}, u32[]{:S(2)}) collective-permute-start(bf16[96,1920]{1,0:T(8,128)(2,1)} %get-tuple-element.186), channel_id=1, source_target_pairs={{0,4},{1,5},{2,6},{3,7},{4,8},{5,9},{6,10},{7,11},{8,12},{9,13},{1... | collective-permute-start | bytes 1105928 | tf_op jit(solution)/shard_map/ppermute | solution.py:766
  513.3 32.7 %collective-permute-start.29 = (bf16[4,96,1920]{2,1,0:T(8,128)(2,1)}, bf16[4,96,1920]{2,1,0:T(8,128)(2,1)S(1)}, u32[]{:S(2)}, u32[]{:S(2)}) collective-permute-start(bf16[4,96,1920]{2,1,0:T(8,128)(2,1)} %dynamic-slice_bitcast_fusion), channel_id=1, source_target_pairs={{0,2},{1,3},{2,0},{3,1},{4,6},{5,7},{6,4},{7,5},{8,10},{9,11},{10,... | collective-permute-start | bytes 4423688 | tf_op jit(solution)/shard_map/ppermute | solution.py:763
  518.9 83.8 %collective-permute-start.27 = (bf16[512,768]{1,0:T(8,128)(2,1)}, bf16[512,768]{1,0:T(8,128)(2,1)}, u32[]{:S(2)}, u32[]{:S(2)}) collective-permute-start(bf16[512,768]{1,0:T(8,128)(2,1)} %convolution_convert_fusion.6.refs_2_), channel_id=1, source_target_pairs={{0,16},{16,0},{1,17},{17,1},{2,18},{18,2},{3,19},{19,3},{4,20},{20... | collective-permute-start | bytes 2359304 | tf_op jit(solution)/shard_map/ppermute | solution.py:758
  550.2 39.3 %collective-permute-start.35 = (bf16[96,1920]{1,0:T(8,128)(2,1)S(1)}, bf16[96,1920]{1,0:T(8,128)(2,1)}, u32[]{:S(2)}, u32[]{:S(2)}) collective-permute-start(bf16[96,1920]{1,0:T(8,128)(2,1)S(1)} %get-tuple-element.184), channel_id=1, source_target_pairs={{0,12},{1,13},{2,14},{3,15},{4,0},{5,1},{6,2},{7,3},{8,4},{9,5},{1... | collective-permute-start | bytes 1105928 | tf_op jit(solution)/shard_map/ppermute | solution.py:766
  552.8 45.2 %collective-permute-start.34 = (bf16[96,1920]{1,0:T(8,128)(2,1)S(1)}, bf16[96,1920]{1,0:T(8,128)(2,1)}, u32[]{:S(2)}, u32[]{:S(2)}) collective-permute-start(bf16[96,1920]{1,0:T(8,128)(2,1)S(1)} %get-tuple-element.185), channel_id=1, source_target_pairs={{0,8},{1,9},{2,10},{3,11},{4,12},{5,13},{6,14},{7,15},{8,0},{9,1},... | collective-permute-start | bytes 1105928 | tf_op jit(solution)/shard_map/ppermute | solution.py:766
  553.1 35.8 %collective-permute-start.33 = (bf16[96,1920]{1,0:T(8,128)(2,1)}, bf16[96,1920]{1,0:T(8,128)(2,1)S(1)}, u32[]{:S(2)}, u32[]{:S(2)}) collective-permute-start(bf16[96,1920]{1,0:T(8,128)(2,1)} %get-tuple-element.183), channel_id=1, source_target_pairs={{0,4},{1,5},{2,6},{3,7},{4,8},{5,9},{6,10},{7,11},{8,12},{9,13},{1... | collective-permute-start | bytes 1105928 | tf_op jit(solution)/shard_map/ppermute | solution.py:766
  (85 other events, 487.6 us)
Sparse Core Ops, SparseCore 0:
  10.3 89.4 all-gather.5
  102.6 57.3 all-gather.3
  434.6 69.6 reduce-scatter.4
  523.4 86.1 reduce-scatter.2
